TPU v7x, 128 devices: a whole 4x4x4 slice. The times are simulated.
128 devices in a mesh: depth: 8 (over y, core), image: 16 (over z, x).
Axes of the slice: x: 4, y: 4, z: 4, core: 2. Of those that a mesh axis runs over, the one named last changes fastest.
Arguments:
- populations: float32 [19, 256, 256, 128], P(None, 'depth', 'image'), may hold values from 0 to 0.4, as said below
- transfer: float32 [16, 5, 8], P('image'), may hold values from 0.1 to 1
- direction: int32 [16], P('image'), may hold values from 0 to 1
Outputs:
- final_populations: float32 [19, 256, 256, 128], P(None, 'depth', 'image')
- vorticity: bfloat16 [256, 256, 128], P('depth', 'image')
- images: float32 [16, 4, 256, 128], P('image', None, 'depth')
Inputs may be any that keep to these rules, and one draw needn't show every extreme that they name: `populations`: each population is positive, its lattice weight times a density near one with a perturbation by a rough flow of small speed. `direction`: 0 views from the side of small x, 1 from the side of large x.
All inputs are finite; a program needn't handle non-finite values.
Results may differ from a plain program's by a relative error of at most 0.001.
Values may be sent and summed in bfloat16 or wider, within the bound.
No kernel may reach another device: no remote copies, remote signals or barrier semaphores. Data moves between devices by JAX's collectives and lax.ppermute only.
A program may use at most 128 MiB of HBM per device.

v0:
```python
import jax
import jax.numpy as jnp
from jax import lax
from jax.sharding import PartitionSpec as P

STEPS = 4


lattice_velocities = (
    (0, 0, 0),
    (1, 0, 0),
    (-1, 0, 0),
    (0, 1, 0),
    (0, -1, 0),
    (0, 0, 1),
    (0, 0, -1),
    (1, 1, 0),
    (-1, -1, 0),
    (1, -1, 0),
    (-1, 1, 0),
    (1, 0, 1),
    (-1, 0, -1),
    (1, 0, -1),
    (-1, 0, 1),
    (0, 1, 1),
    (0, -1, -1),
    (0, 1, -1),
    (0, -1, 1),
)
lattice_weights = (1.0 / 3.0,) + (1.0 / 18.0,) * 6 + (1.0 / 36.0,) * 12
relaxation = 1.25
bump_width = 0.15
level_offset = 0.05


def with_halo(shard, sides, width):
    edges = {}
    for axis, dim in sides:
        devices, length = (lax.axis_size(axis), shard.shape[dim])
        up = [(i, (i + 1) % devices) for i in range(devices)]
        last = lax.slice_in_dim(shard, length - width, length, axis=dim)
        first = lax.slice_in_dim(shard, 0, width, axis=dim)
        edges[dim] = (
            lax.ppermute(last, axis, up),
            lax.ppermute(first, axis, [(b, a) for a, b in up]),
        )
    done = []
    for _, dim in sides:
        low, high = edges[dim]
        around = [(width, width) if d in done else (0, 0) for d in range(shard.ndim)]
        shard = jnp.concatenate([jnp.pad(low, around), shard, jnp.pad(high, around)], axis=dim)
        done.append(dim)
    return shard


def with_halo_2(shard, sides, width):
    for axis, dim in sides:
        devices, length = (lax.axis_size(axis), shard.shape[dim])
        up = [(i, (i + 1) % devices) for i in range(devices)]
        down = [(j, i) for i, j in up]
        last = lax.slice_in_dim(shard, length - width, length, axis=dim)
        first = lax.slice_in_dim(shard, 0, width, axis=dim)
        before = lax.ppermute(last, axis, up)
        after = lax.ppermute(first, axis, down)
        shard = jnp.concatenate([before, shard, after], axis=dim)
    return shard


def sent_to_all(shard, axis):
    devices = lax.axis_size(axis)
    return lax.all_to_all(
        jnp.broadcast_to(shard[None], (devices, *shard.shape)), axis, 0, 0, tiled=True
    )


def laid_out(tiles, dim):
    tiles = jnp.moveaxis(tiles, 0, dim)
    lengths = tiles.shape
    return tiles.reshape(*lengths[:dim], lengths[dim] * lengths[dim + 1], *lengths[dim + 2 :])


def gather_directly(shard, axis, dim):
    tiles = sent_to_all(shard, axis)
    return laid_out(tiles, dim)


def moments(field):
    density = field[0]
    for number in range(1, 19):
        density = density + field[number]
    components = []
    for axis_index in range(3):
        total = jnp.zeros_like(density)
        for number in range(19):
            factor = lattice_velocities[number][axis_index]
            if factor != 0:
                total = total + factor * field[number]
        components.append(total / density)
    return (density, components)


def collide(field):
    density, flow = moments(field)
    squared = flow[0] * flow[0] + flow[1] * flow[1] + flow[2] * flow[2]
    result = []
    for number in range(19):
        project = jnp.zeros_like(density)
        for axis_index in range(3):
            factor = lattice_velocities[number][axis_index]
            if factor != 0:
                project = project + factor * flow[axis_index]
        equilibrium = (
            lattice_weights[number]
            * density
            * (1.0 + 3.0 * project + 4.5 * project * project - 1.5 * squared)
        )
        result.append(field[number] - relaxation * (field[number] - equilibrium))
    return jnp.stack(result)


def stream(padded, depth_cells, width_cells):
    pieces = []
    for number in range(19):
        shift_x, shift_y, shift_z = lattice_velocities[number]
        window = padded[
            number,
            1 - shift_x : 1 - shift_x + depth_cells,
            1 - shift_y : 1 - shift_y + width_cells,
            :,
        ]
        if shift_z != 0:
            window = jnp.roll(window, shift_z, axis=2)
        pieces.append(window)
    return jnp.stack(pieces)


def spin_magnitude(field):
    density, flow = moments(field)
    padded = with_halo(jnp.stack(flow), (("depth", 1), ("image", 2)), 1)
    inner = padded[:, 1:-1, 1:-1, :]

    def across_x(component):
        return (padded[component, 2:, 1:-1, :] - padded[component, :-2, 1:-1, :]) * 0.5

    def across_y(component):
        return (padded[component, 1:-1, 2:, :] - padded[component, 1:-1, :-2, :]) * 0.5

    def across_z(component):
        return (jnp.roll(inner[component], -1, 2) - jnp.roll(inner[component], 1, 2)) * 0.5

    spin_x = across_y(2) - across_z(1)
    spin_y = across_z(0) - across_x(2)
    spin_z = across_x(1) - across_y(0)
    return jnp.sqrt(spin_x * spin_x + spin_y * spin_y + spin_z * spin_z).astype(jnp.bfloat16)


def render_block(level, params, backward, ray_cells):
    extinction = jnp.zeros_like(level)
    emission = [jnp.zeros_like(level) for channel in range(3)]
    for bump_index in range(params.shape[1]):
        bump = jnp.exp(-jnp.square((level - params[0, bump_index]) / bump_width))
        extinction = extinction + params[1, bump_index] * bump
        for channel in range(3):
            emission[channel] = emission[channel] + params[2 + channel, bump_index] * bump
    optical = extinction / ray_cells
    inclusive = jnp.cumsum(optical, axis=0)
    total = inclusive[-1]
    front = jnp.where(backward, total[None] - inclusive, inclusive - optical)
    weight = jnp.exp(-front) * (1.0 - jnp.exp(-optical))
    colors = [jnp.sum(weight * emission[channel], axis=0) for channel in range(3)]
    return jnp.stack(colors + [jnp.exp(-total)])


def render_many(brick, params, backward, ray_cells):
    level = brick.astype(jnp.float32)
    level = level / (level + level_offset)

    def render_single(pair):
        return render_block(level, pair[0], pair[1], ray_cells)

    return lax.map(render_single, (params, backward))


def over(front_part, back_part):
    colors = front_part[:, :3] + front_part[:, 3:4] * back_part[:, :3]
    return jnp.concatenate([colors, front_part[:, 3:4] * back_part[:, 3:4]], axis=1)


def composite_direct(fragments, backward):
    slab_total = lax.axis_size("depth")
    moved = lax.all_to_all(fragments, "depth", split_axis=2, concat_axis=0, tiled=True)
    tf_count = fragments.shape[0]
    slabs = moved.reshape((slab_total, tf_count) + moved.shape[1:])
    start = jnp.concatenate(
        [jnp.zeros_like(slabs[0][:, :3]), jnp.ones_like(slabs[0][:, 3:4])], axis=1
    )
    chooser = backward[:, None, None, None]

    def absorb(carry, pair):
        forward_piece, backward_piece = pair
        piece = jnp.where(chooser, backward_piece, forward_piece)
        return (over(carry, piece), None)

    result, unused = lax.scan(absorb, start, (slabs, slabs[::-1]))
    return result


def on_device(populations, transfer, direction):
    depth_cells = populations.shape[1]
    width_cells = populations.shape[2]
    field = populations
    for turn_index in range(STEPS):
        collided = collide(field)
        padded = with_halo_2(collided, (("depth", 1), ("image", 2)), 1)
        field = stream(padded, depth_cells, width_cells)
    vorticity = spin_magnitude(field)
    ray_cells = depth_cells * lax.axis_size("depth")
    backward = direction == 1
    fragments = render_many(gather_directly(vorticity, "image", 1), transfer, backward, ray_cells)
    combined = composite_direct(fragments, backward)
    images = jnp.concatenate([combined[:, :3], 1.0 - combined[:, 3:4]], axis=1)
    return (field, vorticity, images)


def solution(mesh):
    in_specs = (P(None, "depth", "image", None), P("image", None, None), P("image"))
    out_specs = (
        P(None, "depth", "image", None),
        P("depth", "image", None),
        P("image", None, "depth", None),
    )
    return jax.shard_map(
        on_device, mesh=mesh, in_specs=in_specs, out_specs=out_specs, check_vma=False
    )
```

profile of v0, /device:TPU:1, one launch (start us, length us, event | category | flops | bytes accessed | tf_op | source)
XLA Modules:
  0.0 375.3 jit_solution(10239020122123399476)
XLA Ops:
  0.6 3.9 %constant_dynamic-update-slice_fusion = (f32[19,32,16,128]{3,2,1,0:T(8,128)S(1)}, f32[1,32,16,128]{3,2,1,0:T(8,128)}, f32[1,32,16,128]{3,2,1,0:T(8,128)S(1)}, f3...) fusion(f32[19,32,16,128]{3,2,1,0:T(8,128)} %param.5), kind=kLoop, calls=%fused_computation.1154 | loop fusion | flops 4718591 | bytes 6815744
  13.7 4.6 %pad_maximum_fusion.12 = (f32[19,34,1,128]{3,2,1,0:T(1,128)}, f32[19,34,1,128]{3,2,1,0:T(1,128)}) fusion(f32[19,1,16,128]{3,2,1,0:T(8,128)S(1)} %collective-permute-done.1, f32[19,32,16,128]{3,2,1,0:T(8,128)} %copy-done.6, f32[19,1,16,128]{3,2,1,0:T(8,128)S(1)} %collective-permute-done), kind=kLoop, calls=%fused_computation.177 | loop fusion | flops 330752 | bytes 5953536 | tf_op jit(solution)/shard_map/slice | solution.py:61
  19.5 5.0 %collective-permute-start.3 = (f32[19,34,1,128]{3,2,1,0:T(1,128)}, f32[19,34,1,128]{3,2,1,0:T(1,128)S(1)}, u32[]{:S(2)}, u32[]{:S(2)}) collective-permute-start(f32[19,34,1,128]{3,2,1,0:T(1,128)} %get-tuple-element.217), channel_id=1, source_target_pairs={{1,0},{2,1},{3,2},{4,3},{5,4},{6,5},{7,6},{8,7},{9,8},{10,9},{11,1... | collective-permute-start | bytes 992264 | tf_op jit(solution)/shard_map/ppermute | solution.py:64
  36.2 5.3 %fusion.297 = (f32[32,16,128]{2,1,0:T(8,128)S(1)}, f32[32,16,128]{2,1,0:T(8,128)S(1)}, f32[32,16,128]{2,1,0:T(8,128)S(1)}, f32[32,16,128]{2,1,0:T(8,128)S(1)}, f...) fusion(f32[32,16,127]{2,1,0:T(8,128)} %get-tuple-element.398, ...), kind=kLoop, calls=%fused_computation.399 | loop fusion | flops 7405568 | bytes 12769280 | tf_op jit(solution)/shard_map/sub | solution.py:117
  43.4 4.5 %constant_dynamic-update-slice_fusion.1 = (f32[19,32,16,128]{3,2,1,0:T(8,128)S(1)}, f32[1,32,16,128]{3,2,1,0:T(8,128)}, f32[1,32,16,128]{3,2,1,0:T(8,128)S(1)}, ...) fusion(f32[1,32,16,128]{3,2,1,0:T(8,128)} %get-tuple-element.17, ...), kind=kLoop, calls=%fused_computation.1155 | loop fusion | flops 5373951 | bytes 8912896
  59.6 4.5 %pad_maximum_fusion.9 = (f32[19,34,1,128]{3,2,1,0:T(1,128)}, f32[19,34,1,128]{3,2,1,0:T(1,128)}) fusion(f32[19,1,16,128]{3,2,1,0:T(8,128)S(1)} %collective-permute-done.5, f32[19,32,16,128]{3,2,1,0:T(8,128)} %copy-done.4, f32[19,1,16,128]{3,2,1,0:T(8,128)S(1)} %collective-permute-done.4), kind=kLoop, calls=%fused_computation.174 | loop fusion | flops 330752 | bytes 5953536 | tf_op jit(solution)/shard_map/slice | solution.py:61
  64.1 5.3 %collective-permute-start.7 = (f32[19,34,1,128]{3,2,1,0:T(1,128)}, f32[19,34,1,128]{3,2,1,0:T(1,128)}, u32[]{:S(2)}, u32[]{:S(2)}) collective-permute-start(f32[19,34,1,128]{3,2,1,0:T(1,128)} %get-tuple-element.213), channel_id=1, source_target_pairs={{1,0},{2,1},{3,2},{4,3},{5,4},{6,5},{7,6},{8,7},{9,8},{10,9},{11,1... | collective-permute-start | bytes 992264 | tf_op jit(solution)/shard_map/ppermute | solution.py:64
  88.3 4.1 %fusion.408 = (f32[32,16,128]{2,1,0:T(8,128)S(1)}, f32[32,16,128]{2,1,0:T(8,128)S(1)}, f32[32,16,128]{2,1,0:T(8,128)S(1)}, f32[32,16,128]{2,1,0:T(8,128)S(1)}, f...) fusion(f32[32,16,127]{2,1,0:T(8,128)} %get-tuple-element.327, ...), kind=kLoop, calls=%fused_computation.510 | loop fusion | flops 7405568 | bytes 12507136 | tf_op jit(solution)/shard_map/sub | solution.py:117
  100.2 4.0 %collective-permute-start.9 = (f32[19,1,16,128]{3,2,1,0:T(8,128)S(1)}, f32[19,1,16,128]{3,2,1,0:T(8,128)S(1)}, u32[]{:S(2)}, u32[]{:S(2)}) collective-permute-start(f32[19,1,16,128]{3,2,1,0:T(8,128)S(1)} %get-tuple-element.239), channel_id=1, source_target_pairs={{16,0},{32,16},{48,32},{64,48},{80,64},{96,80},{112,96},{0,112},{1... | collective-permute-start | bytes 466952 | tf_op jit(solution)/shard_map/ppermute | solution.py:64
  108.4 3.9 %pad_maximum_fusion.6 = (f32[19,34,1,128]{3,2,1,0:T(1,128)}, f32[19,34,1,128]{3,2,1,0:T(1,128)}) fusion(f32[19,1,16,128]{3,2,1,0:T(8,128)S(1)} %collective-permute-done.9, f32[19,32,16,128]{3,2,1,0:T(8,128)} %copy-done.2, f32[19,1,16,128]{3,2,1,0:T(8,128)S(1)} %collective-permute-done.8), kind=kLoop, calls=%fused_computation.171 | loop fusion | flops 330752 | bytes 5953536 | tf_op jit(solution)/shard_map/slice | solution.py:61
  112.3 4.9 %collective-permute-start.11 = (f32[19,34,1,128]{3,2,1,0:T(1,128)}, f32[19,34,1,128]{3,2,1,0:T(1,128)}, u32[]{:S(2)}, u32[]{:S(2)}) collective-permute-start(f32[19,34,1,128]{3,2,1,0:T(1,128)} %get-tuple-element.209), channel_id=1, source_target_pairs={{1,0},{2,1},{3,2},{4,3},{5,4},{6,5},{7,6},{8,7},{9,8},{10,9},{11,1... | collective-permute-start | bytes 992264 | tf_op jit(solution)/shard_map/ppermute | solution.py:64
  136.1 5.0 %multiply_subtract_fusion = (f32[32,16,128]{2,1,0:T(8,128)S(1)}, f32[32,16,128]{2,1,0:T(8,128)S(1)}, f32[32,16,128]{2,1,0:T(8,128)S(1)}, f32[32,16,128]{2,1,0:T(...) fusion(f32[32,16,1]{2,1,0:T(8,128)S(1)} %bitcast.1205, ...), kind=kLoop, calls=%fused_computation.1107 | loop fusion | flops 7864320 | bytes 13293568 | tf_op jit(solution)/shard_map/sub | solution.py:117
  160.8 5.0 %collective-permute-start.15 = (f32[19,34,1,128]{3,2,1,0:T(1,128)S(1)}, f32[19,34,1,128]{3,2,1,0:T(1,128)S(1)}, u32[]{:S(2)}, u32[]{:S(2)}) collective-permute-start(f32[19,34,1,128]{3,2,1,0:T(1,128)S(1)} %get-tuple-element.205), channel_id=1, source_target_pairs={{1,0},{2,1},{3,2},{4,3},{5,4},{6,5},{7,6},{8,7},{9,8},{10,9},{11,1... | collective-permute-start | bytes 992264 | tf_op jit(solution)/shard_map/ppermute | solution.py:64
  183.6 4.1 %add_divide_fusion.4 = (f32[1,32,16,128]{3,2,1,0:T(8,128)S(1)}, f32[1,32,16,128]{3,2,1,0:T(8,128)S(1)}, f32[1,32,16,128]{3,2,1,0:T(8,128)S(1)}, f32[1,32,16,128]...) fusion(f32[1,32,16,127]{3,2,1,0:T(8,128)} %get-tuple-element.27, ...), kind=kLoop, calls=%fused_computation.1106 | loop fusion | flops 4128768 | bytes 11458560 | tf_op jit(solution)/shard_map/div | solution.py:98
  199.7 4.6 %collective-permute-start.18 = (f32[3,32,1,128]{3,2,1,0:T(1,128)S(1)}, f32[3,32,1,128]{3,2,1,0:T(1,128)}, u32[]{:S(2)}, u32[]{:S(2)}) collective-permute-start(f32[3,32,1,128]{3,2,1,0:T(1,128)S(1)} %get-tuple-element.252), channel_id=1, source_target_pairs={{1,0},{2,1},{3,2},{4,3},{5,4},{6,5},{7,6},{8,7},{9,8},{10,9},{11,1... | collective-permute-start | bytes 147464 | tf_op jit(solution)/shard_map/ppermute | solution.py:45
  215.1 3.3 fusion.716
  220.1 6.4 %all-to-all-start = ((bf16[16,32,16,128]{3,2,1,0:T(8,128)(2,1)}), bf16[16,32,16,128]{3,2,1,0:T(8,128)(2,1)S(1)}, u32[]{:S(2)}, u32[]{:S(2)}) async-start(bf16[16,32,16,128]{3,2,1,0:T(8,128)(2,1)} %broadcast_in_dim.29), calls=%async_computation | async-start | bytes 4194304 | tf_op jit(solution)/shard_map/all_to_all | solution.py:71
  240.7 14.1 %all-to-all-done = bf16[16,32,16,128]{3,2,1,0:T(8,128)(2,1)S(1)} async-done(((bf16[16,32,16,128]{3,2,1,0:T(8,128)(2,1)}), bf16[16,32,16,128]{3,2,1,0:T(8,128)(2,1)S(1)}, u32[]{:S(2)}, u32[]{:S(2)}) %all-to-all-start) | async-done | bytes 2097184 | tf_op jit(solution)/shard_map/all_to_all | solution.py:71
  255.9 17.8 %fusion.1 = f32[32,256,128]{2,1,0:T(8,128)S(1)} fusion(f32[32,256,128]{2,1,0:T(8,128)S(1)} %add_divide_fusion.1, f32[]{:T(128)} %bitcast.208, f32[]{:T(128)} %bitcast.207, f32[]{:T(128)} %bitcast.206, f32[]{:T(128)} %bitcast.205, f32[]{:T(128)} %bitcast.204, f32[]{:T(128)} %bitcast.203, f32[]{:T(128)} %bitcast.202, f32[]{:T(128)} %bitcast.201, ...), kind=kOutput, calls=%fused_computation.20 | output fusion | flops 82837504 | bytes 8388672 | tf_op jit(solution)/shard_map/while/body/eval_jaxpr/jit(cumsum)/reduce_window_sum | solution.py:166
  273.7 27.1 %multiply_reduce_fusion = f32[16,16,128]{2,1,0:T(8,128)S(1)} fusion(f32[32,16,16,128]{3,2,1,0:T(8,128)S(1)} %bitcast.1270, f32[]{:T(128)} %bitcast.236, f32[]{:T(128)} %bitcast.235, f32[]{:T(128)} %bitcast.234, f32[]{:T(128)} %bitcast.233, f32[]{:T(128)} %bitcast.232, f32[]{:T(128)} %bitcast.231, f32[]{:T(128)} %bitcast.230, f32[]{:T(128)} %bitcast.229, ...), kind=kLoop, calls=%fused_computation.8 | loop fusion | flops 78610432 | bytes 6553697 | tf_op jit(solution)/shard_map/while/body/eval_jaxpr/reduce_sum | solution.py:170
  300.8 27.0 %multiply_reduce_fusion.1 = f32[16,16,128]{2,1,0:T(8,128)S(1)} fusion(f32[32,16,16,128]{3,2,1,0:T(8,128)S(1)} %bitcast.1271, f32[]{:T(128)} %bitcast.227, f32[]{:T(128)} %bitcast.226, f32[]{:T(128)} %bitcast.225, f32[]{:T(128)} %bitcast.224, f32[]{:T(128)} %bitcast.223, f32[]{:T(128)} %bitcast.222, f32[]{:T(128)} %bitcast.221, f32[]{:T(128)} %bitcast.220, ...), kind=kLoop, calls=%fused_computation.9 | loop fusion | flops 78610432 | bytes 6553697 | tf_op jit(solution)/shard_map/while/body/eval_jaxpr/reduce_sum | solution.py:170
  327.8 27.1 %multiply_reduce_fusion.2 = f32[16,16,128]{2,1,0:T(8,128)S(1)} fusion(f32[32,16,16,128]{3,2,1,0:T(8,128)S(1)} %bitcast.1272, f32[]{:T(128)} %bitcast.218, f32[]{:T(128)} %bitcast.217, f32[]{:T(128)} %bitcast.216, f32[]{:T(128)} %bitcast.215, f32[]{:T(128)} %bitcast.214, f32[]{:T(128)} %bitcast.213, f32[]{:T(128)} %bitcast.212, f32[]{:T(128)} %bitcast.211, ...), kind=kLoop, calls=%fused_computation.10 | loop fusion | flops 78610432 | bytes 6553697 | tf_op jit(solution)/shard_map/while/body/eval_jaxpr/reduce_sum | solution.py:170
  356.2 7.6 %all-to-all-start.1 = ((f32[1,4,256,128]{3,1,0,2:T(4,128)}), f32[1,4,256,128]{3,1,0,2:T(4,128)S(1)}, u32[]{:S(2)}, u32[]{:S(2)}) async-start(f32[1,4,256,128]{3,1,0,2:T(4,128)} %copy.2321), calls=%async_computation.1 | async-start | bytes 1048576 | tf_op jit(solution)/shard_map/all_to_all | solution.py:191
  368.0 5.4 %all-to-all-done.1 = f32[1,4,256,128]{3,1,0,2:T(4,128)S(1)} async-done(((f32[1,4,256,128]{3,1,0,2:T(4,128)}), f32[1,4,256,128]{3,1,0,2:T(4,128)S(1)}, u32[]{:S(2)}, u32[]{:S(2)}) %all-to-all-start.1) | async-done | bytes 524320 | tf_op jit(solution)/shard_map/all_to_all | solution.py:191
  (649 shorter events, 166.3 us)
Async XLA Ops:
  6.8 6.9 %collective-permute-start.1 = (f32[19,1,16,128]{3,2,1,0:T(8,128)S(1)}, f32[19,1,16,128]{3,2,1,0:T(8,128)S(1)}, u32[]{:S(2)}, u32[]{:S(2)}) collective-permute-start(f32[19,1,16,128]{3,2,1,0:T(8,128)S(1)} %get-tuple-element.247), channel_id=1, source_target_pairs={{16,0},{32,16},{48,32},{64,48},{80,64},{96,80},{112,96},{0,112},{1... | collective-permute-start | bytes 466952 | tf_op jit(solution)/shard_map/ppermute | solution.py:64
  8.2 5.5 %collective-permute-start = (f32[19,1,16,128]{3,2,1,0:T(8,128)S(1)}, f32[19,1,16,128]{3,2,1,0:T(8,128)S(1)}, u32[]{:S(2)}, u32[]{:S(2)}) collective-permute-start(f32[19,1,16,128]{3,2,1,0:T(8,128)S(1)} %get-tuple-element.246), channel_id=1, source_target_pairs={{0,16},{16,32},{32,48},{48,64},{64,80},{80,96},{96,112},{112,0},{1... | collective-permute-start | bytes 466952 | tf_op jit(solution)/shard_map/ppermute | solution.py:63
  18.3 13.1 %collective-permute-start.2 = (f32[19,34,1,128]{3,2,1,0:T(1,128)}, f32[19,34,1,128]{3,2,1,0:T(1,128)S(1)}, u32[]{:S(2)}, u32[]{:S(2)}) collective-permute-start(f32[19,34,1,128]{3,2,1,0:T(1,128)} %get-tuple-element.216), channel_id=1, source_target_pairs={{0,1},{1,2},{2,3},{3,4},{4,5},{5,6},{6,7},{7,8},{8,9},{9,10},{10,1... | collective-permute-start | bytes 992264 | tf_op jit(solution)/shard_map/ppermute | solution.py:63
  19.5 11.9 %collective-permute-start.3 = (f32[19,34,1,128]{3,2,1,0:T(1,128)}, f32[19,34,1,128]{3,2,1,0:T(1,128)S(1)}, u32[]{:S(2)}, u32[]{:S(2)}) collective-permute-start(f32[19,34,1,128]{3,2,1,0:T(1,128)} %get-tuple-element.217), channel_id=1, source_target_pairs={{1,0},{2,1},{3,2},{4,3},{5,4},{6,5},{7,6},{8,7},{9,8},{10,9},{11,1... | collective-permute-start | bytes 992264 | tf_op jit(solution)/shard_map/ppermute | solution.py:64
  53.2 6.3 %collective-permute-start.5 = (f32[19,1,16,128]{3,2,1,0:T(8,128)S(1)}, f32[19,1,16,128]{3,2,1,0:T(8,128)S(1)}, u32[]{:S(2)}, u32[]{:S(2)}) collective-permute-start(f32[19,1,16,128]{3,2,1,0:T(8,128)S(1)} %get-tuple-element.243), channel_id=1, source_target_pairs={{16,0},{32,16},{48,32},{64,48},{80,64},{96,80},{112,96},{0,112},{1... | collective-permute-start | bytes 466952 | tf_op jit(solution)/shard_map/ppermute | solution.py:64
  55.7 3.9 %collective-permute-start.4 = (f32[19,1,16,128]{3,2,1,0:T(8,128)S(1)}, f32[19,1,16,128]{3,2,1,0:T(8,128)S(1)}, u32[]{:S(2)}, u32[]{:S(2)}) collective-permute-start(f32[19,1,16,128]{3,2,1,0:T(8,128)S(1)} %get-tuple-element.242), channel_id=1, source_target_pairs={{0,16},{16,32},{32,48},{48,64},{64,80},{80,96},{96,112},{112,0},{1... | collective-permute-start | bytes 466952 | tf_op jit(solution)/shard_map/ppermute | solution.py:63
  64.1 13.6 %collective-permute-start.6 = (f32[19,34,1,128]{3,2,1,0:T(1,128)}, f32[19,34,1,128]{3,2,1,0:T(1,128)S(1)}, u32[]{:S(2)}, u32[]{:S(2)}) collective-permute-start(f32[19,34,1,128]{3,2,1,0:T(1,128)} %get-tuple-element.212), channel_id=1, source_target_pairs={{0,1},{1,2},{2,3},{3,4},{4,5},{5,6},{6,7},{7,8},{8,9},{9,10},{10,1... | collective-permute-start | bytes 992264 | tf_op jit(solution)/shard_map/ppermute | solution.py:63
  64.1 14.3 %collective-permute-start.7 = (f32[19,34,1,128]{3,2,1,0:T(1,128)}, f32[19,34,1,128]{3,2,1,0:T(1,128)}, u32[]{:S(2)}, u32[]{:S(2)}) collective-permute-start(f32[19,34,1,128]{3,2,1,0:T(1,128)} %get-tuple-element.213), channel_id=1, source_target_pairs={{1,0},{2,1},{3,2},{4,3},{5,4},{6,5},{7,6},{8,7},{9,8},{10,9},{11,1... | collective-permute-start | bytes 992264 | tf_op jit(solution)/shard_map/ppermute | solution.py:64
  100.2 8.2 %collective-permute-start.9 = (f32[19,1,16,128]{3,2,1,0:T(8,128)S(1)}, f32[19,1,16,128]{3,2,1,0:T(8,128)S(1)}, u32[]{:S(2)}, u32[]{:S(2)}) collective-permute-start(f32[19,1,16,128]{3,2,1,0:T(8,128)S(1)} %get-tuple-element.239), channel_id=1, source_target_pairs={{16,0},{32,16},{48,32},{64,48},{80,64},{96,80},{112,96},{0,112},{1... | collective-permute-start | bytes 466952 | tf_op jit(solution)/shard_map/ppermute | solution.py:64
  104.2 4.3 %collective-permute-start.8 = (f32[19,1,16,128]{3,2,1,0:T(8,128)S(1)}, f32[19,1,16,128]{3,2,1,0:T(8,128)S(1)}, u32[]{:S(2)}, u32[]{:S(2)}) collective-permute-start(f32[19,1,16,128]{3,2,1,0:T(8,128)S(1)} %get-tuple-element.238), channel_id=1, source_target_pairs={{0,16},{16,32},{32,48},{48,64},{64,80},{80,96},{96,112},{112,0},{1... | collective-permute-start | bytes 466952 | tf_op jit(solution)/shard_map/ppermute | solution.py:63
  112.3 13.2 %collective-permute-start.10 = (f32[19,34,1,128]{3,2,1,0:T(1,128)}, f32[19,34,1,128]{3,2,1,0:T(1,128)S(1)}, u32[]{:S(2)}, u32[]{:S(2)}) collective-permute-start(f32[19,34,1,128]{3,2,1,0:T(1,128)} %get-tuple-element.208), channel_id=1, source_target_pairs={{0,1},{1,2},{2,3},{3,4},{4,5},{5,6},{6,7},{7,8},{8,9},{9,10},{10,1... | collective-permute-start | bytes 992264 | tf_op jit(solution)/shard_map/ppermute | solution.py:63
  112.3 13.9 %collective-permute-start.11 = (f32[19,34,1,128]{3,2,1,0:T(1,128)}, f32[19,34,1,128]{3,2,1,0:T(1,128)}, u32[]{:S(2)}, u32[]{:S(2)}) collective-permute-start(f32[19,34,1,128]{3,2,1,0:T(1,128)} %get-tuple-element.209), channel_id=1, source_target_pairs={{1,0},{2,1},{3,2},{4,3},{5,4},{6,5},{7,6},{8,7},{9,8},{10,9},{11,1... | collective-permute-start | bytes 992264 | tf_op jit(solution)/shard_map/ppermute | solution.py:64
  150.1 7.3 %collective-permute-start.13 = (f32[19,1,16,128]{3,2,1,0:T(8,128)S(1)}, f32[19,1,16,128]{3,2,1,0:T(8,128)S(1)}, u32[]{:S(2)}, u32[]{:S(2)}) collective-permute-start(f32[19,1,16,128]{3,2,1,0:T(8,128)S(1)} %get-tuple-element.235), channel_id=1, source_target_pairs={{16,0},{32,16},{48,32},{64,48},{80,64},{96,80},{112,96},{0,112},{1... | collective-permute-start | bytes 466952 | tf_op jit(solution)/shard_map/ppermute | solution.py:64
  153.0 4.4 %collective-permute-start.12 = (f32[19,1,16,128]{3,2,1,0:T(8,128)S(1)}, f32[19,1,16,128]{3,2,1,0:T(8,128)S(1)}, u32[]{:S(2)}, u32[]{:S(2)}) collective-permute-start(f32[19,1,16,128]{3,2,1,0:T(8,128)S(1)} %get-tuple-element.234), channel_id=1, source_target_pairs={{0,16},{16,32},{32,48},{48,64},{64,80},{80,96},{96,112},{112,0},{1... | collective-permute-start | bytes 466952 | tf_op jit(solution)/shard_map/ppermute | solution.py:63
  160.7 11.0 %collective-permute-start.14 = (f32[19,34,1,128]{3,2,1,0:T(1,128)S(1)}, f32[19,34,1,128]{3,2,1,0:T(1,128)S(1)}, u32[]{:S(2)}, u32[]{:S(2)}) collective-permute-start(f32[19,34,1,128]{3,2,1,0:T(1,128)S(1)} %get-tuple-element.204), channel_id=1, source_target_pairs={{0,1},{1,2},{2,3},{3,4},{4,5},{5,6},{6,7},{7,8},{8,9},{9,10},{10,1... | collective-permute-start | bytes 992264 | tf_op jit(solution)/shard_map/ppermute | solution.py:63
  160.8 11.0 %collective-permute-start.15 = (f32[19,34,1,128]{3,2,1,0:T(1,128)S(1)}, f32[19,34,1,128]{3,2,1,0:T(1,128)S(1)}, u32[]{:S(2)}, u32[]{:S(2)}) collective-permute-start(f32[19,34,1,128]{3,2,1,0:T(1,128)S(1)} %get-tuple-element.205), channel_id=1, source_target_pairs={{1,0},{2,1},{3,2},{4,3},{5,4},{6,5},{7,6},{8,7},{9,8},{10,9},{11,1... | collective-permute-start | bytes 992264 | tf_op jit(solution)/shard_map/ppermute | solution.py:64
  199.7 14.3 %collective-permute-start.18 = (f32[3,32,1,128]{3,2,1,0:T(1,128)S(1)}, f32[3,32,1,128]{3,2,1,0:T(1,128)}, u32[]{:S(2)}, u32[]{:S(2)}) collective-permute-start(f32[3,32,1,128]{3,2,1,0:T(1,128)S(1)} %get-tuple-element.252), channel_id=1, source_target_pairs={{1,0},{2,1},{3,2},{4,3},{5,4},{6,5},{7,6},{8,7},{9,8},{10,9},{11,1... | collective-permute-start | bytes 147464 | tf_op jit(solution)/shard_map/ppermute | solution.py:45
  204.4 9.6 %collective-permute-start.17 = (f32[3,1,16,128]{3,2,1,0:T(8,128)}, f32[3,1,16,128]{3,2,1,0:T(8,128)S(1)}, u32[]{:S(2)}, u32[]{:S(2)}) collective-permute-start(f32[3,1,16,128]{3,2,1,0:T(8,128)} %get-tuple-element.255), channel_id=1, source_target_pairs={{16,0},{32,16},{48,32},{64,48},{80,64},{96,80},{112,96},{0,112},{1... | collective-permute-start | bytes 73736 | tf_op jit(solution)/shard_map/ppermute | solution.py:45
  207.5 6.5 %collective-permute-start.16 = (f32[3,1,16,128]{3,2,1,0:T(8,128)}, f32[3,1,16,128]{3,2,1,0:T(8,128)S(1)}, u32[]{:S(2)}, u32[]{:S(2)}) collective-permute-start(f32[3,1,16,128]{3,2,1,0:T(8,128)} %get-tuple-element.254), channel_id=1, source_target_pairs={{0,16},{16,32},{32,48},{48,64},{64,80},{80,96},{96,112},{112,0},{1... | collective-permute-start | bytes 73736 | tf_op jit(solution)/shard_map/ppermute | solution.py:44
  207.5 6.6 %collective-permute-start.19 = (f32[3,32,1,128]{3,2,1,0:T(1,128)S(1)}, f32[3,32,1,128]{3,2,1,0:T(1,128)}, u32[]{:S(2)}, u32[]{:S(2)}) collective-permute-start(f32[3,32,1,128]{3,2,1,0:T(1,128)S(1)} %get-tuple-element.253), channel_id=1, source_target_pairs={{0,1},{1,2},{2,3},{3,4},{4,5},{5,6},{6,7},{7,8},{8,9},{9,10},{10,1... | collective-permute-start | bytes 147464 | tf_op jit(solution)/shard_map/ppermute | solution.py:44
  220.1 34.7 %all-to-all-start = ((bf16[16,32,16,128]{3,2,1,0:T(8,128)(2,1)}), bf16[16,32,16,128]{3,2,1,0:T(8,128)(2,1)S(1)}, u32[]{:S(2)}, u32[]{:S(2)}) async-start(bf16[16,32,16,128]{3,2,1,0:T(8,128)(2,1)} %broadcast_in_dim.29), calls=%async_computation | async-start | bytes 4194304 | tf_op jit(solution)/shard_map/all_to_all | solution.py:71
  327.8 36.9 %copy-start.13 = (f32[32,16,1]{2,1,0:T(8,128)S(1)}, f32[32,16,1]{2,1,0:T(8,128)}, u32[]{:S(2)}) copy-start(f32[32,16,1]{2,1,0:T(8,128)} %copy-done.12) | copy-start | bytes 6148
  327.8 36.9 %copy-start.29 = (f32[32,16,127]{2,1,0:T(8,128)S(1)}, f32[32,16,127]{2,1,0:T(8,128)}, u32[]{:S(2)}) copy-start(f32[32,16,127]{2,1,0:T(8,128)} %get-tuple-element.270) | copy-start | bytes 780292
  356.2 17.1 %all-to-all-start.1 = ((f32[1,4,256,128]{3,1,0,2:T(4,128)}), f32[1,4,256,128]{3,1,0,2:T(4,128)S(1)}, u32[]{:S(2)}, u32[]{:S(2)}) async-start(f32[1,4,256,128]{3,1,0,2:T(4,128)} %copy.2321), calls=%async_computation.1 | async-start | bytes 1048576 | tf_op jit(solution)/shard_map/all_to_all | solution.py:191
  (149 other events, 1014.6 us)
where the time goes:
time: 381 us; the launch traced here: 375 us
  other arithmetic  187 us (49%)
  local copies, waits for them, and re-layouts  107 us (28%)
  starting transfers between devices  56 us (15%)
  waiting for transfers between devices  20.2 us (5%)
  between operations  4.67 us (1%)
    reduce_sum x3, other arithmetic, render_block(): jnp.sum(weight * emission[channel], axis=0)  81.2 us
    concatenate x65, local copies, waits for them, and re-layouts, stream(): window = jnp.roll(window, shift_z, axis=2)  57.5 us
    unnamed x81, other arithmetic  31.9 us
    ppermute x8, starting transfers between devices, with_halo_2(): after = lax.ppermute(first, axis, down)  31 us
    slice x70, local copies, waits for them, and re-layouts, stream(): window = jnp.roll(window, shift_z, axis=2)  18.8 us
    another operation x1, other arithmetic, render_block(): inclusive = jnp.cumsum(optical, axis=0)  17.8 us
    unnamed x311, local copies, waits for them, and re-layouts  17.6 us
    sub x8, other arithmetic, collide(): result.append(field[number] - relaxation * (field[number] - equilibrium))  15.8 us
  transfers between devices with their start and end apart: 22, of which 3 were waited for; matrix products, arithmetic and copies ran while one was open for 18% of the time, Pallas kernels for 0%

commit v1 on v0

v1 whole, which is shorter than its diff:
```python
import functools

import jax
import jax.numpy as jnp
import numpy as np
from jax import lax
from jax.experimental import pallas as pl
from jax.experimental.pallas import tpu as pltpu
from jax.sharding import PartitionSpec as P

VEL = (
    (0, 0, 0),
    (1, 0, 0), (-1, 0, 0), (0, 1, 0), (0, -1, 0), (0, 0, 1), (0, 0, -1),
    (1, 1, 0), (-1, -1, 0), (1, -1, 0), (-1, 1, 0),
    (1, 0, 1), (-1, 0, -1), (1, 0, -1), (-1, 0, 1),
    (0, 1, 1), (0, -1, -1), (0, 1, -1), (0, -1, 1),
)
WEIGHT = (1.0 / 3.0,) + (1.0 / 18.0,) * 6 + (1.0 / 36.0,) * 12
OMEGA = 1.25
Q = len(VEL)
STEPS = 4
HALO = STEPS + 1
AXIS_PAIRS = ((1, 2), (3, 4), (5, 6))
DIAG_PAIRS = ((7, 8), (9, 10), (11, 12), (13, 14), (15, 16), (17, 18))
SCALE = 8192.0

X_PAIRS = tuple(
    (a, b, 5) for a, b in zip((1, 7, 9, 11, 13), (2, 8, 10, 12, 14))
) + ((0, 3, 4), (4, 5, 4), (6, 15, 4), (16, 17, 4), (18, None, 4))


def low_rows(p):
    return 4 + VEL[p][0]


def face_list(nearest, step):
    sent = []
    for layer in range(1, HALO + 1):
        y = nearest + step * (layer - 1)
        for p in range(Q):
            inward = VEL[p][1] * (-step)
            if layer <= 4 + inward:
                sent.append((y, p))
    return sent


def momentum(f):
    s = {}
    d = {}
    for a, b in AXIS_PAIRS + DIAG_PAIRS:
        s[a] = f[a] + f[b]
        d[a] = f[a] - f[b]
    density = ((s[1] + s[3]) + (s[5] + s[7])) + ((s[9] + s[11]) + (s[13] + s[15])) + (s[17] + f[0])
    jx = (d[1] + d[7]) + (d[9] + d[11]) + d[13]
    jy = (d[3] + d[7]) - (d[9] - d[15]) + d[17]
    jz = (d[5] + d[11]) - (d[13] - d[15]) - d[17]
    return density, (jx, jy, jz), s, d


def collide(f):
    density, j, s, d = momentum(f)
    inverse = 1.0 / density
    u = [c * inverse for c in j]
    speed = j[0] * u[0] + j[1] * u[1] + j[2] * u[2]
    common = density - 1.5 * speed
    out = [None] * Q
    out[0] = (OMEGA * WEIGHT[0]) * common - (OMEGA - 1.0) * f[0]
    rest = 0.5 * (OMEGA - 1.0)
    for pairs, w in ((AXIS_PAIRS, WEIGHT[1]), (DIAG_PAIRS, WEIGHT[7])):
        base = (OMEGA * w) * common
        jw = [(3.0 * OMEGA * w) * c for c in j]
        uw = [1.5 * c for c in u]
        for a, b in pairs:
            project_j = None
            project_u = None
            for axis in range(3):
                c = VEL[a][axis]
                if c == 0:
                    continue
                if project_j is None:
                    assert c == 1
                    project_j, project_u = jw[axis], uw[axis]
                elif c > 0:
                    project_j, project_u = project_j + jw[axis], project_u + uw[axis]
                else:
                    project_j, project_u = project_j - jw[axis], project_u - uw[axis]
            even = (base + project_j * project_u) - rest * s[a]
            odd = project_j - rest * d[a]
            out[a] = even + odd
            out[b] = even - odd
    return out


def code(value, p):
    return jnp.round(value * (SCALE / WEIGHT[p]) - SCALE)


def decode(value, p):
    return value * (WEIGHT[p] / SCALE) + WEIGHT[p]


def row_index():
    return lax.broadcasted_iota(jnp.int32, (8, 128), 0)


def pack16(first, second):
    return jnp.concatenate([first, second], axis=0).astype(jnp.int32).astype(jnp.int16)


def wide(value):
    return value.astype(jnp.int32).astype(jnp.float32)


def first_kernel(depth_cells, width_cells, parity_ref, f_ref, r_ref, da_ref, db_ref, ia_ref, ib_ref):
    tiles = depth_cells // 8
    rows = row_index()

    def at_y(y, carry):
        for j in range(tiles):
            f = [
                f_ref[p, pl.ds(j * 8 * width_cells + y, 8, stride=width_cells), :]
                for p in range(Q)
            ]
            out = collide(f)
            for p in range(Q):
                r_ref[p, y, 8 * j : 8 * j + 8, :] = pltpu.roll(out[p], low_rows(p), 0)
        return carry

    lax.fori_loop(0, width_cells, at_y, 0)

    odd_depth = jnp.full((8, 128), parity_ref[0], jnp.int32) == 1
    odd_image = jnp.full((8, 128), parity_ref[1], jnp.int32) == 1

    def face_x(t, carry):
        for number, (a, b, n) in enumerate(X_PAIRS):
            low, high = [], []
            for k in range(2):
                y = 2 * t + k
                for sent, first_row in ((low, 0), (high, depth_cells - 8)):
                    piece = code(r_ref[a, y, first_row : first_row + 8, :], a)
                    if b is not None:
                        other = code(r_ref[b, y, first_row : first_row + 8, :], b)
                        other = pltpu.roll(other, n, 0)
                        keep = rows < n if sent is high else rows >= n
                        piece = jnp.where(keep, piece, other)
                    sent.append(piece)
            da = [jnp.where(odd_depth, l, h) for l, h in zip(low, high)]
            db = [jnp.where(odd_depth, h, l) for l, h in zip(low, high)]
            da_ref[number, t] = pack16(*da)
            db_ref[number, t] = pack16(*db)
        return carry

    lax.fori_loop(0, width_cells // 2, face_x, 0)

    low_face = face_list(0, 1)
    high_face = face_list(width_cells - 1, -1)
    for index, ((yl, pl_), (yh, ph)) in enumerate(zip(low_face, high_face)):
        for c in range(depth_cells // 16):
            a, b = [], []
            for k in range(2):
                first_row = 16 * c + 8 * k
                low = code(r_ref[pl_, yl, first_row : first_row + 8, :], pl_)
                high = code(r_ref[ph, yh, first_row : first_row + 8, :], ph)
                a.append(jnp.where(odd_image, low, high))
                b.append(jnp.where(odd_image, high, low))
            ia_ref[index, 16 * c : 16 * c + 16, :] = pack16(*a)
            ib_ref[index, 16 * c : 16 * c + 16, :] = pack16(*b)


def x_halo(low, high, n, second, rows):
    if second:
        low = pltpu.roll(low, 8 - n, 0)
        high = pltpu.roll(high, 8 - n, 0)
        n = 8 - n
    return jnp.where(rows < n, low, high)


X_PLACE = {}
for number_, (a_, b_, n_) in enumerate(X_PAIRS):
    X_PLACE[a_] = (number_, n_, False)
    if b_ is not None:
        X_PLACE[b_] = (number_, n_, True)


def corner_kernel(width_cells, parity_ref, xa_ref, xb_ref, h_ref, ca_ref, cb_ref):
    rows = row_index()
    odd_depth = jnp.full((8, 128), parity_ref[0], jnp.int32) == 1
    odd_image = jnp.full((8, 128), parity_ref[1], jnp.int32) == 1

    def halo(t, carry):
        for number, (a, b, n) in enumerate(X_PAIRS):
            va = wide(xa_ref[number, t])
            vb = wide(xb_ref[number, t])
            for k in range(2):
                pa, pb = va[8 * k : 8 * k + 8], vb[8 * k : 8 * k + 8]
                low = jnp.where(odd_depth, pa, pb)
                high = jnp.where(odd_depth, pb, pa)
                h_ref[a, 2 * t + k] = x_halo(low, high, n, False, rows)
                if b is not None:
                    h_ref[b, 2 * t + k] = x_halo(low, high, n, True, rows)
        return carry

    lax.fori_loop(0, width_cells // 2, halo, 0)
    low_face = face_list(0, 1)
    high_face = face_list(width_cells - 1, -1)
    for index in range(0, len(low_face), 2):
        a, b = [], []
        for (yl, pl_), (yh, ph) in zip(low_face[index : index + 2], high_face[index : index + 2]):
            low, high = h_ref[pl_, yl], h_ref[ph, yh]
            a.append(jnp.where(odd_image, low, high))
            b.append(jnp.where(odd_image, high, low))
        ca_ref[index // 2] = pack16(*a)
        cb_ref[index // 2] = pack16(*b)


PAD = 8


def steps_kernel(
    depth_cells, width_cells, parity_ref, r_ref, h_ref, ya_ref, yb_ref, ca_ref, cb_ref,
    out_ref, vort_ref, sa_ref, sb_ref, flow_ref, plain_ref,
):
    tiles = depth_cells // 8
    wide_tiles = tiles + 1
    rows = row_index()
    odd_image = jnp.full((8, 128), parity_ref[1], jnp.int32) == 1

    def streamed(p, y, pieces, halo):
        n = low_rows(p)
        before = halo
        for t in range(wide_tiles):
            here = pieces[t] if t < tiles else halo
            sa_ref[p, y, PAD + 8 * t : PAD + 8 * t + 8, :] = jnp.where(rows < n, before, here)
            before = here

    def own(y, carry):
        for p in range(Q):
            pieces = [r_ref[p, y, 8 * t : 8 * t + 8, :] for t in range(tiles)]
            streamed(p, y + HALO, pieces, decode(h_ref[p, y], p))
        return carry

    lax.fori_loop(0, width_cells, own, 0)

    low_face = face_list(0, 1)
    high_face = face_list(width_cells - 1, -1)
    for index in range(0, len(low_face), 2):
        corner_a, corner_b = wide(ca_ref[index // 2]), wide(cb_ref[index // 2])
        for k in range(2):
            (yl, pl_), (yh, ph) = low_face[index + k], high_face[index + k]
            ca, cb = corner_a[8 * k : 8 * k + 8], corner_b[8 * k : 8 * k + 8]
            low = [jnp.where(odd_image, ca, cb)]
            high = [jnp.where(odd_image, cb, ca)]
            for c in range(depth_cells // 16):
                ya = wide(ya_ref[index + k, 16 * c : 16 * c + 16, :])
                yb = wide(yb_ref[index + k, 16 * c : 16 * c + 16, :])
                for half in range(2):
                    a, b = ya[8 * half : 8 * half + 8], yb[8 * half : 8 * half + 8]
                    low.append(jnp.where(odd_image, a, b))
                    high.append(jnp.where(odd_image, b, a))
            low = [decode(v, ph) for v in low]
            high = [decode(v, pl_) for v in high]
            streamed(ph, yh - width_cells + HALO, low[1:], low[0])
            streamed(pl_, yl + width_cells + HALO, high[1:], high[0])

    def step(source, target, reach, shift):
        def at_y(y, carry):
            for t in range(wide_tiles):
                first = PAD + 8 * t
                f = [source[p, y - VEL[p][1], first : first + 8, :] for p in range(Q)]
                out = collide(f)
                for p in range(Q):
                    cx, _, cz = VEL[p]
                    value = out[p] if cz == 0 else pltpu.roll(out[p], cz % 128, 1)
                    row = first + shift + cx
                    target[p, y, row : row + 8, :] = value
            return carry

        lax.fori_loop(HALO - reach, HALO + width_cells + reach, at_y, 0)

    def first_step(source, target, reach):
        def at_y(y, carry):
            for t in range(wide_tiles):
                first = PAD + 8 * t
                f = []
                for p in range(Q):
                    cz = VEL[p][2]
                    value = source[p, y - VEL[p][1], first : first + 8, :]
                    f.append(value if cz == 0 else pltpu.roll(value, cz % 128, 1))
                out = collide(f)
                for p in range(Q):
                    cx, _, cz = VEL[p]
                    value = out[p] if cz == 0 else pltpu.roll(out[p], cz % 128, 1)
                    target[p, y, first + cx : first + cx + 8, :] = value
            return carry

        lax.fori_loop(HALO - reach, HALO + width_cells + reach, at_y, 0)

    first_step(sa_ref, sb_ref, 4)
    step(sb_ref, sa_ref, 3, 0)
    step(sa_ref, sb_ref, 2, 4)
    base = PAD + 8

    def flow_at(y, carry):
        for t in range(-1, tiles + 1):
            first = base + 8 * t
            f = [sb_ref[p, y - VEL[p][1], first : first + 8, :] for p in range(Q)]
            density, j, _, _ = momentum(f)
            inverse = 1.0 / density
            for axis in range(3):
                flow_ref[axis, y, first : first + 8, :] = j[axis] * inverse
        return carry

    lax.fori_loop(HALO - 1, HALO + width_cells + 1, flow_at, 0)

    def final_at(y, carry):
        for t in range(tiles):
            first = base + 8 * t
            for p in range(Q):
                out_ref[p, pl.ds(8 * t * width_cells + y - HALO, 8, stride=width_cells), :] = sb_ref[
                    p, y - VEL[p][1], first : first + 8, :
                ]
        return carry

    lax.fori_loop(HALO, HALO + width_cells, final_at, 0)

    def spin_at(y, carry):
        for t in range(tiles):
            first = base + 8 * t

            def dx(axis):
                return (flow_ref[axis, y, first + 1 : first + 9, :] - flow_ref[axis, y, first - 1 : first + 7, :]) * 0.5

            def dy(axis):
                return (flow_ref[axis, y + 1, first : first + 8, :] - flow_ref[axis, y - 1, first : first + 8, :]) * 0.5

            def dz(axis):
                value = flow_ref[axis, y, first : first + 8, :]
                return (pltpu.roll(value, 127, 1) - pltpu.roll(value, 1, 1)) * 0.5

            sx = dy(2) - dz(1)
            sy = dz(0) - dx(2)
            sz = dx(1) - dy(0)
            plain_ref[pl.ds(8 * t * width_cells + y - HALO, 8, stride=width_cells), :] = jnp.sqrt(
                sx * sx + sy * sy + sz * sz
            )
        return carry

    lax.fori_loop(HALO, HALO + width_cells, spin_at, 0)

    def rounded(x, carry):
        at = pl.ds(pl.multiple_of(x * 16, 16), 16)
        vort_ref[at, :] = plain_ref[at, :].astype(jnp.bfloat16)
        return carry

    lax.fori_loop(0, depth_cells * width_cells // 16, rounded, 0)


BUMP_WIDTH = 0.15
LEVEL_OFFSET = 0.05
STRETCH = float(np.sqrt(np.log2(np.e)) / BUMP_WIDTH)
CENTRE = 4.0
LOG2E = float(np.log2(np.e))


def bump_tables(transfer, ray_cells):
    b = STRETCH * transfer[:, 0] - CENTRE
    fade = jnp.exp2(-b * b)
    strength = transfer[:, 1:] * fade[:, None]
    strength = strength.at[:, 0].multiply(LOG2E / ray_cells)
    return jnp.concatenate([(2.0 * b)[:, None], strength], axis=1)


def render_kernel(depth_cells, width_cells, groups, pick_ref, table_ref, backward_ref, vort_ref, image_ref, place_ref, fade_ref):
    bumps = table_ref.shape[1] // 5

    def prepare(x, carry):
        at = pl.ds(pl.multiple_of(x * width_cells, width_cells), width_cells)
        value = vort_ref[at, :].astype(jnp.float32)
        level = value / (value + LEVEL_OFFSET)
        place = STRETCH * level - CENTRE
        place_ref[x] = place
        fade_ref[x] = jnp.exp2(-place * place)
        return carry

    lax.fori_loop(0, depth_cells, prepare, 0)

    def one(group, carry):
        m = 2 * group + pick_ref[0]
        backward = backward_ref[m]
        centre = [table_ref[m, k] for k in range(bumps)]
        strength = [[table_ref[m, (1 + c) * bumps + k] for k in range(bumps)] for c in range(4)]

        def cell(step, state):
            clear, red, green, blue = state
            x = jnp.where(backward == 1, depth_cells - 1 - step, step)
            place, fade = place_ref[x], fade_ref[x]
            total = [None] * 4
            for k in range(bumps):
                bump = jnp.exp2(place * centre[k])
                for c in range(4):
                    term = bump * strength[c][k]
                    total[c] = term if total[c] is None else total[c] + term
            behind = clear * jnp.exp2(-(total[0] * fade))
            weight = (clear - behind) * fade
            return (behind, red + weight * total[1], green + weight * total[2], blue + weight * total[3])

        zero = jnp.zeros((width_cells, 128), jnp.float32)
        clear, red, green, blue = lax.fori_loop(0, depth_cells, cell, (zero + 1.0, zero, zero, zero))
        image_ref[group, 0] = red
        image_ref[group, 1] = green
        image_ref[group, 2] = blue
        image_ref[group, 3] = clear
        return carry

    lax.fori_loop(0, groups, one, 0)


def composite_kernel(slabs, pick_ref, backward_ref, piece_ref, image_ref):
    backward = backward_ref[pick_ref[0]]
    shape = piece_ref.shape[2:]
    clear = jnp.ones(shape, jnp.float32)
    color = [jnp.zeros(shape, jnp.float32) for c in range(3)]
    for step in range(slabs):
        s = jnp.where(backward == 1, slabs - 1 - step, step)
        color = [color[c] + clear * piece_ref[s, c] for c in range(3)]
        clear = clear * piece_ref[s, 3]
    for c in range(3):
        image_ref[c] = color[c]
    image_ref[3] = 1.0 - clear


VMEM = pl.BlockSpec(memory_space=pltpu.VMEM)
SMEM = pl.BlockSpec(memory_space=pltpu.SMEM)
GRANT = pltpu.CompilerParams(vmem_limit_bytes=58 * 1024 * 1024)


def partner(index, count, phase):
    return index ^ 1 if phase == 0 else (((index + 1) ^ 1) - 1) % count


def swap(value, axis, count, phase):
    return lax.ppermute(value, axis, [(i, partner(i, count, phase)) for i in range(count)])


def on_device(populations, transfer, direction):
    _, depth_cells, width_cells, lanes = populations.shape
    depth_count, image_count = lax.axis_size("depth"), lax.axis_size("image")
    ray_cells = depth_cells * depth_count
    cells = depth_cells * width_cells
    f32, i16 = jnp.float32, jnp.int16
    d, i = lax.axis_index("depth"), lax.axis_index("image")
    parity = jnp.stack([d % 2, i % 2]).astype(jnp.int32)
    faces = len(face_list(0, 1))

    tables = lax.all_gather(
        jnp.concatenate([transfer.reshape(1, -1), direction.astype(f32)[:, None]], axis=1),
        "image", axis=0, tiled=True,
    )
    backward = tables[:, -1].astype(jnp.int32)
    bumps = transfer.shape[2]
    tables = bump_tables(tables[:, :-1].reshape(-1, 5, bumps), ray_cells).reshape(-1, 5 * bumps)

    x_shape = jax.ShapeDtypeStruct((len(X_PAIRS), width_cells // 2, 16, lanes), i16)
    y_shape = jax.ShapeDtypeStruct((faces, depth_cells, lanes), i16)
    c_shape = jax.ShapeDtypeStruct((faces // 2, 16, lanes), i16)
    turned, da, db, ia, ib = pl.pallas_call(
        functools.partial(first_kernel, depth_cells, width_cells),
        out_shape=(
            jax.ShapeDtypeStruct((Q, width_cells, depth_cells, lanes), f32),
            x_shape, x_shape, y_shape, y_shape,
        ),
        in_specs=[SMEM, VMEM],
        out_specs=(VMEM,) * 5,
        compiler_params=GRANT,
        name="first",
    )(parity, populations.reshape(Q, cells, lanes))

    xa = swap(da, "depth", depth_count, 0)
    xb = swap(db, "depth", depth_count, 1)
    ya = swap(ia, "image", image_count, 0)
    yb = swap(ib, "image", image_count, 1)
    halo, ca, cb = pl.pallas_call(
        functools.partial(corner_kernel, width_cells),
        out_shape=(jax.ShapeDtypeStruct((Q, width_cells, 8, lanes), f32), c_shape, c_shape),
        in_specs=[SMEM, VMEM, VMEM],
        out_specs=(VMEM,) * 3,
        compiler_params=GRANT,
        name="corner",
    )(parity, xa, xb)
    ca = swap(ca, "image", image_count, 0)
    cb = swap(cb, "image", image_count, 1)

    depth_rows = depth_cells + 8 + 2 * PAD
    width_rows = width_cells + 2 * HALO
    final, vorticity = pl.pallas_call(
        functools.partial(steps_kernel, depth_cells, width_cells),
        out_shape=(
            jax.ShapeDtypeStruct((Q, cells, lanes), f32),
            jax.ShapeDtypeStruct((cells, lanes), jnp.bfloat16),
        ),
        in_specs=[SMEM] + [VMEM] * 6,
        out_specs=(VMEM, VMEM),
        scratch_shapes=[
            pltpu.VMEM((Q, width_rows, depth_rows, lanes), f32),
            pltpu.VMEM((Q, width_rows, depth_rows, lanes), f32),
            pltpu.VMEM((3, width_rows, depth_rows, lanes), f32),
            pltpu.VMEM((cells, lanes), f32),
        ],
        compiler_params=GRANT,
        name="steps",
    )(parity, turned, halo, ya, yb, ca, cb)

    groups = depth_count
    pieces = []
    for k in range(2):
        pick = ((i + k) % 2).astype(jnp.int32)[None]
        partial = pl.pallas_call(
            functools.partial(render_kernel, depth_cells, width_cells, groups),
            out_shape=jax.ShapeDtypeStruct((groups, 4, width_cells, lanes), f32),
            in_specs=[SMEM, SMEM, SMEM, VMEM],
            out_specs=VMEM,
            scratch_shapes=[
                pltpu.VMEM((depth_cells, width_cells, lanes), f32),
                pltpu.VMEM((depth_cells, width_cells, lanes), f32),
            ],
            compiler_params=GRANT,
            name="render",
        )(pick, tables, backward, vorticity)
        slabs = lax.all_to_all(partial, "depth", 0, 0, tiled=True)
        image = pl.pallas_call(
            functools.partial(composite_kernel, depth_count),
            out_shape=jax.ShapeDtypeStruct((4, width_cells, lanes), f32),
            in_specs=[SMEM, SMEM, VMEM],
            out_specs=VMEM,
            name="composite",
        )(2 * d.astype(jnp.int32)[None] + pick, backward, slabs)
        route = []
        for sd in range(depth_count):
            for si in range(image_count):
                route.append((sd * image_count + si, (si // 2) * image_count + 2 * sd + (si + k) % 2))
        pieces.append(lax.ppermute(image, ("depth", "image"), route))
    flip = (i % 2) == 1
    top = jnp.where(flip, pieces[1], pieces[0])
    bottom = jnp.where(flip, pieces[0], pieces[1])
    images = jnp.concatenate([top, bottom], axis=1)[None]
    return (
        final.reshape(populations.shape),
        vorticity.reshape(depth_cells, width_cells, lanes),
        images,
    )


def solution(mesh):
    in_specs = (P(None, "depth", "image", None), P("image", None, None), P("image"))
    out_specs = (
        P(None, "depth", "image", None),
        P("depth", "image", None),
        P("image", None, "depth", None),
    )
    return jax.shard_map(
        on_device, mesh=mesh, in_specs=in_specs, out_specs=out_specs, check_vma=False
    )
```

time: 381 us -> 139 us (0.36)
  the two profiles are of different devices: /device:TPU:1 before, /device:TPU:17 now
where the time goes in v1:
time: 139 us; the launch traced here: 138 us
  Pallas kernels  65 us (47%)
  starting transfers between devices  30.9 us (22%)
  blocking collectives  23.9 us (17%)
  waiting for transfers between devices  10.8 us (8%)
  local copies, waits for them, and re-layouts  4.07 us (3%)
  other arithmetic  1.95 us (1%)
    pallas_call x1, Pallas kernels, on_device(): pl.pallas_call(functools.partial(steps_kernel, depth_cells, width_cells),...  26.6 us
    all_gather x1, blocking collectives, on_device(): lax.all_gather(jnp.concatenate([transfer.reshape(1, -1), direction.astype...  23.9 us
    pallas_call x2, Pallas kernels, on_device(): pl.pallas_call(functools.partial(render_kernel, depth_cells, width_cells,...  23.5 us
    all_to_all x2, starting transfers between devices, on_device(): slabs = lax.all_to_all(partial, 'depth', 0, 0, tiled=True)  14.5 us
    ppermute x6, starting transfers between devices, swap(): lax.ppermute(value, axis, [(i, partner(i, count, phase)) for i in range(c...  9.89 us
    pallas_call x1, Pallas kernels, on_device(): pl.pallas_call(functools.partial(first_kernel, depth_cells, width_cells),...  9.3 us
    ppermute x2, starting transfers between devices, on_device(): pieces.append(lax.ppermute(image, ('depth', 'image'), route))  6.55 us
    ppermute x6, waiting for transfers between devices, swap(): lax.ppermute(value, axis, [(i, partner(i, count, phase)) for i in range(c...  5.27 us
  transfers between devices with their start and end apart: 10, of which 5 were waited for; matrix products, arithmetic and copies ran while one was open for 1% of the time, Pallas kernels for 13%

profile of v1, /device:TPU:17, one launch (start us, length us, event | category | flops | bytes accessed | tf_op | source)
XLA Modules:
  0.0 138.1 jit_solution(15327625515925626202)
XLA Ops:
  1.3 9.3 %first.1 = (f32[19,16,32,128]{3,2,1,0:T(8,128)}, s16[10,8,16,128]{3,2,1,0:T(8,128)(2,1)}, s16[10,8,16,128]{3,2,1,0:T(8,128)(2,1)}, s16[76,32,128]{2,1,0:T(8,128)(2,1)}, s16[76,32,128]{2,1,0:T(8,128)(2,1)}) custom-call(s32[2]{0:T(128)} %pad_add_fusion.parity_ref, f32[19,512,128]{2,1,0:T(8,128)} %bitcast.21), custom_call_target="tpu_custom_call" | custom-call | tf_op jit(solution)/shard_map/first/pallas_call | solution.py:466
  10.6 0.7 collective-permute-start
  11.3 0.9 collective-permute-start.1
  12.2 1.2 collective-permute-start.2
  13.4 5.3 %collective-permute-start.3 = (s16[76,32,128]{2,1,0:T(8,128)(2,1)}, s16[76,32,128]{2,1,0:T(8,128)(2,1)S(1)}, u32[]{:S(2)}, u32[]{:S(2)}) collective-permute-start(s16[76,32,128]{2,1,0:T(8,128)(2,1)} %get-tuple-element.30), channel_id=1, source_target_pairs={{0,15},{1,2},{2,1},{3,4},{4,3},{5,6},{6,5},{7,8},{8,7},{9,10},{10,... | collective-permute-start | bytes 1867784 | tf_op jit(solution)/shard_map/ppermute | solution.py:442
  19.5 23.9 %all-gather = f32[16,1,41]{2,1,0:T(1,128)S(1)} all-gather(f32[1,1,41]{2,1,0:T(1,128)S(1)} %maximum_bitcast_fusion.2), channel_id=1, replica_groups=mesh['depth'=8,'image'=16] {'image'}, dimensions={0}, use_global_device_ids=true | all-gather | bytes 2788 | tf_op jit(solution)/shard_map/all_gather | solution.py:455
  44.2 0.7 copy-done.4
  45.0 0.7 copy-done.5
  45.7 2.5 %corner.1 = (f32[19,16,8,128]{3,2,1,0:T(8,128)}, s16[38,16,128]{2,1,0:T(8,128)(2,1)}, s16[38,16,128]{2,1,0:T(8,128)(2,1)}) custom-call(s32[2]{0:T(128)} %pad_add_fusion.parity_ref, s16[10,8,16,128]{3,2,1,0:T(8,128)(2,1)} %copy-done.4, s16[10,8,16,128]{3,2,1,0:T(8,128)(2,1)} %copy-done.5), custom_call_target="tpu_custom_call" | custom-call | tf_op jit(solution)/shard_map/corner/pallas_call | solution.py:482
  48.2 1.8 %collective-permute-start.5 = (s16[38,16,128]{2,1,0:T(8,128)(2,1)}, s16[38,16,128]{2,1,0:T(8,128)(2,1)S(1)}, u32[]{:S(2)}, u32[]{:S(2)}) collective-permute-start(s16[38,16,128]{2,1,0:T(8,128)(2,1)} %get-tuple-element.32), channel_id=1, source_target_pairs={{0,15},{1,2},{2,1},{3,4},{4,3},{5,6},{6,5},{7,8},{8,7},{9,10},{10,... | collective-permute-start | bytes 466952 | tf_op jit(solution)/shard_map/ppermute | solution.py:442
  50.5 1.9 %collective-permute-done.4.ca_ref = s16[38,16,128]{2,1,0:T(8,128)(2,1)S(1)} collective-permute-done((s16[38,16,128]{2,1,0:T(8,128)(2,1)}, s16[38,16,128]{2,1,0:T(8,128)(2,1)S(1)}, u32[]{:S(2)}, u32[]{:S(2)}) %collective-permute-start.4) | collective-permute-done | bytes 155680 | tf_op jit(solution)/shard_map/ppermute | solution.py:442
  52.5 3.3 %collective-permute-done.5.cb_ref = s16[38,16,128]{2,1,0:T(8,128)(2,1)S(1)} collective-permute-done((s16[38,16,128]{2,1,0:T(8,128)(2,1)}, s16[38,16,128]{2,1,0:T(8,128)(2,1)S(1)}, u32[]{:S(2)}, u32[]{:S(2)}) %collective-permute-start.5) | collective-permute-done | bytes 155680 | tf_op jit(solution)/shard_map/ppermute | solution.py:442
  56.9 26.6 %steps.1 = (f32[19,512,128]{2,1,0:T(8,128)}, bf16[512,128]{1,0:T(8,128)(2,1)}) custom-call(s32[2]{0:T(128)} %pad_add_fusion.parity_ref, f32[19,16,32,128]{3,2,1,0:T(8,128)} %get-tuple-element.25.r_ref, f32[19,16,8,128]{3,2,1,0:T(8,128)} %get-tuple-element.28.h_ref, s16[76,32,128]{2,1,0:T(8,128)(2,1)} %copy-done.2, s16[76,32,128]{2,1,0:T(8,128)(2,1)} %copy-done.3, ...), custom_call_target="tpu_custom_call" | custom-call | tf_op jit(solution)/shard_map/steps/pallas_call | solution.py:495
  83.5 11.7 %render.3 = f32[8,4,16,128]{3,2,1,0:T(8,128)} custom-call(s32[1]{0:T(128)} %bitcast.1.pick_ref, f32[16,40]{1,0:T(8,128)} %copy.13.table_ref, s32[16]{0:T(128)} %fusion.6.backward_ref, bf16[512,128]{1,0:T(8,128)(2,1)} %get-tuple-element.34.vort_ref), custom_call_target="tpu_custom_call" | custom-call | tf_op jit(solution)/shard_map/render/pallas_call | solution.py:517
  95.2 9.7 %all-to-all-start.1 = ((f32[8,4,16,128]{3,2,1,0:T(8,128)}), f32[8,4,16,128]{3,2,1,0:T(8,128)S(1)}, u32[]{:S(2)}, u32[]{:S(2)}) async-start(f32[8,4,16,128]{3,2,1,0:T(8,128)} %render.3), calls=%async_computation.1 | async-start | bytes 524288 | tf_op jit(solution)/shard_map/all_to_all | solution.py:529
  104.9 11.7 %render.2 = f32[8,4,16,128]{3,2,1,0:T(8,128)} custom-call(s32[1]{0:T(128)} %bitcast.6.pick_ref, f32[16,40]{1,0:T(8,128)} %copy.13.table_ref, s32[16]{0:T(128)} %fusion.6.backward_ref, bf16[512,128]{1,0:T(8,128)(2,1)} %get-tuple-element.34.vort_ref), custom_call_target="tpu_custom_call" | custom-call | tf_op jit(solution)/shard_map/render/pallas_call | solution.py:517
  116.6 4.8 %all-to-all-start = ((f32[8,4,16,128]{3,2,1,0:T(8,128)}), f32[8,4,16,128]{3,2,1,0:T(8,128)S(1)}, u32[]{:S(2)}, u32[]{:S(2)}) async-start(f32[8,4,16,128]{3,2,1,0:T(8,128)} %render.2), calls=%async_computation | async-start | bytes 524288 | tf_op jit(solution)/shard_map/all_to_all | solution.py:529
  121.4 1.6 %composite.3 = f32[4,16,128]{2,1,0:T(8,128)} custom-call(s32[1]{0:T(128)S(6)} %add.31.pick_ref, s32[16]{0:T(128)} %fusion.6.backward_ref, f32[8,4,16,128]{3,2,1,0:T(8,128)} %copy-done), custom_call_target="tpu_custom_call" | custom-call | tf_op jit(solution)/shard_map/composite/pallas_call | solution.py:530
  123.0 1.9 %collective-permute-start.7 = (f32[4,16,128]{2,1,0:T(8,128)}, f32[4,16,128]{2,1,0:T(8,128)S(1)}, u32[]{:S(2)}, u32[]{:S(2)}) collective-permute-start(f32[4,16,128]{2,1,0:T(8,128)} %composite.3), channel_id=1, source_target_pairs={{0,0},{1,1},{2,16},{3,17},{4,32},{5,33},{6,48},{7,49},{8,64},{9,65... | collective-permute-start | bytes 98312 | tf_op jit(solution)/shard_map/ppermute | solution.py:541
  125.6 0.7 copy-done.1
  126.3 1.6 %composite.2 = f32[4,16,128]{2,1,0:T(8,128)} custom-call(s32[1]{0:T(128)S(6)} %add.30.pick_ref, s32[16]{0:T(128)} %fusion.6.backward_ref, f32[8,4,16,128]{3,2,1,0:T(8,128)} %copy-done.1), custom_call_target="tpu_custom_call" | custom-call | tf_op jit(solution)/shard_map/composite/pallas_call | solution.py:530
  127.9 4.6 %collective-permute-start.6 = (f32[4,16,128]{2,1,0:T(8,128)}, f32[4,16,128]{2,1,0:T(8,128)S(1)}, u32[]{:S(2)}, u32[]{:S(2)}) collective-permute-start(f32[4,16,128]{2,1,0:T(8,128)} %composite.2), channel_id=1, source_target_pairs={{0,1},{1,0},{2,17},{3,16},{4,33},{5,32},{6,49},{7,48},{8,65},{9,64... | collective-permute-start | bytes 98312 | tf_op jit(solution)/shard_map/ppermute | solution.py:541
  132.5 2.5 %collective-permute-done.7 = f32[4,16,128]{2,1,0:T(8,128)S(1)} collective-permute-done((f32[4,16,128]{2,1,0:T(8,128)}, f32[4,16,128]{2,1,0:T(8,128)S(1)}, u32[]{:S(2)}, u32[]{:S(2)}) %collective-permute-start.7) | collective-permute-done | bytes 32800 | tf_op jit(solution)/shard_map/ppermute | solution.py:541
  135.0 2.5 %collective-permute-done.6 = f32[4,16,128]{2,1,0:T(8,128)S(1)} collective-permute-done((f32[4,16,128]{2,1,0:T(8,128)}, f32[4,16,128]{2,1,0:T(8,128)S(1)}, u32[]{:S(2)}, u32[]{:S(2)}) %collective-permute-start.6) | collective-permute-done | bytes 32800 | tf_op jit(solution)/shard_map/ppermute | solution.py:541
  (36 shorter events, 4.6 us)
Async XLA Ops:
  0.6 18.1 %copy-start.8 = (f32[1,5,8]{2,0,1:T(1,128)S(1)}, f32[1,5,8]{2,0,1:T(1,128)}, u32[]{:S(2)}) copy-start(f32[1,5,8]{2,0,1:T(1,128)} %param.6) | copy-start | bytes 484
  10.6 33.6 %collective-permute-start = (s16[10,8,16,128]{3,2,1,0:T(8,128)(2,1)}, s16[10,8,16,128]{3,2,1,0:T(8,128)(2,1)S(1)}, u32[]{:S(2)}, u32[]{:S(2)}) collective-permute-start(s16[10,8,16,128]{3,2,1,0:T(8,128)(2,1)} %get-tuple-element.26), channel_id=1, source_target_pairs={{0,16},{16,0},{32,48},{48,32},{64,80},{80,64},{96,112},{112,96},{1... | collective-permute-start | bytes 983048 | tf_op jit(solution)/shard_map/ppermute | solution.py:442
  11.3 32.9 %collective-permute-start.1 = (s16[10,8,16,128]{3,2,1,0:T(8,128)(2,1)}, s16[10,8,16,128]{3,2,1,0:T(8,128)(2,1)S(1)}, u32[]{:S(2)}, u32[]{:S(2)}) collective-permute-start(s16[10,8,16,128]{3,2,1,0:T(8,128)(2,1)} %get-tuple-element.27), channel_id=1, source_target_pairs={{0,112},{16,32},{32,16},{48,64},{64,48},{80,96},{96,80},{112,0},{1... | collective-permute-start | bytes 983048 | tf_op jit(solution)/shard_map/ppermute | solution.py:442
  12.2 43.6 %collective-permute-start.2 = (s16[76,32,128]{2,1,0:T(8,128)(2,1)}, s16[76,32,128]{2,1,0:T(8,128)(2,1)S(1)}, u32[]{:S(2)}, u32[]{:S(2)}) collective-permute-start(s16[76,32,128]{2,1,0:T(8,128)(2,1)} %get-tuple-element.29), channel_id=1, source_target_pairs={{0,1},{1,0},{2,3},{3,2},{4,5},{5,4},{6,7},{7,6},{8,9},{9,8},{10,11... | collective-permute-start | bytes 1867784 | tf_op jit(solution)/shard_map/ppermute | solution.py:442
  13.4 42.4 %collective-permute-start.3 = (s16[76,32,128]{2,1,0:T(8,128)(2,1)}, s16[76,32,128]{2,1,0:T(8,128)(2,1)S(1)}, u32[]{:S(2)}, u32[]{:S(2)}) collective-permute-start(s16[76,32,128]{2,1,0:T(8,128)(2,1)} %get-tuple-element.30), channel_id=1, source_target_pairs={{0,15},{1,2},{2,1},{3,4},{4,3},{5,6},{6,5},{7,8},{8,7},{9,10},{10,... | collective-permute-start | bytes 1867784 | tf_op jit(solution)/shard_map/ppermute | solution.py:442
  44.2 0.7 copy-start.4
  44.9 0.7 copy-start.5
  48.2 4.3 %collective-permute-start.4 = (s16[38,16,128]{2,1,0:T(8,128)(2,1)}, s16[38,16,128]{2,1,0:T(8,128)(2,1)S(1)}, u32[]{:S(2)}, u32[]{:S(2)}) collective-permute-start(s16[38,16,128]{2,1,0:T(8,128)(2,1)} %get-tuple-element.31), channel_id=1, source_target_pairs={{0,1},{1,0},{2,3},{3,2},{4,5},{5,4},{6,7},{7,6},{8,9},{9,8},{10,11... | collective-permute-start | bytes 466952 | tf_op jit(solution)/shard_map/ppermute | solution.py:442
  48.2 7.6 %collective-permute-start.5 = (s16[38,16,128]{2,1,0:T(8,128)(2,1)}, s16[38,16,128]{2,1,0:T(8,128)(2,1)S(1)}, u32[]{:S(2)}, u32[]{:S(2)}) collective-permute-start(s16[38,16,128]{2,1,0:T(8,128)(2,1)} %get-tuple-element.32), channel_id=1, source_target_pairs={{0,15},{1,2},{2,1},{3,4},{4,3},{5,6},{6,5},{7,8},{8,7},{9,10},{10,... | collective-permute-start | bytes 466952 | tf_op jit(solution)/shard_map/ppermute | solution.py:442
  52.5 3.3 %copy-start.6 = (s16[38,16,128]{2,1,0:T(8,128)(2,1)}, s16[38,16,128]{2,1,0:T(8,128)(2,1)S(1)}, u32[]{:S(2)}) copy-start(s16[38,16,128]{2,1,0:T(8,128)(2,1)S(1)} %collective-permute-done.4.ca_ref) | copy-start | bytes 466948
  55.8 0.7 copy-start.7
  55.8 0.9 copy-start.2
  55.8 1.1 copy-start.3
  95.2 21.4 %all-to-all-start.1 = ((f32[8,4,16,128]{3,2,1,0:T(8,128)}), f32[8,4,16,128]{3,2,1,0:T(8,128)S(1)}, u32[]{:S(2)}, u32[]{:S(2)}) async-start(f32[8,4,16,128]{3,2,1,0:T(8,128)} %render.3), calls=%async_computation.1 | async-start | bytes 524288 | tf_op jit(solution)/shard_map/all_to_all | solution.py:529
  116.6 4.8 %copy-start = (f32[8,4,16,128]{3,2,1,0:T(8,128)}, f32[8,4,16,128]{3,2,1,0:T(8,128)S(1)}, u32[]{:S(2)}) copy-start(f32[8,4,16,128]{3,2,1,0:T(8,128)S(1)} %all-to-all-done.1.piece_ref) | copy-start | bytes 786436
  116.6 9.0 %all-to-all-start = ((f32[8,4,16,128]{3,2,1,0:T(8,128)}), f32[8,4,16,128]{3,2,1,0:T(8,128)S(1)}, u32[]{:S(2)}, u32[]{:S(2)}) async-start(f32[8,4,16,128]{3,2,1,0:T(8,128)} %render.2), calls=%async_computation | async-start | bytes 524288 | tf_op jit(solution)/shard_map/all_to_all | solution.py:529
  123.0 12.0 %collective-permute-start.7 = (f32[4,16,128]{2,1,0:T(8,128)}, f32[4,16,128]{2,1,0:T(8,128)S(1)}, u32[]{:S(2)}, u32[]{:S(2)}) collective-permute-start(f32[4,16,128]{2,1,0:T(8,128)} %composite.3), channel_id=1, source_target_pairs={{0,0},{1,1},{2,16},{3,17},{4,32},{5,33},{6,48},{7,49},{8,64},{9,65... | collective-permute-start | bytes 98312 | tf_op jit(solution)/shard_map/ppermute | solution.py:541
  125.6 0.7 copy-start.1
  127.9 9.6 %collective-permute-start.6 = (f32[4,16,128]{2,1,0:T(8,128)}, f32[4,16,128]{2,1,0:T(8,128)S(1)}, u32[]{:S(2)}, u32[]{:S(2)}) collective-permute-start(f32[4,16,128]{2,1,0:T(8,128)} %composite.2), channel_id=1, source_target_pairs={{0,1},{1,0},{2,17},{3,16},{4,33},{5,32},{6,49},{7,48},{8,65},{9,64... | collective-permute-start | bytes 98312 | tf_op jit(solution)/shard_map/ppermute | solution.py:541

commit v2 on v1

--- a/solution.py
+++ b/solution.py
@@ -123,7 +123,9 @@
             ]
             out = collide(f)
             for p in range(Q):
-                r_ref[p, y, 8 * j : 8 * j + 8, :] = pltpu.roll(out[p], low_rows(p), 0)
+                value = pltpu.roll(out[p], low_rows(p), 0)
+                cz = VEL[p][2]
+                r_ref[p, y, 8 * j : 8 * j + 8, :] = value if cz == 0 else pltpu.roll(value, cz % 128, 1)
         return carry
 
     lax.fori_loop(0, width_cells, at_y, 0)
@@ -277,25 +279,7 @@
 
         lax.fori_loop(HALO - reach, HALO + width_cells + reach, at_y, 0)
 
-    def first_step(source, target, reach):
-        def at_y(y, carry):
-            for t in range(wide_tiles):
-                first = PAD + 8 * t
-                f = []
-                for p in range(Q):
-                    cz = VEL[p][2]
-                    value = source[p, y - VEL[p][1], first : first + 8, :]
-                    f.append(value if cz == 0 else pltpu.roll(value, cz % 128, 1))
-                out = collide(f)
-                for p in range(Q):
-                    cx, _, cz = VEL[p]
-                    value = out[p] if cz == 0 else pltpu.roll(out[p], cz % 128, 1)
-                    target[p, y, first + cx : first + cx + 8, :] = value
-            return carry
-
-        lax.fori_loop(HALO - reach, HALO + width_cells + reach, at_y, 0)
-
-    first_step(sa_ref, sb_ref, 4)
+    step(sa_ref, sb_ref, 4, 0)
     step(sb_ref, sa_ref, 3, 0)
     step(sa_ref, sb_ref, 2, 4)
     base = PAD + 8
@@ -370,6 +354,9 @@
     return jnp.concatenate([(2.0 * b)[:, None], strength], axis=1)
 
 
+BLOCK = 4
+
+
 def render_kernel(depth_cells, width_cells, groups, pick_ref, table_ref, backward_ref, vort_ref, image_ref, place_ref, fade_ref):
     bumps = table_ref.shape[1] // 5
 
@@ -378,34 +365,41 @@
         value = vort_ref[at, :].astype(jnp.float32)
         level = value / (value + LEVEL_OFFSET)
         place = STRETCH * level - CENTRE
-        place_ref[x] = place
-        fade_ref[x] = jnp.exp2(-place * place)
+        fade = jnp.exp2(-place * place)
+        for order, to in ((0, x), (1, depth_cells - 1 - x)):
+            place_ref[order, to] = place
+            fade_ref[order, to] = fade
         return carry
 
     lax.fori_loop(0, depth_cells, prepare, 0)
 
     def one(group, carry):
         m = 2 * group + pick_ref[0]
-        backward = backward_ref[m]
-        centre = [table_ref[m, k] for k in range(bumps)]
-        strength = [[table_ref[m, (1 + c) * bumps + k] for k in range(bumps)] for c in range(4)]
-
-        def cell(step, state):
+        order = backward_ref[m]
+
+        def cells(block, state):
             clear, red, green, blue = state
-            x = jnp.where(backward == 1, depth_cells - 1 - step, step)
-            place, fade = place_ref[x], fade_ref[x]
+            at = pl.ds(block * BLOCK, BLOCK)
+            place = place_ref[order, at]
             total = [None] * 4
             for k in range(bumps):
-                bump = jnp.exp2(place * centre[k])
+                bump = jnp.exp2(place * table_ref[m, k])
                 for c in range(4):
-                    term = bump * strength[c][k]
+                    term = bump * table_ref[m, (1 + c) * bumps + k]
                     total[c] = term if total[c] is None else total[c] + term
-            behind = clear * jnp.exp2(-(total[0] * fade))
-            weight = (clear - behind) * fade
-            return (behind, red + weight * total[1], green + weight * total[2], blue + weight * total[3])
+            fade = fade_ref[order, at]
+            passing = jnp.exp2(-(total[0] * fade))
+            for b in range(BLOCK):
+                behind = clear * passing[b]
+                weight = (clear - behind) * fade[b]
+                clear = behind
+                red = red + weight * total[1][b]
+                green = green + weight * total[2][b]
+                blue = blue + weight * total[3][b]
+            return clear, red, green, blue
 
         zero = jnp.zeros((width_cells, 128), jnp.float32)
-        clear, red, green, blue = lax.fori_loop(0, depth_cells, cell, (zero + 1.0, zero, zero, zero))
+        clear, red, green, blue = lax.fori_loop(0, depth_cells // BLOCK, cells, (zero + 1.0, zero, zero, zero))
         image_ref[group, 0] = red
         image_ref[group, 1] = green
         image_ref[group, 2] = blue
@@ -434,6 +428,10 @@
 GRANT = pltpu.CompilerParams(vmem_limit_bytes=58 * 1024 * 1024)
 
 
+def cost(microseconds):
+    return pl.CostEstimate(flops=0, bytes_accessed=int(microseconds * 3.69e6), transcendentals=0)
+
+
 def partner(index, count, phase):
     return index ^ 1 if phase == 0 else (((index + 1) ^ 1) - 1) % count
 
@@ -451,14 +449,6 @@
     d, i = lax.axis_index("depth"), lax.axis_index("image")
     parity = jnp.stack([d % 2, i % 2]).astype(jnp.int32)
     faces = len(face_list(0, 1))
-
-    tables = lax.all_gather(
-        jnp.concatenate([transfer.reshape(1, -1), direction.astype(f32)[:, None]], axis=1),
-        "image", axis=0, tiled=True,
-    )
-    backward = tables[:, -1].astype(jnp.int32)
-    bumps = transfer.shape[2]
-    tables = bump_tables(tables[:, :-1].reshape(-1, 5, bumps), ray_cells).reshape(-1, 5 * bumps)
 
     x_shape = jax.ShapeDtypeStruct((len(X_PAIRS), width_cells // 2, 16, lanes), i16)
     y_shape = jax.ShapeDtypeStruct((faces, depth_cells, lanes), i16)
@@ -472,6 +462,7 @@
         in_specs=[SMEM, VMEM],
         out_specs=(VMEM,) * 5,
         compiler_params=GRANT,
+        cost_estimate=cost(12),
         name="first",
     )(parity, populations.reshape(Q, cells, lanes))
 
@@ -485,10 +476,22 @@
         in_specs=[SMEM, VMEM, VMEM],
         out_specs=(VMEM,) * 3,
         compiler_params=GRANT,
+        cost_estimate=cost(2),
         name="corner",
     )(parity, xa, xb)
-    ca = swap(ca, "image", image_count, 0)
-    cb = swap(cb, "image", image_count, 1)
+    sent_a, sent_b = ca, cb
+    ca = swap(sent_a, "image", image_count, 0)
+    cb = swap(sent_b, "image", image_count, 1)
+
+    bumps = transfer.shape[2]
+    row = jnp.concatenate([transfer.reshape(-1), direction.astype(f32)])
+    row = jnp.pad(row, (0, lanes - row.shape[0]))
+    row, _ = lax.optimization_barrier((row, ia))
+    tables = lax.all_to_all(
+        jnp.broadcast_to(row, (image_count, 8, lanes)), "image", 0, 0, tiled=True
+    )[:, 0]
+    backward = tables[:, 5 * bumps].astype(jnp.int32)
+    tables = bump_tables(tables[:, : 5 * bumps].reshape(-1, 5, bumps), ray_cells).reshape(-1, 5 * bumps)
 
     depth_rows = depth_cells + 8 + 2 * PAD
     width_rows = width_cells + 2 * HALO
@@ -507,6 +510,7 @@
             pltpu.VMEM((cells, lanes), f32),
         ],
         compiler_params=GRANT,
+        cost_estimate=cost(25),
         name="steps",
     )(parity, turned, halo, ya, yb, ca, cb)
 
@@ -520,10 +524,11 @@
             in_specs=[SMEM, SMEM, SMEM, VMEM],
             out_specs=VMEM,
             scratch_shapes=[
-                pltpu.VMEM((depth_cells, width_cells, lanes), f32),
-                pltpu.VMEM((depth_cells, width_cells, lanes), f32),
+                pltpu.VMEM((2, depth_cells, width_cells, lanes), f32),
+                pltpu.VMEM((2, depth_cells, width_cells, lanes), f32),
             ],
             compiler_params=GRANT,
+            cost_estimate=cost(10),
             name="render",
         )(pick, tables, backward, vorticity)
         slabs = lax.all_to_all(partial, "depth", 0, 0, tiled=True)
@@ -532,6 +537,7 @@
             out_shape=jax.ShapeDtypeStruct((4, width_cells, lanes), f32),
             in_specs=[SMEM, SMEM, VMEM],
             out_specs=VMEM,
+            cost_estimate=cost(1),
             name="composite",
         )(2 * d.astype(jnp.int32)[None] + pick, backward, slabs)
         route = []

time: 139 us -> 120 us (0.86)
  blocking collectives: 23.9 us -> 0 us
  starting transfers between devices: 30.9 us -> 38.4 us
  Pallas kernels: 65 us -> 58.6 us
  waiting for transfers between devices: 10.8 us -> 13.3 us
    all_gather x1 -> x0, blocking collectives: 23.9 us -> none  [on_device(): lax.all_gather(jnp.concatenate([transfer.reshape(1, -1), direction.astype...]
    all_to_all x0 -> x1, starting transfers between devices: none -> 7.6 us  [on_device(): lax.all_to_all(jnp.broadcast_to(row, (image_count, 8, lanes)), 'image', 0...]
    pallas_call x2, Pallas kernels: 23.5 us -> 18.2 us  [on_device(): pl.pallas_call(functools.partial(render_kernel, depth_cells, width_cells,...]
    all_to_all x2, starting transfers between devices: 14.5 us -> 9.78 us  [on_device(): slabs = lax.all_to_all(partial, 'depth', 0, 0, tiled=True)]
    ppermute x6, waiting for transfers between devices: 5.27 us -> 9.31 us  [swap(): lax.ppermute(value, axis, [(i, partner(i, count, phase)) for i in range(c...]
    ppermute x6, starting transfers between devices: 9.89 us -> 12.5 us  [swap(): lax.ppermute(value, axis, [(i, partner(i, count, phase)) for i in range(c...]
    pallas_call x1, Pallas kernels: 26.6 us -> 24.4 us  [on_device(): pl.pallas_call(functools.partial(steps_kernel, depth_cells, width_cells),...]
    ppermute x2, starting transfers between devices: 6.55 us -> 8.6 us  [on_device(): pieces.append(lax.ppermute(image, ('depth', 'image'), route))]
  transfers between devices with their start and end apart: 10 -> 11, of which waited for: 5 -> 5; matrix products, arithmetic and copies ran while one was open for 1% -> 1% of each run, Pallas kernels for 13% -> 12%
where the time goes in v2:
time: 120 us; the launch traced here: 119 us
  Pallas kernels  58.6 us (49%)
  starting transfers between devices  38.4 us (32%)
  waiting for transfers between devices  13.3 us (11%)
  local copies, waits for them, and re-layouts  3.99 us (3%)
  other arithmetic  2.82 us (2%)
  between operations  1.4 us (1%)
    pallas_call x1, Pallas kernels, on_device(): pl.pallas_call(functools.partial(steps_kernel, depth_cells, width_cells),...  24.4 us
    pallas_call x2, Pallas kernels, on_device(): pl.pallas_call(functools.partial(render_kernel, depth_cells, width_cells,...  18.2 us
    ppermute x6, starting transfers between devices, swap(): lax.ppermute(value, axis, [(i, partner(i, count, phase)) for i in range(c...  12.5 us
    pallas_call x1, Pallas kernels, on_device(): pl.pallas_call(functools.partial(first_kernel, depth_cells, width_cells),...  10.3 us
    all_to_all x2, starting transfers between devices, on_device(): slabs = lax.all_to_all(partial, 'depth', 0, 0, tiled=True)  9.78 us
    ppermute x6, waiting for transfers between devices, swap(): lax.ppermute(value, axis, [(i, partner(i, count, phase)) for i in range(c...  9.31 us
    ppermute x2, starting transfers between devices, on_device(): pieces.append(lax.ppermute(image, ('depth', 'image'), route))  8.6 us
    all_to_all x1, starting transfers between devices, on_device(): lax.all_to_all(jnp.broadcast_to(row, (image_count, 8, lanes)), 'image', 0...  7.6 us
  transfers between devices with their start and end apart: 11, of which 5 were waited for; matrix products, arithmetic and copies ran while one was open for 1% of the time, Pallas kernels for 12%

profile of v2, /device:TPU:17, one launch (start us, length us, event | category | flops | bytes accessed | tf_op | source)
XLA Modules:
  0.0 118.6 jit_solution(14579702347345053620)
XLA Ops:
  1.3 0.7 reduce.2
  2.8 10.3 %first.1 = (f32[19,16,32,128]{3,2,1,0:T(8,128)}, s16[10,8,16,128]{3,2,1,0:T(8,128)(2,1)}, s16[10,8,16,128]{3,2,1,0:T(8,128)(2,1)}, s16[76,32,128]{2,1,0:T(8,128)(2,1)}, s16[76,32,128]{2,1,0:T(8,128)(2,1)}) custom-call(s32[2]{0:T(128)} %pad_add_fusion.parity_ref, f32[19,512,128]{2,1,0:T(8,128)} %bitcast.16), custom_call_target="tpu_custom_call" | custom-call | bytes 44280000 | tf_op jit(solution)/shard_map/first/pallas_call | solution.py:456
  13.8 7.6 %all-to-all-start = ((f32[16,8,128]{2,1,0:T(8,128)}), f32[16,8,128]{2,1,0:T(8,128)S(1)}, u32[]{:S(2)}, u32[]{:S(2)}) async-start(f32[16,8,128]{2,1,0:T(8,128)} %broadcast_in_dim.7), calls=%async_computation | async-start | bytes 131072 | tf_op jit(solution)/shard_map/all_to_all | solution.py:490
  21.4 1.4 %collective-permute-start.2 = (s16[76,32,128]{2,1,0:T(8,128)(2,1)}, s16[76,32,128]{2,1,0:T(8,128)(2,1)S(1)}, u32[]{:S(2)}, u32[]{:S(2)}) collective-permute-start(s16[76,32,128]{2,1,0:T(8,128)(2,1)} %get-tuple-element.30), channel_id=1, source_target_pairs={{0,1},{1,0},{2,3},{3,2},{4,5},{5,4},{6,7},{7,6},{8,9},{9,8},{10,11... | collective-permute-start | bytes 1867784 | tf_op jit(solution)/shard_map/ppermute | solution.py:440
  22.7 1.5 %collective-permute-start = (s16[10,8,16,128]{3,2,1,0:T(8,128)(2,1)}, s16[10,8,16,128]{3,2,1,0:T(8,128)(2,1)S(1)}, u32[]{:S(2)}, u32[]{:S(2)}) collective-permute-start(s16[10,8,16,128]{3,2,1,0:T(8,128)(2,1)} %get-tuple-element.27), channel_id=1, source_target_pairs={{0,16},{16,0},{32,48},{48,32},{64,80},{80,64},{96,112},{112,96},{1... | collective-permute-start | bytes 983048 | tf_op jit(solution)/shard_map/ppermute | solution.py:440
  24.2 0.9 collective-permute-start.1
  25.1 3.9 %collective-permute-start.3 = (s16[76,32,128]{2,1,0:T(8,128)(2,1)}, s16[76,32,128]{2,1,0:T(8,128)(2,1)S(1)}, u32[]{:S(2)}, u32[]{:S(2)}) collective-permute-start(s16[76,32,128]{2,1,0:T(8,128)(2,1)} %get-tuple-element.31), channel_id=1, source_target_pairs={{0,15},{1,2},{2,1},{3,4},{4,3},{5,6},{6,5},{7,8},{8,7},{9,10},{10,... | collective-permute-start | bytes 1867784 | tf_op jit(solution)/shard_map/ppermute | solution.py:440
  29.2 2.1 %collective-permute-done.1.xb_ref = s16[10,8,16,128]{3,2,1,0:T(8,128)(2,1)S(1)} collective-permute-done((s16[10,8,16,128]{3,2,1,0:T(8,128)(2,1)}, s16[10,8,16,128]{3,2,1,0:T(8,128)(2,1)S(1)}, u32[]{:S(2)}, u32[]{:S(2)}) %collective-permute-start.1) | collective-permute-done | bytes 327712 | tf_op jit(solution)/shard_map/ppermute | solution.py:440
  31.3 0.7 copy-done.5
  32.0 2.5 %corner.1 = (f32[19,16,8,128]{3,2,1,0:T(8,128)}, s16[38,16,128]{2,1,0:T(8,128)(2,1)}, s16[38,16,128]{2,1,0:T(8,128)(2,1)}) custom-call(s32[2]{0:T(128)} %pad_add_fusion.parity_ref, s16[10,8,16,128]{3,2,1,0:T(8,128)(2,1)} %copy-done.4, s16[10,8,16,128]{3,2,1,0:T(8,128)(2,1)} %copy-done.5), custom_call_target="tpu_custom_call" | custom-call | bytes 7380000 | tf_op jit(solution)/shard_map/corner/pallas_call | solution.py:473
  34.5 4.8 %collective-permute-start.5 = (s16[38,16,128]{2,1,0:T(8,128)(2,1)}, s16[38,16,128]{2,1,0:T(8,128)(2,1)S(1)}, u32[]{:S(2)}, u32[]{:S(2)}) collective-permute-start(s16[38,16,128]{2,1,0:T(8,128)(2,1)} %get-tuple-element.33), channel_id=1, source_target_pairs={{0,15},{1,2},{2,1},{3,4},{4,3},{5,6},{6,5},{7,8},{8,7},{9,10},{10,... | collective-permute-start | bytes 466952 | tf_op jit(solution)/shard_map/ppermute | solution.py:440
  40.0 0.7 fusion.backward_ref
  40.8 7.1 %collective-permute-done.5.cb_ref = s16[38,16,128]{2,1,0:T(8,128)(2,1)S(1)} collective-permute-done((s16[38,16,128]{2,1,0:T(8,128)(2,1)}, s16[38,16,128]{2,1,0:T(8,128)(2,1)S(1)}, u32[]{:S(2)}, u32[]{:S(2)}) %collective-permute-start.5) | collective-permute-done | bytes 155680 | tf_op jit(solution)/shard_map/ppermute | solution.py:440
  49.0 24.4 %steps.1 = (f32[19,512,128]{2,1,0:T(8,128)}, bf16[512,128]{1,0:T(8,128)(2,1)}) custom-call(s32[2]{0:T(128)} %pad_add_fusion.parity_ref, f32[19,16,32,128]{3,2,1,0:T(8,128)} %get-tuple-element.26.r_ref, f32[19,16,8,128]{3,2,1,0:T(8,128)} %get-tuple-element.29.h_ref, s16[76,32,128]{2,1,0:T(8,128)(2,1)} %copy-done.2, s16[76,32,128]{2,1,0:T(8,128)(2,1)} %copy-done.3, ...), custom_call_target="tpu_custom_call" | custom-call | bytes 92250000 | tf_op jit(solution)/shard_map/steps/pallas_call | solution.py:498
  73.4 9.1 %render.3 = f32[8,4,16,128]{3,2,1,0:T(8,128)} custom-call(s32[1]{0:T(128)} %bitcast.1.pick_ref, f32[16,40]{1,0:T(8,128)} %copy.13.table_ref, s32[16]{0:T(128)} %fusion.backward_ref, bf16[512,128]{1,0:T(8,128)(2,1)} %get-tuple-element.35.vort_ref), custom_call_target="tpu_custom_call" | custom-call | bytes 36900000 | tf_op jit(solution)/shard_map/render/pallas_call | solution.py:521
  82.5 5.0 %all-to-all-start.2 = ((f32[8,4,16,128]{3,2,1,0:T(8,128)}), f32[8,4,16,128]{3,2,1,0:T(8,128)S(1)}, u32[]{:S(2)}, u32[]{:S(2)}) async-start(f32[8,4,16,128]{3,2,1,0:T(8,128)} %render.3), calls=%async_computation.2 | async-start | bytes 524288 | tf_op jit(solution)/shard_map/all_to_all | solution.py:534
  87.5 9.1 %render.2 = f32[8,4,16,128]{3,2,1,0:T(8,128)} custom-call(s32[1]{0:T(128)} %bitcast.6.pick_ref, f32[16,40]{1,0:T(8,128)} %copy.13.table_ref, s32[16]{0:T(128)} %fusion.backward_ref, bf16[512,128]{1,0:T(8,128)(2,1)} %get-tuple-element.35.vort_ref), custom_call_target="tpu_custom_call" | custom-call | bytes 36900000 | tf_op jit(solution)/shard_map/render/pallas_call | solution.py:521
  96.6 4.8 %all-to-all-start.1 = ((f32[8,4,16,128]{3,2,1,0:T(8,128)}), f32[8,4,16,128]{3,2,1,0:T(8,128)S(1)}, u32[]{:S(2)}, u32[]{:S(2)}) async-start(f32[8,4,16,128]{3,2,1,0:T(8,128)} %render.2), calls=%async_computation.1 | async-start | bytes 524288 | tf_op jit(solution)/shard_map/all_to_all | solution.py:534
  101.4 1.6 %composite.3 = f32[4,16,128]{2,1,0:T(8,128)} custom-call(s32[1]{0:T(128)S(6)} %add.33.pick_ref, s32[16]{0:T(128)} %fusion.backward_ref, f32[8,4,16,128]{3,2,1,0:T(8,128)} %copy-done), custom_call_target="tpu_custom_call" | custom-call | bytes 3690000 | tf_op jit(solution)/shard_map/composite/pallas_call | solution.py:535
  103.0 3.1 %collective-permute-start.7 = (f32[4,16,128]{2,1,0:T(8,128)}, f32[4,16,128]{2,1,0:T(8,128)S(1)}, u32[]{:S(2)}, u32[]{:S(2)}) collective-permute-start(f32[4,16,128]{2,1,0:T(8,128)} %composite.3), channel_id=1, source_target_pairs={{0,0},{1,1},{2,16},{3,17},{4,32},{5,33},{6,48},{7,49},{8,64},{9,65... | collective-permute-start | bytes 98312 | tf_op jit(solution)/shard_map/ppermute | solution.py:547
  106.8 1.6 %composite.2 = f32[4,16,128]{2,1,0:T(8,128)} custom-call(s32[1]{0:T(128)S(6)} %add.32.pick_ref, s32[16]{0:T(128)} %fusion.backward_ref, f32[8,4,16,128]{3,2,1,0:T(8,128)} %copy-done.1), custom_call_target="tpu_custom_call" | custom-call | bytes 3690000 | tf_op jit(solution)/shard_map/composite/pallas_call | solution.py:535
  108.4 5.5 %collective-permute-start.6 = (f32[4,16,128]{2,1,0:T(8,128)}, f32[4,16,128]{2,1,0:T(8,128)S(1)}, u32[]{:S(2)}, u32[]{:S(2)}) collective-permute-start(f32[4,16,128]{2,1,0:T(8,128)} %composite.2), channel_id=1, source_target_pairs={{0,1},{1,0},{2,17},{3,16},{4,33},{5,32},{6,49},{7,48},{8,65},{9,64... | collective-permute-start | bytes 98312 | tf_op jit(solution)/shard_map/ppermute | solution.py:547
  113.9 1.0 collective-permute-done.7
  114.9 3.0 %collective-permute-done.6 = f32[4,16,128]{2,1,0:T(8,128)S(1)} collective-permute-done((f32[4,16,128]{2,1,0:T(8,128)}, f32[4,16,128]{2,1,0:T(8,128)S(1)}, u32[]{:S(2)}, u32[]{:S(2)}) %collective-permute-start.6) | collective-permute-done | bytes 32800 | tf_op jit(solution)/shard_map/ppermute | solution.py:547
  (36 shorter events, 4.8 us)
Async XLA Ops:
  13.8 15.3 %all-to-all-start = ((f32[16,8,128]{2,1,0:T(8,128)}), f32[16,8,128]{2,1,0:T(8,128)S(1)}, u32[]{:S(2)}, u32[]{:S(2)}) async-start(f32[16,8,128]{2,1,0:T(8,128)} %broadcast_in_dim.7), calls=%async_computation | async-start | bytes 131072 | tf_op jit(solution)/shard_map/all_to_all | solution.py:490
  21.4 26.6 %collective-permute-start.2 = (s16[76,32,128]{2,1,0:T(8,128)(2,1)}, s16[76,32,128]{2,1,0:T(8,128)(2,1)S(1)}, u32[]{:S(2)}, u32[]{:S(2)}) collective-permute-start(s16[76,32,128]{2,1,0:T(8,128)(2,1)} %get-tuple-element.30), channel_id=1, source_target_pairs={{0,1},{1,0},{2,3},{3,2},{4,5},{5,4},{6,7},{7,6},{8,9},{9,8},{10,11... | collective-permute-start | bytes 1867784 | tf_op jit(solution)/shard_map/ppermute | solution.py:440
  22.7 6.4 %collective-permute-start = (s16[10,8,16,128]{3,2,1,0:T(8,128)(2,1)}, s16[10,8,16,128]{3,2,1,0:T(8,128)(2,1)S(1)}, u32[]{:S(2)}, u32[]{:S(2)}) collective-permute-start(s16[10,8,16,128]{3,2,1,0:T(8,128)(2,1)} %get-tuple-element.27), channel_id=1, source_target_pairs={{0,16},{16,0},{32,48},{48,32},{64,80},{80,64},{96,112},{112,96},{1... | collective-permute-start | bytes 983048 | tf_op jit(solution)/shard_map/ppermute | solution.py:440
  24.2 7.0 %collective-permute-start.1 = (s16[10,8,16,128]{3,2,1,0:T(8,128)(2,1)}, s16[10,8,16,128]{3,2,1,0:T(8,128)(2,1)S(1)}, u32[]{:S(2)}, u32[]{:S(2)}) collective-permute-start(s16[10,8,16,128]{3,2,1,0:T(8,128)(2,1)} %get-tuple-element.28), channel_id=1, source_target_pairs={{0,112},{16,32},{32,16},{48,64},{64,48},{80,96},{96,80},{112,0},{1... | collective-permute-start | bytes 983048 | tf_op jit(solution)/shard_map/ppermute | solution.py:440
  25.1 22.8 %collective-permute-start.3 = (s16[76,32,128]{2,1,0:T(8,128)(2,1)}, s16[76,32,128]{2,1,0:T(8,128)(2,1)S(1)}, u32[]{:S(2)}, u32[]{:S(2)}) collective-permute-start(s16[76,32,128]{2,1,0:T(8,128)(2,1)} %get-tuple-element.31), channel_id=1, source_target_pairs={{0,15},{1,2},{2,1},{3,4},{4,3},{5,6},{6,5},{7,8},{8,7},{9,10},{10,... | collective-permute-start | bytes 1867784 | tf_op jit(solution)/shard_map/ppermute | solution.py:440
  29.2 2.1 %copy-start.4 = (s16[10,8,16,128]{3,2,1,0:T(8,128)(2,1)}, s16[10,8,16,128]{3,2,1,0:T(8,128)(2,1)S(1)}, u32[]{:S(2)}) copy-start(s16[10,8,16,128]{3,2,1,0:T(8,128)(2,1)S(1)} %collective-permute-done.xa_ref) | copy-start | bytes 983044
  31.3 0.7 copy-start.5
  34.5 6.3 %collective-permute-start.4 = (s16[38,16,128]{2,1,0:T(8,128)(2,1)}, s16[38,16,128]{2,1,0:T(8,128)(2,1)S(1)}, u32[]{:S(2)}, u32[]{:S(2)}) collective-permute-start(s16[38,16,128]{2,1,0:T(8,128)(2,1)} %get-tuple-element.32), channel_id=1, source_target_pairs={{0,1},{1,0},{2,3},{3,2},{4,5},{5,4},{6,7},{7,6},{8,9},{9,8},{10,11... | collective-permute-start | bytes 466952 | tf_op jit(solution)/shard_map/ppermute | solution.py:440
  34.5 13.4 %collective-permute-start.5 = (s16[38,16,128]{2,1,0:T(8,128)(2,1)}, s16[38,16,128]{2,1,0:T(8,128)(2,1)S(1)}, u32[]{:S(2)}, u32[]{:S(2)}) collective-permute-start(s16[38,16,128]{2,1,0:T(8,128)(2,1)} %get-tuple-element.33), channel_id=1, source_target_pairs={{0,15},{1,2},{2,1},{3,4},{4,3},{5,6},{6,5},{7,8},{8,7},{9,10},{10,... | collective-permute-start | bytes 466952 | tf_op jit(solution)/shard_map/ppermute | solution.py:440
  40.8 7.1 %copy-start.6 = (s16[38,16,128]{2,1,0:T(8,128)(2,1)}, s16[38,16,128]{2,1,0:T(8,128)(2,1)S(1)}, u32[]{:S(2)}) copy-start(s16[38,16,128]{2,1,0:T(8,128)(2,1)S(1)} %collective-permute-done.4.ca_ref) | copy-start | bytes 466948
  47.9 0.7 copy-start.7
  47.9 0.9 copy-start.3
  47.9 1.1 copy-start.2
  82.5 14.1 %all-to-all-start.2 = ((f32[8,4,16,128]{3,2,1,0:T(8,128)}), f32[8,4,16,128]{3,2,1,0:T(8,128)S(1)}, u32[]{:S(2)}, u32[]{:S(2)}) async-start(f32[8,4,16,128]{3,2,1,0:T(8,128)} %render.3), calls=%async_computation.2 | async-start | bytes 524288 | tf_op jit(solution)/shard_map/all_to_all | solution.py:534
  96.6 4.8 %copy-start = (f32[8,4,16,128]{3,2,1,0:T(8,128)}, f32[8,4,16,128]{3,2,1,0:T(8,128)S(1)}, u32[]{:S(2)}) copy-start(f32[8,4,16,128]{3,2,1,0:T(8,128)S(1)} %all-to-all-done.2.piece_ref) | copy-start | bytes 786436
  96.6 9.5 %all-to-all-start.1 = ((f32[8,4,16,128]{3,2,1,0:T(8,128)}), f32[8,4,16,128]{3,2,1,0:T(8,128)S(1)}, u32[]{:S(2)}, u32[]{:S(2)}) async-start(f32[8,4,16,128]{3,2,1,0:T(8,128)} %render.2), calls=%async_computation.1 | async-start | bytes 524288 | tf_op jit(solution)/shard_map/all_to_all | solution.py:534
  103.0 11.9 %collective-permute-start.7 = (f32[4,16,128]{2,1,0:T(8,128)}, f32[4,16,128]{2,1,0:T(8,128)S(1)}, u32[]{:S(2)}, u32[]{:S(2)}) collective-permute-start(f32[4,16,128]{2,1,0:T(8,128)} %composite.3), channel_id=1, source_target_pairs={{0,0},{1,1},{2,16},{3,17},{4,32},{5,33},{6,48},{7,49},{8,64},{9,65... | collective-permute-start | bytes 98312 | tf_op jit(solution)/shard_map/ppermute | solution.py:547
  106.1 0.7 copy-start.1
  108.4 9.6 %collective-permute-start.6 = (f32[4,16,128]{2,1,0:T(8,128)}, f32[4,16,128]{2,1,0:T(8,128)S(1)}, u32[]{:S(2)}, u32[]{:S(2)}) collective-permute-start(f32[4,16,128]{2,1,0:T(8,128)} %composite.2), channel_id=1, source_target_pairs={{0,1},{1,0},{2,17},{3,16},{4,33},{5,32},{6,49},{7,48},{8,65},{9,64... | collective-permute-start | bytes 98312 | tf_op jit(solution)/shard_map/ppermute | solution.py:547

commit v3 on v2

--- a/solution.py
+++ b/solution.py
@@ -111,24 +111,37 @@
     return value.astype(jnp.int32).astype(jnp.float32)
 
 
-def first_kernel(depth_cells, width_cells, parity_ref, f_ref, r_ref, da_ref, db_ref, ia_ref, ib_ref):
+def first_kernel(
+    depth_cells, width_cells, parity_ref, f_hbm, r_hbm, da_ref, db_ref, ia_ref, ib_ref, f_ref, r_ref, in_sems, out_sem
+):
     tiles = depth_cells // 8
     rows = row_index()
-
-    def at_y(y, carry):
-        for j in range(tiles):
-            f = [
-                f_ref[p, pl.ds(j * 8 * width_cells + y, 8, stride=width_cells), :]
-                for p in range(Q)
-            ]
+    chunk = 8 * width_cells
+    loads = [
+        pltpu.make_async_copy(
+            f_hbm.at[:, pl.ds(j * chunk, chunk)], f_ref.at[:, pl.ds(j * chunk, chunk)], in_sems.at[j]
+        )
+        for j in range(tiles)
+    ]
+    for load in loads:
+        load.start()
+
+    for j in range(tiles):
+        loads[j].wait()
+
+        def at_y(y, carry):
+            f = [f_ref[p, pl.ds(j * chunk + y, 8, stride=width_cells), :] for p in range(Q)]
             out = collide(f)
             for p in range(Q):
                 value = pltpu.roll(out[p], low_rows(p), 0)
                 cz = VEL[p][2]
                 r_ref[p, y, 8 * j : 8 * j + 8, :] = value if cz == 0 else pltpu.roll(value, cz % 128, 1)
-        return carry
-
-    lax.fori_loop(0, width_cells, at_y, 0)
+            return carry
+
+        lax.fori_loop(0, width_cells, at_y, 0, unroll=2)
+
+    keep_r = pltpu.make_async_copy(r_ref, r_hbm, out_sem)
+    keep_r.start()
 
     odd_depth = jnp.full((8, 128), parity_ref[0], jnp.int32) == 1
     odd_image = jnp.full((8, 128), parity_ref[1], jnp.int32) == 1
@@ -167,6 +180,7 @@
                 b.append(jnp.where(odd_image, high, low))
             ia_ref[index, 16 * c : 16 * c + 16, :] = pack16(*a)
             ib_ref[index, 16 * c : 16 * c + 16, :] = pack16(*b)
+    keep_r.wait()
 
 
 def x_halo(low, high, n, second, rows):
@@ -218,30 +232,120 @@
 PAD = 8
 
 
-def steps_kernel(
-    depth_cells, width_cells, parity_ref, r_ref, h_ref, ya_ref, yb_ref, ca_ref, cb_ref,
-    out_ref, vort_ref, sa_ref, sb_ref, flow_ref, plain_ref,
+def put_streamed(target, p, y, pieces, halo, rows):
+    n = low_rows(p)
+    before = halo
+    for t in range(len(pieces) + 1):
+        here = pieces[t] if t < len(pieces) else halo
+        target[p, y, PAD + 8 * t : PAD + 8 * t + 8, :] = jnp.where(rows < n, before, here)
+        before = here
+
+
+def step_row(source, target, y, wide_tiles, shift):
+    for t in range(wide_tiles):
+        first = PAD + 8 * t
+        out = collide([source[p, y - VEL[p][1], first : first + 8, :] for p in range(Q)])
+        for p in range(Q):
+            cx, _, cz = VEL[p]
+            value = out[p] if cz == 0 else pltpu.roll(out[p], cz % 128, 1)
+            row = first + shift + cx
+            target[p, y, row : row + 8, :] = value
+
+
+BASE = PAD + 8
+
+
+def flow_row(source, flow_ref, y, tiles):
+    for t in range(-1, tiles + 1):
+        first = BASE + 8 * t
+        density, j, _, _ = momentum([source[p, y - VEL[p][1], first : first + 8, :] for p in range(Q)])
+        inverse = 1.0 / density
+        for axis in range(3):
+            flow_ref[axis, y, first : first + 8, :] = j[axis] * inverse
+
+
+def final_row(source, out_ref, y, origin, tiles, width_cells):
+    for t in range(tiles):
+        first = BASE + 8 * t
+        for p in range(Q):
+            out_ref[p, pl.ds(8 * t * width_cells + y - origin, 8, stride=width_cells), :] = source[
+                p, y - VEL[p][1], first : first + 8, :
+            ]
+
+
+def inner_kernel(
+    depth_cells, width_cells, r_ref, h_ref, final_ref, flow_ref, s2_hbm, s3_hbm, s4_hbm, sa_ref, sb_ref, sems
 ):
     tiles = depth_cells // 8
-    wide_tiles = tiles + 1
     rows = row_index()
-    odd_image = jnp.full((8, 128), parity_ref[1], jnp.int32) == 1
-
-    def streamed(p, y, pieces, halo):
-        n = low_rows(p)
-        before = halo
-        for t in range(wide_tiles):
-            here = pieces[t] if t < tiles else halo
-            sa_ref[p, y, PAD + 8 * t : PAD + 8 * t + 8, :] = jnp.where(rows < n, before, here)
-            before = here
 
     def own(y, carry):
         for p in range(Q):
             pieces = [r_ref[p, y, 8 * t : 8 * t + 8, :] for t in range(tiles)]
-            streamed(p, y + HALO, pieces, decode(h_ref[p, y], p))
+            put_streamed(sa_ref, p, y, pieces, decode(h_ref[p, y], p), rows)
         return carry
 
     lax.fori_loop(0, width_cells, own, 0)
+
+    def hand_on(source, target, step):
+        low, high = (step, width_cells - 2 - step)
+        copies = [
+            pltpu.make_async_copy(source.at[:, pl.ds(low, 2)], target.at[:, pl.ds(0, 2)], sems.at[step - 1, 0]),
+            pltpu.make_async_copy(source.at[:, pl.ds(high, 2)], target.at[:, pl.ds(2, 2)], sems.at[step - 1, 1]),
+        ]
+        for copy in copies:
+            copy.start()
+        return copies
+
+    def stage(source, target, step, shift):
+        def pair(k, carry):
+            step_row(source, target, step + 2 * k, tiles + 1, shift)
+            step_row(source, target, step + 2 * k + 1, tiles + 1, shift)
+            return carry
+
+        lax.fori_loop(0, (width_cells - 2 * step) // 2, pair, 0)
+
+    stage(sa_ref, sb_ref, 1, 0)
+    kept2 = hand_on(sb_ref, s2_hbm, 1)
+    stage(sb_ref, sa_ref, 2, 0)
+    kept3 = hand_on(sa_ref, s3_hbm, 2)
+    for copy in kept2:
+        copy.wait()
+    stage(sa_ref, sb_ref, 3, 4)
+    kept4 = hand_on(sb_ref, s4_hbm, 3)
+
+    def last(y, carry):
+        flow_row(sb_ref, flow_ref, y, tiles)
+        final_row(sb_ref, final_ref, y, 0, tiles, width_cells)
+        return carry
+
+    lax.fori_loop(STEPS, width_cells - STEPS, last, 0)
+    for copy in kept3 + kept4:
+        copy.wait()
+
+
+def outer_kernel(
+    depth_cells, width_cells, parity_ref, r_hbm, h_ref, ya_ref, yb_ref, ca_ref, cb_ref,
+    final_in, flow_in, s2_in, s3_in, s4_in, out_hbm, vort_ref,
+    r_ref, sa_ref, sb_ref, flow_ref, out_ref, plain_ref, sems,
+):
+    tiles = depth_cells // 8
+    rows = row_index()
+    odd_image = jnp.full((8, 128), parity_ref[1], jnp.int32) == 1
+
+    moves = [
+        (r_hbm.at[:, pl.ds(0, 2)], r_ref.at[:, pl.ds(0, 2)]),
+        (r_hbm.at[:, pl.ds(width_cells - 2, 2)], r_ref.at[:, pl.ds(2, 2)]),
+    ]
+    for step, source, target in ((1, s2_in, sb_ref), (2, s3_in, sa_ref), (3, s4_in, sb_ref)):
+        moves.append((source.at[:, pl.ds(0, 2)], target.at[:, pl.ds(HALO + step, 2)]))
+        moves.append((source.at[:, pl.ds(2, 2)], target.at[:, pl.ds(HALO + width_cells - 2 - step, 2)]))
+    inner = pl.ds(STEPS, width_cells - 2 * STEPS)
+    moves.append((flow_in.at[:, inner], flow_ref.at[:, pl.ds(HALO + STEPS, width_cells - 2 * STEPS)]))
+    moves.append((final_in, out_ref))
+    copies = [pltpu.make_async_copy(a, b, sems.at[k]) for k, (a, b) in enumerate(moves)]
+    for copy in copies:
+        copy.start()
 
     low_face = face_list(0, 1)
     high_face = face_list(width_cells - 1, -1)
@@ -261,55 +365,57 @@
                     high.append(jnp.where(odd_image, b, a))
             low = [decode(v, ph) for v in low]
             high = [decode(v, pl_) for v in high]
-            streamed(ph, yh - width_cells + HALO, low[1:], low[0])
-            streamed(pl_, yl + width_cells + HALO, high[1:], high[0])
-
-    def step(source, target, reach, shift):
-        def at_y(y, carry):
-            for t in range(wide_tiles):
-                first = PAD + 8 * t
-                f = [source[p, y - VEL[p][1], first : first + 8, :] for p in range(Q)]
-                out = collide(f)
-                for p in range(Q):
-                    cx, _, cz = VEL[p]
-                    value = out[p] if cz == 0 else pltpu.roll(out[p], cz % 128, 1)
-                    row = first + shift + cx
-                    target[p, y, row : row + 8, :] = value
+            put_streamed(sa_ref, ph, yh - width_cells + HALO, low[1:], low[0], rows)
+            put_streamed(sa_ref, pl_, yl + width_cells + HALO, high[1:], high[0], rows)
+
+    copies[0].wait()
+    copies[1].wait()
+    for k, y in enumerate((0, 1, width_cells - 2, width_cells - 1)):
+        for p in range(Q):
+            pieces = [r_ref[p, k, 8 * t : 8 * t + 8, :] for t in range(tiles)]
+            put_streamed(sa_ref, p, y + HALO, pieces, decode(h_ref[p, y], p), rows)
+
+    def stage(source, target, step, shift):
+        reach = HALO - step
+
+        def both(k, carry):
+            step_row(source, target, HALO - reach + k, tiles + 1, shift)
+            step_row(source, target, HALO + width_cells - step + k, tiles + 1, shift)
             return carry
 
-        lax.fori_loop(HALO - reach, HALO + width_cells + reach, at_y, 0)
-
-    step(sa_ref, sb_ref, 4, 0)
-    step(sb_ref, sa_ref, 3, 0)
-    step(sa_ref, sb_ref, 2, 4)
-    base = PAD + 8
-
-    def flow_at(y, carry):
-        for t in range(-1, tiles + 1):
-            first = base + 8 * t
-            f = [sb_ref[p, y - VEL[p][1], first : first + 8, :] for p in range(Q)]
-            density, j, _, _ = momentum(f)
-            inverse = 1.0 / density
-            for axis in range(3):
-                flow_ref[axis, y, first : first + 8, :] = j[axis] * inverse
-        return carry
-
-    lax.fori_loop(HALO - 1, HALO + width_cells + 1, flow_at, 0)
-
-    def final_at(y, carry):
-        for t in range(tiles):
-            first = base + 8 * t
-            for p in range(Q):
-                out_ref[p, pl.ds(8 * t * width_cells + y - HALO, 8, stride=width_cells), :] = sb_ref[
-                    p, y - VEL[p][1], first : first + 8, :
-                ]
-        return carry
-
-    lax.fori_loop(HALO, HALO + width_cells, final_at, 0)
+        lax.fori_loop(0, HALO, both, 0)
+
+    stage(sa_ref, sb_ref, 1, 0)
+    copies[2].wait()
+    copies[3].wait()
+    stage(sb_ref, sa_ref, 2, 0)
+    copies[4].wait()
+    copies[5].wait()
+    stage(sa_ref, sb_ref, 3, 4)
+    copies[6].wait()
+    copies[7].wait()
+    copies[9].wait()
+
+    def finish(k, carry):
+        final_row(sb_ref, out_ref, HALO + k, HALO, tiles, width_cells)
+        final_row(sb_ref, out_ref, HALO + width_cells - STEPS + k, HALO, tiles, width_cells)
+        return carry
+
+    lax.fori_loop(0, STEPS, finish, 0)
+    keep_out = pltpu.make_async_copy(out_ref, out_hbm, sems.at[10])
+    keep_out.start()
+
+    def flows(k, carry):
+        flow_row(sb_ref, flow_ref, HALO - 1 + k, tiles)
+        flow_row(sb_ref, flow_ref, HALO + width_cells - STEPS + k, tiles)
+        return carry
+
+    lax.fori_loop(0, HALO, flows, 0)
+    copies[8].wait()
 
     def spin_at(y, carry):
         for t in range(tiles):
-            first = base + 8 * t
+            first = BASE + 8 * t
 
             def dx(axis):
                 return (flow_ref[axis, y, first + 1 : first + 9, :] - flow_ref[axis, y, first - 1 : first + 7, :]) * 0.5
@@ -329,14 +435,15 @@
             )
         return carry
 
-    lax.fori_loop(HALO, HALO + width_cells, spin_at, 0)
+    lax.fori_loop(HALO, HALO + width_cells, spin_at, 0, unroll=2)
 
     def rounded(x, carry):
         at = pl.ds(pl.multiple_of(x * 16, 16), 16)
         vort_ref[at, :] = plain_ref[at, :].astype(jnp.bfloat16)
         return carry
 
-    lax.fori_loop(0, depth_cells * width_cells // 16, rounded, 0)
+    lax.fori_loop(0, depth_cells * width_cells // 16, rounded, 0, unroll=4)
+    keep_out.wait()
 
 
 BUMP_WIDTH = 0.15
@@ -373,8 +480,10 @@
 
     lax.fori_loop(0, depth_cells, prepare, 0)
 
-    def one(group, carry):
-        m = 2 * group + pick_ref[0]
+    def one(number, carry):
+        group = number // 2
+        slot = number % 2
+        m = 2 * group + (pick_ref[0] + slot) % 2
         order = backward_ref[m]
 
         def cells(block, state):
@@ -400,29 +509,36 @@
 
         zero = jnp.zeros((width_cells, 128), jnp.float32)
         clear, red, green, blue = lax.fori_loop(0, depth_cells // BLOCK, cells, (zero + 1.0, zero, zero, zero))
-        image_ref[group, 0] = red
-        image_ref[group, 1] = green
-        image_ref[group, 2] = blue
-        image_ref[group, 3] = clear
-        return carry
-
-    lax.fori_loop(0, groups, one, 0)
-
-
-def composite_kernel(slabs, pick_ref, backward_ref, piece_ref, image_ref):
-    backward = backward_ref[pick_ref[0]]
-    shape = piece_ref.shape[2:]
-    clear = jnp.ones(shape, jnp.float32)
-    color = [jnp.zeros(shape, jnp.float32) for c in range(3)]
-    for step in range(slabs):
-        s = jnp.where(backward == 1, slabs - 1 - step, step)
-        color = [color[c] + clear * piece_ref[s, c] for c in range(3)]
-        clear = clear * piece_ref[s, 3]
-    for c in range(3):
-        image_ref[c] = color[c]
-    image_ref[3] = 1.0 - clear
-
-
+        image_ref[group, slot, 0] = red
+        image_ref[group, slot, 1] = green
+        image_ref[group, slot, 2] = blue
+        image_ref[group, slot, 3] = clear
+        return carry
+
+    lax.fori_loop(0, 2 * groups, one, 0)
+
+
+def composite(slabs, backward):
+    chooser = backward[:, :, None] == 1
+    count = slabs.shape[0]
+    clear = 1.0
+    color = [0.0] * 3
+    for step in range(count):
+        piece = [jnp.where(chooser, slabs[count - 1 - step, :, c], slabs[step, :, c]) for c in range(4)]
+        color = [color[c] + clear * piece[c] for c in range(3)]
+        clear = clear * piece[3]
+    return jnp.stack(color + [1.0 - clear], axis=1)
+
+
+GATHER_ROWS = 128
+
+
+def first_rows_kernel(in_ref, out_ref):
+    for m in range(out_ref.shape[0]):
+        out_ref[m : m + 1, :] = in_ref[m * GATHER_ROWS : m * GATHER_ROWS + 1, :]
+
+
+ANY = pl.BlockSpec(memory_space=pl.ANY)
 VMEM = pl.BlockSpec(memory_space=pltpu.VMEM)
 SMEM = pl.BlockSpec(memory_space=pltpu.SMEM)
 GRANT = pltpu.CompilerParams(vmem_limit_bytes=58 * 1024 * 1024)
@@ -450,6 +566,11 @@
     parity = jnp.stack([d % 2, i % 2]).astype(jnp.int32)
     faces = len(face_list(0, 1))
 
+    bumps = transfer.shape[2]
+    row = jnp.concatenate([transfer.reshape(-1), direction.astype(f32)])
+    row = jnp.pad(row[None], ((0, GATHER_ROWS - 1), (0, lanes - row.shape[0])))
+    gathered = lax.all_gather(row, "image", axis=0, tiled=True)
+
     x_shape = jax.ShapeDtypeStruct((len(X_PAIRS), width_cells // 2, 16, lanes), i16)
     y_shape = jax.ShapeDtypeStruct((faces, depth_cells, lanes), i16)
     c_shape = jax.ShapeDtypeStruct((faces // 2, 16, lanes), i16)
@@ -459,8 +580,14 @@
             jax.ShapeDtypeStruct((Q, width_cells, depth_cells, lanes), f32),
             x_shape, x_shape, y_shape, y_shape,
         ),
-        in_specs=[SMEM, VMEM],
-        out_specs=(VMEM,) * 5,
+        in_specs=[SMEM, ANY],
+        out_specs=(ANY,) + (VMEM,) * 4,
+        scratch_shapes=[
+            pltpu.VMEM((Q, cells, lanes), f32),
+            pltpu.VMEM((Q, width_cells, depth_cells, lanes), f32),
+            pltpu.SemaphoreType.DMA((depth_cells // 8,)),
+            pltpu.SemaphoreType.DMA,
+        ],
         compiler_params=GRANT,
         cost_estimate=cost(12),
         name="first",
@@ -483,68 +610,83 @@
     ca = swap(sent_a, "image", image_count, 0)
     cb = swap(sent_b, "image", image_count, 1)
 
-    bumps = transfer.shape[2]
-    row = jnp.concatenate([transfer.reshape(-1), direction.astype(f32)])
-    row = jnp.pad(row, (0, lanes - row.shape[0]))
-    row, _ = lax.optimization_barrier((row, ia))
-    tables = lax.all_to_all(
-        jnp.broadcast_to(row, (image_count, 8, lanes)), "image", 0, 0, tiled=True
-    )[:, 0]
-    backward = tables[:, 5 * bumps].astype(jnp.int32)
-    tables = bump_tables(tables[:, : 5 * bumps].reshape(-1, 5, bumps), ray_cells).reshape(-1, 5 * bumps)
-
     depth_rows = depth_cells + 8 + 2 * PAD
     width_rows = width_cells + 2 * HALO
+    side = jax.ShapeDtypeStruct((Q, 4, depth_rows, lanes), f32)
+    inner_final, inner_flow, s2, s3, s4 = pl.pallas_call(
+        functools.partial(inner_kernel, depth_cells, width_cells),
+        out_shape=(
+            jax.ShapeDtypeStruct((Q, cells, lanes), f32),
+            jax.ShapeDtypeStruct((3, width_cells, depth_rows, lanes), f32),
+            side, side, side,
+        ),
+        in_specs=[VMEM, VMEM],
+        out_specs=(VMEM, VMEM, ANY, ANY, ANY),
+        scratch_shapes=[
+            pltpu.VMEM((Q, width_cells, depth_rows, lanes), f32),
+            pltpu.VMEM((Q, width_cells, depth_rows, lanes), f32),
+            pltpu.SemaphoreType.DMA((3, 2)),
+        ],
+        compiler_params=GRANT,
+        cost_estimate=cost(12),
+        name="inner",
+    )(turned, halo)
     final, vorticity = pl.pallas_call(
-        functools.partial(steps_kernel, depth_cells, width_cells),
+        functools.partial(outer_kernel, depth_cells, width_cells),
         out_shape=(
             jax.ShapeDtypeStruct((Q, cells, lanes), f32),
             jax.ShapeDtypeStruct((cells, lanes), jnp.bfloat16),
         ),
-        in_specs=[SMEM] + [VMEM] * 6,
-        out_specs=(VMEM, VMEM),
+        in_specs=[SMEM, ANY] + [VMEM] * 5 + [ANY] * 5,
+        out_specs=(ANY, VMEM),
         scratch_shapes=[
+            pltpu.VMEM((Q, 4, depth_cells, lanes), f32),
             pltpu.VMEM((Q, width_rows, depth_rows, lanes), f32),
             pltpu.VMEM((Q, width_rows, depth_rows, lanes), f32),
             pltpu.VMEM((3, width_rows, depth_rows, lanes), f32),
+            pltpu.VMEM((Q, cells, lanes), f32),
             pltpu.VMEM((cells, lanes), f32),
+            pltpu.SemaphoreType.DMA((11,)),
         ],
         compiler_params=GRANT,
-        cost_estimate=cost(25),
-        name="steps",
-    )(parity, turned, halo, ya, yb, ca, cb)
-
+        cost_estimate=cost(12),
+        name="outer",
+    )(parity, turned, halo, ya, yb, ca, cb, inner_final, inner_flow, s2, s3, s4)
+
+    tables = pl.pallas_call(
+        first_rows_kernel,
+        out_shape=jax.ShapeDtypeStruct((image_count, lanes), f32),
+        in_specs=[VMEM],
+        out_specs=VMEM,
+        cost_estimate=cost(1),
+        name="rows",
+    )(gathered)
+    backward = tables[:, 5 * bumps].astype(jnp.int32)
+    tables = bump_tables(tables[:, : 5 * bumps].reshape(-1, 5, bumps), ray_cells).reshape(-1, 5 * bumps)
     groups = depth_count
+    partial = pl.pallas_call(
+        functools.partial(render_kernel, depth_cells, width_cells, groups),
+        out_shape=jax.ShapeDtypeStruct((groups, 2, 4, width_cells, lanes), f32),
+        in_specs=[SMEM, SMEM, SMEM, VMEM],
+        out_specs=VMEM,
+        scratch_shapes=[
+            pltpu.VMEM((2, depth_cells, width_cells, lanes), f32),
+            pltpu.VMEM((2, depth_cells, width_cells, lanes), f32),
+        ],
+        compiler_params=GRANT,
+        cost_estimate=cost(18),
+        name="render",
+    )((i % 2).astype(jnp.int32)[None], tables, backward, vorticity)
+    slabs = lax.all_to_all(partial, "depth", 0, 0, tiled=True)
+    mine = jnp.stack([backward[2 * d + (i + k) % 2] for k in range(2)])
+    image = composite(slabs, mine[:, None])
     pieces = []
     for k in range(2):
-        pick = ((i + k) % 2).astype(jnp.int32)[None]
-        partial = pl.pallas_call(
-            functools.partial(render_kernel, depth_cells, width_cells, groups),
-            out_shape=jax.ShapeDtypeStruct((groups, 4, width_cells, lanes), f32),
-            in_specs=[SMEM, SMEM, SMEM, VMEM],
-            out_specs=VMEM,
-            scratch_shapes=[
-                pltpu.VMEM((2, depth_cells, width_cells, lanes), f32),
-                pltpu.VMEM((2, depth_cells, width_cells, lanes), f32),
-            ],
-            compiler_params=GRANT,
-            cost_estimate=cost(10),
-            name="render",
-        )(pick, tables, backward, vorticity)
-        slabs = lax.all_to_all(partial, "depth", 0, 0, tiled=True)
-        image = pl.pallas_call(
-            functools.partial(composite_kernel, depth_count),
-            out_shape=jax.ShapeDtypeStruct((4, width_cells, lanes), f32),
-            in_specs=[SMEM, SMEM, VMEM],
-            out_specs=VMEM,
-            cost_estimate=cost(1),
-            name="composite",
-        )(2 * d.astype(jnp.int32)[None] + pick, backward, slabs)
         route = []
         for sd in range(depth_count):
             for si in range(image_count):
                 route.append((sd * image_count + si, (si // 2) * image_count + 2 * sd + (si + k) % 2))
-        pieces.append(lax.ppermute(image, ("depth", "image"), route))
+        pieces.append(lax.ppermute(image[k], ("depth", "image"), route))
     flip = (i % 2) == 1
     top = jnp.where(flip, pieces[1], pieces[0])
     bottom = jnp.where(flip, pieces[0], pieces[1])

time: 120 us -> 125 us (1.042)
  starting transfers between devices: 38.4 us -> 24.6 us
  between operations: 1.4 us -> 14.9 us
  waiting for transfers between devices: 13.3 us -> 18.7 us
  other arithmetic: 2.82 us -> 5.95 us
  Pallas kernels: 58.6 us -> 56 us
    all_to_all x1 -> x0, starting transfers between devices: 7.6 us -> none  [on_device(): lax.all_to_all(jnp.broadcast_to(row, (image_count, 8, lanes)), 'image', 0...]
    all_to_all x2 -> x1, starting transfers between devices: 9.78 us -> 5.14 us  [on_device(): slabs = lax.all_to_all(partial, 'depth', 0, 0, tiled=True)]
    all_to_all x2 -> x1, waiting for transfers between devices: 0.01 us -> 4.31 us  [on_device(): slabs = lax.all_to_all(partial, 'depth', 0, 0, tiled=True)]
    ppermute x2, waiting for transfers between devices: 4.03 us -> 8.07 us  [on_device(): pieces.append(lax.ppermute(image[k], ('depth', 'image'), route))]
    ppermute x6, starting transfers between devices: 12.5 us -> 9.32 us  [swap(): lax.ppermute(value, axis, [(i, partner(i, count, phase)) for i in range(c...]
    ppermute x6, waiting for transfers between devices: 9.31 us -> 6.23 us  [swap(): lax.ppermute(value, axis, [(i, partner(i, count, phase)) for i in range(c...]
    pallas_call x2 -> x1, Pallas kernels: 18.2 us -> 16.2 us  [on_device(): pl.pallas_call(functools.partial(render_kernel, depth_cells, width_cells,...]
    convert_element_type x1 -> x2, other arithmetic: 0.73 us -> 2.23 us  [on_device(): backward = tables[:, 5 * bumps].astype(jnp.int32)]
  transfers between devices with their start and end apart: 11 -> 10, of which waited for: 5 -> 4; matrix products, arithmetic and copies ran while one was open for 1% -> 3% of each run, Pallas kernels for 12% -> 30%
where the time goes in v3:
time: 125 us
  Pallas kernels  56 us (45%)
  starting transfers between devices  24.6 us (20%)
  waiting for transfers between devices  18.7 us (15%)
  between operations  14.9 us (12%)
  other arithmetic  5.95 us (5%)
  local copies, waits for them, and re-layouts  4.52 us (4%)
    pallas_call x1, Pallas kernels, on_device(): pl.pallas_call(functools.partial(render_kernel, depth_cells, width_cells,...  16.2 us
    pallas_call x1, Pallas kernels, on_device(): pl.pallas_call(functools.partial(inner_kernel, depth_cells, width_cells),...  12.7 us
    pallas_call x1, Pallas kernels, on_device(): pl.pallas_call(functools.partial(outer_kernel, depth_cells, width_cells),...  11.6 us
    pallas_call x1, Pallas kernels, on_device(): pl.pallas_call(functools.partial(first_kernel, depth_cells, width_cells),...  11.1 us
    ppermute x2, starting transfers between devices, on_device(): pieces.append(lax.ppermute(image[k], ('depth', 'image'), route))  10.1 us
    ppermute x6, starting transfers between devices, swap(): lax.ppermute(value, axis, [(i, partner(i, count, phase)) for i in range(c...  9.32 us
    ppermute x2, waiting for transfers between devices, on_device(): pieces.append(lax.ppermute(image[k], ('depth', 'image'), route))  8.07 us
    ppermute x6, waiting for transfers between devices, swap(): lax.ppermute(value, axis, [(i, partner(i, count, phase)) for i in range(c...  6.23 us
  transfers between devices with their start and end apart: 10, of which 4 were waited for; matrix products, arithmetic and copies ran while one was open for 3% of the time, Pallas kernels for 30%

profile of v3, /device:TPU:17, one launch (start us, length us, event | category | flops | bytes accessed | tf_op | source)
XLA Modules:
  0.0 124.6 jit_solution(16986688422827037540)
XLA Ops:
  7.2 0.7 reduce.2
  9.4 0.7 pad_add_fusion.parity_ref
  10.1 11.1 %first.1 = (f32[19,16,32,128]{3,2,1,0:T(8,128)}, s16[10,8,16,128]{3,2,1,0:T(8,128)(2,1)}, s16[10,8,16,128]{3,2,1,0:T(8,128)(2,1)}, s16[76,32,128]{2,1,0:T(8,128)(2,1)}, s16[76,32,128]{2,1,0:T(8,128)(2,1)}) custom-call(s32[2]{0:T(128)} %pad_add_fusion.parity_ref, f32[19,512,128]{2,1,0:T(8,128)} %bitcast.243), custom_call_target="tpu_custom_call" | custom-call | bytes 44280000 | tf_op jit(solution)/shard_map/first/pallas_call | solution.py:577
  21.2 1.3 %collective-permute-start.2 = (s16[76,32,128]{2,1,0:T(8,128)(2,1)}, s16[76,32,128]{2,1,0:T(8,128)(2,1)S(1)}, u32[]{:S(2)}, u32[]{:S(2)}) collective-permute-start(s16[76,32,128]{2,1,0:T(8,128)(2,1)} %get-tuple-element.34), channel_id=1, source_target_pairs={{0,1},{1,0},{2,3},{3,2},{4,5},{5,4},{6,7},{7,6},{8,9},{9,8},{10,11... | collective-permute-start | bytes 1867784 | tf_op jit(solution)/shard_map/ppermute | solution.py:556
  22.5 5.3 %collective-permute-start.3 = (s16[76,32,128]{2,1,0:T(8,128)(2,1)}, s16[76,32,128]{2,1,0:T(8,128)(2,1)S(1)}, u32[]{:S(2)}, u32[]{:S(2)}) collective-permute-start(s16[76,32,128]{2,1,0:T(8,128)(2,1)} %get-tuple-element.35), channel_id=1, source_target_pairs={{0,15},{1,2},{2,1},{3,4},{4,3},{5,6},{6,5},{7,8},{8,7},{9,10},{10,... | collective-permute-start | bytes 1867784 | tf_op jit(solution)/shard_map/ppermute | solution.py:556
  27.8 1.2 collective-permute-start
  29.0 0.9 collective-permute-start.1
  30.5 5.6 %collective-permute-done.1.xb_ref = s16[10,8,16,128]{3,2,1,0:T(8,128)(2,1)S(1)} collective-permute-done((s16[10,8,16,128]{3,2,1,0:T(8,128)(2,1)}, s16[10,8,16,128]{3,2,1,0:T(8,128)(2,1)S(1)}, u32[]{:S(2)}, u32[]{:S(2)}) %collective-permute-start.1) | collective-permute-done | bytes 327712 | tf_op jit(solution)/shard_map/ppermute | solution.py:556
  36.1 0.7 copy-done.3
  36.9 2.5 %corner.1 = (f32[19,16,8,128]{3,2,1,0:T(8,128)}, s16[38,16,128]{2,1,0:T(8,128)(2,1)}, s16[38,16,128]{2,1,0:T(8,128)(2,1)}) custom-call(s32[2]{0:T(128)} %pad_add_fusion.parity_ref, s16[10,8,16,128]{3,2,1,0:T(8,128)(2,1)} %copy-done.2, s16[10,8,16,128]{3,2,1,0:T(8,128)(2,1)} %copy-done.3), custom_call_target="tpu_custom_call" | custom-call | bytes 7380000 | tf_op jit(solution)/shard_map/corner/pallas_call | solution.py:600
  40.0 12.7 %inner.1 = (f32[19,512,128]{2,1,0:T(8,128)}, f32[3,16,56,128]{3,2,1,0:T(8,128)}, f32[19,4,56,128]{3,2,1,0:T(8,128)}, f32[19,4,56,128]{3,2,1,0:T(8,128)}, f32[19,4,56,128]{3,2,1,0:T(8,128)}) custom-call(f32[19,16,32,128]{3,2,1,0:T(8,128)} %get-tuple-element.30.r_ref.r_hbm, f32[19,16,8,128]{3,2,1,0:T(8,128)} %get-tuple-element.33.h_ref), custom_call_target="tpu_custom_call" | custom-call | bytes 44280000 | tf_op jit(solution)/shard_map/inner/pallas_call | solution.py:616
  53.8 11.6 %outer.1 = (f32[19,512,128]{2,1,0:T(8,128)}, bf16[512,128]{1,0:T(8,128)(2,1)}) custom-call(s32[2]{0:T(128)} %pad_add_fusion.parity_ref, f32[19,16,32,128]{3,2,1,0:T(8,128)} %get-tuple-element.30.r_ref.r_hbm, f32[19,16,8,128]{3,2,1,0:T(8,128)} %get-tuple-element.33.h_ref, s16[76,32,128]{2,1,0:T(8,128)(2,1)} %copy-done, s16[76,32,128]{2,1,0:T(8,128)(2,1)} %copy-done.1, ...), custom_call_target="tpu_custom_call" | custom-call | bytes 44280000 | tf_op jit(solution)/shard_map/outer/pallas_call | solution.py:634
  65.5 1.8 %rows.1 = f32[16,128]{1,0:T(8,128)} custom-call(f32[2048,128]{1,0:T(8,128)} %all-gather.2.cloned.1.call-done.in_ref), custom_call_target="tpu_custom_call" | custom-call | bytes 3690000 | tf_op jit(solution)/shard_map/rows/pallas_call | solution.py:656
  67.3 1.5 %fusion.7.backward_ref = s32[16]{0:T(128)} fusion(f32[16,128]{1,0:T(8,128)} %rows.1), kind=kLoop, calls=%fused_computation.66 | loop fusion | flops 16 | bytes 128 | tf_op jit(solution)/shard_map/convert_element_type | solution.py:664
  68.8 0.8 copy.41
  69.6 0.7 copy.42.table_ref
  70.2 16.2 %render.1 = f32[8,2,4,16,128]{4,3,2,1,0:T(8,128)} custom-call(s32[1]{0:T(128)} %bitcast.1.pick_ref, f32[16,40]{1,0:T(8,128)} %copy.42.table_ref, s32[16]{0:T(128)} %fusion.7.backward_ref, bf16[512,128]{1,0:T(8,128)(2,1)} %get-tuple-element.44.vort_ref), custom_call_target="tpu_custom_call" | custom-call | bytes 66420000 | tf_op jit(solution)/shard_map/render/pallas_call | solution.py:667
  86.5 5.1 %all-to-all-start = ((f32[8,2,4,16,128]{4,3,2,1,0:T(8,128)}), f32[8,2,4,16,128]{4,3,2,1,0:T(8,128)S(1)}, u32[]{:S(2)}, u32[]{:S(2)}) async-start(f32[8,2,4,16,128]{4,3,2,1,0:T(8,128)} %render.1), calls=%async_computation | async-start | bytes 1048576 | tf_op jit(solution)/shard_map/all_to_all | solution.py:680
  91.6 0.8 slice_convert_fusion
  92.9 1.3 %add_compare_fusion = pred[2]{0:T(512)(128)(4,1)S(1)} fusion(s32[1]{0:T(128)} %bitcast.7, s32[1]{0:T(128)} %bitcast.6), kind=kLoop, calls=%fused_computation.65 | loop fusion | flops 4 | bytes 10 | tf_op jit(solution)/shard_map/eq | solution.py:522
  94.3 4.3 %all-to-all-done = f32[8,2,4,16,128]{4,3,2,1,0:T(8,128)S(1)} async-done(((f32[8,2,4,16,128]{4,3,2,1,0:T(8,128)}), f32[8,2,4,16,128]{4,3,2,1,0:T(8,128)S(1)}, u32[]{:S(2)}, u32[]{:S(2)}) %all-to-all-start) | async-done | bytes 524320 | tf_op jit(solution)/shard_map/all_to_all | solution.py:680
  98.9 6.6 %collective-permute-start.6 = (f32[4,16,128]{2,1,0:T(8,128)S(1)}, f32[4,16,128]{2,1,0:T(8,128)S(1)}, u32[]{:S(2)}, u32[]{:S(2)}) collective-permute-start(f32[4,16,128]{2,1,0:T(8,128)S(1)} %get-tuple-element.57), channel_id=1, source_target_pairs={{0,1},{1,0},{2,17},{3,16},{4,33},{5,32},{6,49},{7,48},{8,65},{9,64... | collective-permute-start | bytes 98312 | tf_op jit(solution)/shard_map/ppermute | solution.py:689
  105.5 3.4 %collective-permute-start.7 = (f32[4,16,128]{2,1,0:T(8,128)S(1)}, f32[4,16,128]{2,1,0:T(8,128)S(1)}, u32[]{:S(2)}, u32[]{:S(2)}) collective-permute-start(f32[4,16,128]{2,1,0:T(8,128)S(1)} %get-tuple-element.58), channel_id=1, source_target_pairs={{0,0},{1,1},{2,16},{3,17},{4,32},{5,33},{6,48},{7,49},{8,64},{9,65... | collective-permute-start | bytes 98312 | tf_op jit(solution)/shard_map/ppermute | solution.py:689
  109.0 8.1 %collective-permute-done.7 = f32[4,16,128]{2,1,0:T(8,128)S(1)} collective-permute-done((f32[4,16,128]{2,1,0:T(8,128)S(1)}, f32[4,16,128]{2,1,0:T(8,128)S(1)}, u32[]{:S(2)}, u32[]{:S(2)}) %collective-permute-start.7) | collective-permute-done | bytes 32800 | tf_op jit(solution)/shard_map/ppermute | solution.py:689
  (37 shorter events, 4.7 us)
Async XLA Ops:
  7.2 58.3 %all-gather.2.cloned.1.call-start = ((), (), s32[]{:S(2)}) async-start(), calls=%async_computation.1 | async-start | bytes 1114112 | tf_op jit(solution)/shard_map/all_gather | solution.py:572
  21.2 31.5 %collective-permute-start.2 = (s16[76,32,128]{2,1,0:T(8,128)(2,1)}, s16[76,32,128]{2,1,0:T(8,128)(2,1)S(1)}, u32[]{:S(2)}, u32[]{:S(2)}) collective-permute-start(s16[76,32,128]{2,1,0:T(8,128)(2,1)} %get-tuple-element.34), channel_id=1, source_target_pairs={{0,1},{1,0},{2,3},{3,2},{4,5},{5,4},{6,7},{7,6},{8,9},{9,8},{10,11... | collective-permute-start | bytes 1867784 | tf_op jit(solution)/shard_map/ppermute | solution.py:556
  22.5 30.2 %collective-permute-start.3 = (s16[76,32,128]{2,1,0:T(8,128)(2,1)}, s16[76,32,128]{2,1,0:T(8,128)(2,1)S(1)}, u32[]{:S(2)}, u32[]{:S(2)}) collective-permute-start(s16[76,32,128]{2,1,0:T(8,128)(2,1)} %get-tuple-element.35), channel_id=1, source_target_pairs={{0,15},{1,2},{2,1},{3,4},{4,3},{5,6},{6,5},{7,8},{8,7},{9,10},{10,... | collective-permute-start | bytes 1867784 | tf_op jit(solution)/shard_map/ppermute | solution.py:556
  27.8 2.7 %collective-permute-start = (s16[10,8,16,128]{3,2,1,0:T(8,128)(2,1)}, s16[10,8,16,128]{3,2,1,0:T(8,128)(2,1)S(1)}, u32[]{:S(2)}, u32[]{:S(2)}) collective-permute-start(s16[10,8,16,128]{3,2,1,0:T(8,128)(2,1)} %get-tuple-element.31), channel_id=1, source_target_pairs={{0,16},{16,0},{32,48},{48,32},{64,80},{80,64},{96,112},{112,96},{1... | collective-permute-start | bytes 983048 | tf_op jit(solution)/shard_map/ppermute | solution.py:556
  29.0 7.1 %collective-permute-start.1 = (s16[10,8,16,128]{3,2,1,0:T(8,128)(2,1)}, s16[10,8,16,128]{3,2,1,0:T(8,128)(2,1)S(1)}, u32[]{:S(2)}, u32[]{:S(2)}) collective-permute-start(s16[10,8,16,128]{3,2,1,0:T(8,128)(2,1)} %get-tuple-element.32), channel_id=1, source_target_pairs={{0,112},{16,32},{32,16},{48,64},{64,48},{80,96},{96,80},{112,0},{1... | collective-permute-start | bytes 983048 | tf_op jit(solution)/shard_map/ppermute | solution.py:556
  30.5 5.6 %copy-start.2 = (s16[10,8,16,128]{3,2,1,0:T(8,128)(2,1)}, s16[10,8,16,128]{3,2,1,0:T(8,128)(2,1)S(1)}, u32[]{:S(2)}) copy-start(s16[10,8,16,128]{3,2,1,0:T(8,128)(2,1)S(1)} %collective-permute-done.xa_ref) | copy-start | bytes 983044
  36.1 0.7 copy-start.3
  39.4 13.3 %collective-permute-start.4 = (s16[38,16,128]{2,1,0:T(8,128)(2,1)}, s16[38,16,128]{2,1,0:T(8,128)(2,1)S(1)}, u32[]{:S(2)}, u32[]{:S(2)}) collective-permute-start(s16[38,16,128]{2,1,0:T(8,128)(2,1)} %get-tuple-element.36), channel_id=1, source_target_pairs={{0,1},{1,0},{2,3},{3,2},{4,5},{5,4},{6,7},{7,6},{8,9},{9,8},{10,11... | collective-permute-start | bytes 466952 | tf_op jit(solution)/shard_map/ppermute | solution.py:556
  39.4 13.3 %collective-permute-start.5 = (s16[38,16,128]{2,1,0:T(8,128)(2,1)}, s16[38,16,128]{2,1,0:T(8,128)(2,1)S(1)}, u32[]{:S(2)}, u32[]{:S(2)}) collective-permute-start(s16[38,16,128]{2,1,0:T(8,128)(2,1)} %get-tuple-element.37), channel_id=1, source_target_pairs={{0,15},{1,2},{2,1},{3,4},{4,3},{5,6},{6,5},{7,8},{8,7},{9,10},{10,... | collective-permute-start | bytes 466952 | tf_op jit(solution)/shard_map/ppermute | solution.py:556
  52.7 0.7 copy-start.4
  52.7 0.7 copy-start.5
  52.7 0.9 copy-start
  52.7 1.1 copy-start.1
  86.5 12.1 %all-to-all-start = ((f32[8,2,4,16,128]{4,3,2,1,0:T(8,128)}), f32[8,2,4,16,128]{4,3,2,1,0:T(8,128)S(1)}, u32[]{:S(2)}, u32[]{:S(2)}) async-start(f32[8,2,4,16,128]{4,3,2,1,0:T(8,128)} %render.1), calls=%async_computation | async-start | bytes 1048576 | tf_op jit(solution)/shard_map/all_to_all | solution.py:680
  98.9 10.1 %collective-permute-start.6 = (f32[4,16,128]{2,1,0:T(8,128)S(1)}, f32[4,16,128]{2,1,0:T(8,128)S(1)}, u32[]{:S(2)}, u32[]{:S(2)}) collective-permute-start(f32[4,16,128]{2,1,0:T(8,128)S(1)} %get-tuple-element.57), channel_id=1, source_target_pairs={{0,1},{1,0},{2,17},{3,16},{4,33},{5,32},{6,49},{7,48},{8,65},{9,64... | collective-permute-start | bytes 98312 | tf_op jit(solution)/shard_map/ppermute | solution.py:689
  105.5 11.5 %collective-permute-start.7 = (f32[4,16,128]{2,1,0:T(8,128)S(1)}, f32[4,16,128]{2,1,0:T(8,128)S(1)}, u32[]{:S(2)}, u32[]{:S(2)}) collective-permute-start(f32[4,16,128]{2,1,0:T(8,128)S(1)} %get-tuple-element.58), channel_id=1, source_target_pairs={{0,0},{1,1},{2,16},{3,17},{4,32},{5,33},{6,48},{7,49},{8,64},{9,65... | collective-permute-start | bytes 98312 | tf_op jit(solution)/shard_map/ppermute | solution.py:689
Sparse Core Ops, SparseCore 0:
  10.7 51.6 all-gather.1

commit v4 on v3

--- a/solution.py
+++ b/solution.py
@@ -26,7 +26,7 @@
 
 X_PAIRS = tuple(
     (a, b, 5) for a, b in zip((1, 7, 9, 11, 13), (2, 8, 10, 12, 14))
-) + ((0, 3, 4), (4, 5, 4), (6, 15, 4), (16, 17, 4), (18, None, 4))
+) + ((3, 4, 4), (5, 6, 4), (15, 16, 4), (17, 18, 4), (0, None, 4))
 
 
 def low_rows(p):
@@ -92,7 +92,7 @@
 
 
 def code(value, p):
-    return jnp.round(value * (SCALE / WEIGHT[p]) - SCALE)
+    return value * (SCALE / WEIGHT[p]) + (32768.5 - SCALE)
 
 
 def decode(value, p):
@@ -107,79 +107,122 @@
     return jnp.concatenate([first, second], axis=0).astype(jnp.int32).astype(jnp.int16)
 
 
+def pack_code(first, second):
+    whole = jnp.concatenate([first, second], axis=0).astype(jnp.int32)
+    return (whole - 32768).astype(jnp.int16)
+
+
 def wide(value):
     return value.astype(jnp.int32).astype(jnp.float32)
 
 
-def first_kernel(
-    depth_cells, width_cells, parity_ref, f_hbm, r_hbm, da_ref, db_ref, ia_ref, ib_ref, f_ref, r_ref, in_sems, out_sem
-):
-    tiles = depth_cells // 8
+def collide_chunk(f_ref, r_ref, from_row, to_row, width_cells):
+    def at_y(y, carry):
+        f = [f_ref[p, pl.ds(from_row + y, 8, stride=width_cells), :] for p in range(Q)]
+        out = collide(f)
+        for p in range(Q):
+            value = pltpu.roll(out[p], low_rows(p), 0)
+            cz = VEL[p][2]
+            r_ref[p, y, to_row : to_row + 8, :] = value if cz == 0 else pltpu.roll(value, cz % 128, 1)
+        return carry
+
+    lax.fori_loop(0, width_cells, at_y, 0, unroll=2)
+
+
+def edge_kernel(depth_cells, width_cells, parity_ref, f_hbm, r_hbm, da_ref, db_ref, f_ref, r_ref, in_sems, out_sem):
     rows = row_index()
     chunk = 8 * width_cells
-    loads = [
-        pltpu.make_async_copy(
-            f_hbm.at[:, pl.ds(j * chunk, chunk)], f_ref.at[:, pl.ds(j * chunk, chunk)], in_sems.at[j]
+    loads = []
+    for k, j in enumerate((0, depth_cells // 8 - 1)):
+        loads.append(
+            pltpu.make_async_copy(
+                f_hbm.at[:, pl.ds(j * chunk, chunk)], f_ref.at[:, pl.ds(k * chunk, chunk)], in_sems.at[k]
+            )
         )
-        for j in range(tiles)
-    ]
     for load in loads:
         load.start()
-
-    for j in range(tiles):
-        loads[j].wait()
-
-        def at_y(y, carry):
-            f = [f_ref[p, pl.ds(j * chunk + y, 8, stride=width_cells), :] for p in range(Q)]
-            out = collide(f)
-            for p in range(Q):
-                value = pltpu.roll(out[p], low_rows(p), 0)
-                cz = VEL[p][2]
-                r_ref[p, y, 8 * j : 8 * j + 8, :] = value if cz == 0 else pltpu.roll(value, cz % 128, 1)
-            return carry
-
-        lax.fori_loop(0, width_cells, at_y, 0, unroll=2)
-
+    for k, load in enumerate(loads):
+        load.wait()
+        collide_chunk(f_ref, r_ref, k * chunk, 8 * k, width_cells)
     keep_r = pltpu.make_async_copy(r_ref, r_hbm, out_sem)
     keep_r.start()
 
     odd_depth = jnp.full((8, 128), parity_ref[0], jnp.int32) == 1
-    odd_image = jnp.full((8, 128), parity_ref[1], jnp.int32) == 1
 
     def face_x(t, carry):
         for number, (a, b, n) in enumerate(X_PAIRS):
-            low, high = [], []
+            da, db = [], []
             for k in range(2):
                 y = 2 * t + k
-                for sent, first_row in ((low, 0), (high, depth_cells - 8)):
-                    piece = code(r_ref[a, y, first_row : first_row + 8, :], a)
-                    if b is not None:
-                        other = code(r_ref[b, y, first_row : first_row + 8, :], b)
-                        other = pltpu.roll(other, n, 0)
-                        keep = rows < n if sent is high else rows >= n
-                        piece = jnp.where(keep, piece, other)
-                    sent.append(piece)
-            da = [jnp.where(odd_depth, l, h) for l, h in zip(low, high)]
-            db = [jnp.where(odd_depth, h, l) for l, h in zip(low, high)]
-            da_ref[number, t] = pack16(*da)
-            db_ref[number, t] = pack16(*db)
+                low, high = (r_ref[a, y, first : first + 8, :] for first in (0, 8))
+                if b is not None:
+                    other_low, other_high = (
+                        pltpu.roll(r_ref[b, y, first : first + 8, :], n, 0) for first in (0, 8)
+                    )
+                    low = jnp.where(rows >= n, low, other_low)
+                    high = jnp.where(rows < n, high, other_high)
+                low, high = code(low, a), code(high, a)
+                da.append(jnp.where(odd_depth, low, high))
+                db.append(jnp.where(odd_depth, high, low))
+            da_ref[number, t] = pack_code(*da)
+            db_ref[number, t] = pack_code(*db)
         return carry
 
     lax.fori_loop(0, width_cells // 2, face_x, 0)
+    keep_r.wait()
+
+
+def middle_kernel(
+    depth_cells, width_cells, parity_ref, f_hbm, edge_hbm, r_hbm, ia_ref, ib_ref, f_ref, r_ref, edge_ref, in_sems, out_sem
+):
+    chunk = 8 * width_cells
+    tiles = depth_cells // 8
+    loads = []
+    for j in range(1, tiles - 1):
+        loads.append(
+            pltpu.make_async_copy(
+                f_hbm.at[:, pl.ds(j * chunk, chunk)], f_ref.at[:, pl.ds((j - 1) * chunk, chunk)], in_sems.at[j]
+            )
+        )
+    for side in range(2):
+        first = side * (width_cells - HALO)
+        loads.append(
+            pltpu.make_async_copy(
+                edge_hbm.at[:, pl.ds(first, HALO)], edge_ref.at[:, pl.ds(side * HALO, HALO)],
+                in_sems.at[side * (tiles - 1)],
+            )
+        )
+    for load in loads:
+        load.start()
+    for j in range(tiles - 2):
+        loads[j].wait()
+        collide_chunk(f_ref, r_ref, j * chunk, 8 * j, width_cells)
+    keep_r = pltpu.make_async_copy(r_ref, r_hbm, out_sem)
+    keep_r.start()
+    for load in loads[tiles - 2 :]:
+        load.wait()
+
+    odd_image = jnp.full((8, 128), parity_ref[1], jnp.int32) == 1
+
+    def piece(p, y, t):
+        if t in (0, tiles - 1):
+            row = y if y < HALO else y - (width_cells - 2 * HALO)
+            first = 0 if t == 0 else 8
+            return edge_ref[p, row, first : first + 8, :]
+        return r_ref[p, y, 8 * t - 8 : 8 * t, :]
 
     low_face = face_list(0, 1)
     high_face = face_list(width_cells - 1, -1)
     for index, ((yl, pl_), (yh, ph)) in enumerate(zip(low_face, high_face)):
-        for c in range(depth_cells // 16):
+        for c in range(tiles // 2):
             a, b = [], []
-            for k in range(2):
-                first_row = 16 * c + 8 * k
-                low = code(r_ref[pl_, yl, first_row : first_row + 8, :], pl_)
-                high = code(r_ref[ph, yh, first_row : first_row + 8, :], ph)
+            for t in (2 * c, 2 * c + 1):
+                low = code(piece(pl_, yl, t), pl_)
+                high = code(piece(ph, yh, t), ph)
                 a.append(jnp.where(odd_image, low, high))
                 b.append(jnp.where(odd_image, high, low))
-            ia_ref[index, 16 * c : 16 * c + 16, :] = pack16(*a)
-            ib_ref[index, 16 * c : 16 * c + 16, :] = pack16(*b)
+            ia_ref[index, 16 * c : 16 * c + 16, :] = pack_code(*a)
+            ib_ref[index, 16 * c : 16 * c + 16, :] = pack_code(*b)
     keep_r.wait()
 
 
@@ -273,15 +316,38 @@
             ]
 
 
+def spin_row(flow_ref, out_ref, y, origin, tiles, width_cells):
+    for t in range(tiles):
+        first = BASE + 8 * t
+
+        def dx(axis):
+            return (flow_ref[axis, y, first + 1 : first + 9, :] - flow_ref[axis, y, first - 1 : first + 7, :]) * 0.5
+
+        def dy(axis):
+            return (flow_ref[axis, y + 1, first : first + 8, :] - flow_ref[axis, y - 1, first : first + 8, :]) * 0.5
+
+        def dz(axis):
+            value = flow_ref[axis, y, first : first + 8, :]
+            return (pltpu.roll(value, 127, 1) - pltpu.roll(value, 1, 1)) * 0.5
+
+        sx = dy(2) - dz(1)
+        sy = dz(0) - dx(2)
+        sz = dx(1) - dy(0)
+        out_ref[pl.ds(8 * t * width_cells + y - origin, 8, stride=width_cells), :] = jnp.sqrt(
+            sx * sx + sy * sy + sz * sz
+        )
+
+
 def inner_kernel(
-    depth_cells, width_cells, r_ref, h_ref, final_ref, flow_ref, s2_hbm, s3_hbm, s4_hbm, sa_ref, sb_ref, sems
+    depth_cells, width_cells, e_ref, r_ref, h_ref, final_ref, flow_ref, spin_ref, s2_hbm, s3_hbm, s4_hbm, sa_ref, sb_ref, sems
 ):
     tiles = depth_cells // 8
     rows = row_index()
 
     def own(y, carry):
         for p in range(Q):
-            pieces = [r_ref[p, y, 8 * t : 8 * t + 8, :] for t in range(tiles)]
+            pieces = [r_ref[p, y, 8 * t : 8 * t + 8, :] for t in range(tiles - 2)]
+            pieces = [e_ref[p, y, 0:8, :]] + pieces + [e_ref[p, y, 8:16, :]]
             put_streamed(sa_ref, p, y, pieces, decode(h_ref[p, y], p), rows)
         return carry
 
@@ -320,29 +386,36 @@
         return carry
 
     lax.fori_loop(STEPS, width_cells - STEPS, last, 0)
+
+    def spins(y, carry):
+        spin_row(flow_ref, spin_ref, y, 0, tiles, width_cells)
+        return carry
+
+    lax.fori_loop(HALO, width_cells - HALO, spins, 0, unroll=2)
     for copy in kept3 + kept4:
         copy.wait()
 
 
 def outer_kernel(
-    depth_cells, width_cells, parity_ref, r_hbm, h_ref, ya_ref, yb_ref, ca_ref, cb_ref,
-    final_in, flow_in, s2_in, s3_in, s4_in, out_hbm, vort_ref,
-    r_ref, sa_ref, sb_ref, flow_ref, out_ref, plain_ref, sems,
+    depth_cells, width_cells, parity_ref, e_hbm, r_hbm, h_ref, ya_ref, yb_ref, ca_ref, cb_ref,
+    final_in, flow_in, spin_in, s2_in, s3_in, s4_in, out_hbm, vort_ref,
+    e_ref, r_ref, sa_ref, sb_ref, flow_ref, out_ref, plain_ref, sems,
 ):
     tiles = depth_cells // 8
     rows = row_index()
     odd_image = jnp.full((8, 128), parity_ref[1], jnp.int32) == 1
 
-    moves = [
-        (r_hbm.at[:, pl.ds(0, 2)], r_ref.at[:, pl.ds(0, 2)]),
-        (r_hbm.at[:, pl.ds(width_cells - 2, 2)], r_ref.at[:, pl.ds(2, 2)]),
-    ]
+    moves = []
+    for source, target in ((e_hbm, e_ref), (r_hbm, r_ref)):
+        moves.append((source.at[:, pl.ds(0, 2)], target.at[:, pl.ds(0, 2)]))
+        moves.append((source.at[:, pl.ds(width_cells - 2, 2)], target.at[:, pl.ds(2, 2)]))
     for step, source, target in ((1, s2_in, sb_ref), (2, s3_in, sa_ref), (3, s4_in, sb_ref)):
         moves.append((source.at[:, pl.ds(0, 2)], target.at[:, pl.ds(HALO + step, 2)]))
         moves.append((source.at[:, pl.ds(2, 2)], target.at[:, pl.ds(HALO + width_cells - 2 - step, 2)]))
     inner = pl.ds(STEPS, width_cells - 2 * STEPS)
     moves.append((flow_in.at[:, inner], flow_ref.at[:, pl.ds(HALO + STEPS, width_cells - 2 * STEPS)]))
     moves.append((final_in, out_ref))
+    moves.append((spin_in, plain_ref))
     copies = [pltpu.make_async_copy(a, b, sems.at[k]) for k, (a, b) in enumerate(moves)]
     for copy in copies:
         copy.start()
@@ -368,11 +441,12 @@
             put_streamed(sa_ref, ph, yh - width_cells + HALO, low[1:], low[0], rows)
             put_streamed(sa_ref, pl_, yl + width_cells + HALO, high[1:], high[0], rows)
 
-    copies[0].wait()
-    copies[1].wait()
+    for copy in copies[:4]:
+        copy.wait()
     for k, y in enumerate((0, 1, width_cells - 2, width_cells - 1)):
         for p in range(Q):
-            pieces = [r_ref[p, k, 8 * t : 8 * t + 8, :] for t in range(tiles)]
+            pieces = [r_ref[p, k, 8 * t : 8 * t + 8, :] for t in range(tiles - 2)]
+            pieces = [e_ref[p, k, 0:8, :]] + pieces + [e_ref[p, k, 8:16, :]]
             put_streamed(sa_ref, p, y + HALO, pieces, decode(h_ref[p, y], p), rows)
 
     def stage(source, target, step, shift):
@@ -386,15 +460,14 @@
         lax.fori_loop(0, HALO, both, 0)
 
     stage(sa_ref, sb_ref, 1, 0)
-    copies[2].wait()
-    copies[3].wait()
+    for copy in copies[4:6]:
+        copy.wait()
     stage(sb_ref, sa_ref, 2, 0)
-    copies[4].wait()
-    copies[5].wait()
+    for copy in copies[6:8]:
+        copy.wait()
     stage(sa_ref, sb_ref, 3, 4)
-    copies[6].wait()
-    copies[7].wait()
-    copies[9].wait()
+    for copy in copies[8:13]:
+        copy.wait()
 
     def finish(k, carry):
         final_row(sb_ref, out_ref, HALO + k, HALO, tiles, width_cells)
@@ -402,7 +475,7 @@
         return carry
 
     lax.fori_loop(0, STEPS, finish, 0)
-    keep_out = pltpu.make_async_copy(out_ref, out_hbm, sems.at[10])
+    keep_out = pltpu.make_async_copy(out_ref, out_hbm, sems.at[13])
     keep_out.start()
 
     def flows(k, carry):
@@ -411,31 +484,13 @@
         return carry
 
     lax.fori_loop(0, HALO, flows, 0)
-    copies[8].wait()
-
-    def spin_at(y, carry):
-        for t in range(tiles):
-            first = BASE + 8 * t
-
-            def dx(axis):
-                return (flow_ref[axis, y, first + 1 : first + 9, :] - flow_ref[axis, y, first - 1 : first + 7, :]) * 0.5
-
-            def dy(axis):
-                return (flow_ref[axis, y + 1, first : first + 8, :] - flow_ref[axis, y - 1, first : first + 8, :]) * 0.5
-
-            def dz(axis):
-                value = flow_ref[axis, y, first : first + 8, :]
-                return (pltpu.roll(value, 127, 1) - pltpu.roll(value, 1, 1)) * 0.5
-
-            sx = dy(2) - dz(1)
-            sy = dz(0) - dx(2)
-            sz = dx(1) - dy(0)
-            plain_ref[pl.ds(8 * t * width_cells + y - HALO, 8, stride=width_cells), :] = jnp.sqrt(
-                sx * sx + sy * sy + sz * sz
-            )
-        return carry
-
-    lax.fori_loop(HALO, HALO + width_cells, spin_at, 0, unroll=2)
+
+    def spins(k, carry):
+        spin_row(flow_ref, plain_ref, HALO + k, HALO, tiles, width_cells)
+        spin_row(flow_ref, plain_ref, width_cells + k, HALO, tiles, width_cells)
+        return carry
+
+    lax.fori_loop(0, HALO, spins, 0)
 
     def rounded(x, carry):
         at = pl.ds(pl.multiple_of(x * 16, 16), 16)
@@ -464,9 +519,7 @@
 BLOCK = 4
 
 
-def render_kernel(depth_cells, width_cells, groups, pick_ref, table_ref, backward_ref, vort_ref, image_ref, place_ref, fade_ref):
-    bumps = table_ref.shape[1] // 5
-
+def render_kernel(depth_cells, width_cells, groups, bumps, pick_ref, table_ref, vort_ref, image_ref, place_ref, fade_ref):
     def prepare(x, carry):
         at = pl.ds(pl.multiple_of(x * width_cells, width_cells), width_cells)
         value = vort_ref[at, :].astype(jnp.float32)
@@ -484,7 +537,7 @@
         group = number // 2
         slot = number % 2
         m = 2 * group + (pick_ref[0] + slot) % 2
-        order = backward_ref[m]
+        order = jnp.where(table_ref[m, 0, 5 * bumps] > 0.5, 1, 0)
 
         def cells(block, state):
             clear, red, green, blue = state
@@ -492,9 +545,9 @@
             place = place_ref[order, at]
             total = [None] * 4
             for k in range(bumps):
-                bump = jnp.exp2(place * table_ref[m, k])
+                bump = jnp.exp2(place * table_ref[m, 0, k])
                 for c in range(4):
-                    term = bump * table_ref[m, (1 + c) * bumps + k]
+                    term = bump * table_ref[m, 0, (1 + c) * bumps + k]
                     total[c] = term if total[c] is None else total[c] + term
             fade = fade_ref[order, at]
             passing = jnp.exp2(-(total[0] * fade))
@@ -519,7 +572,7 @@
 
 
 def composite(slabs, backward):
-    chooser = backward[:, :, None] == 1
+    chooser = backward[:, :, None] > 0.5
     count = slabs.shape[0]
     clear = 1.0
     color = [0.0] * 3
@@ -528,14 +581,6 @@
         color = [color[c] + clear * piece[c] for c in range(3)]
         clear = clear * piece[3]
     return jnp.stack(color + [1.0 - clear], axis=1)
-
-
-GATHER_ROWS = 128
-
-
-def first_rows_kernel(in_ref, out_ref):
-    for m in range(out_ref.shape[0]):
-        out_ref[m : m + 1, :] = in_ref[m * GATHER_ROWS : m * GATHER_ROWS + 1, :]
 
 
 ANY = pl.BlockSpec(memory_space=pl.ANY)
@@ -566,32 +611,42 @@
     parity = jnp.stack([d % 2, i % 2]).astype(jnp.int32)
     faces = len(face_list(0, 1))
 
-    bumps = transfer.shape[2]
-    row = jnp.concatenate([transfer.reshape(-1), direction.astype(f32)])
-    row = jnp.pad(row[None], ((0, GATHER_ROWS - 1), (0, lanes - row.shape[0])))
-    gathered = lax.all_gather(row, "image", axis=0, tiled=True)
-
     x_shape = jax.ShapeDtypeStruct((len(X_PAIRS), width_cells // 2, 16, lanes), i16)
     y_shape = jax.ShapeDtypeStruct((faces, depth_cells, lanes), i16)
     c_shape = jax.ShapeDtypeStruct((faces // 2, 16, lanes), i16)
-    turned, da, db, ia, ib = pl.pallas_call(
-        functools.partial(first_kernel, depth_cells, width_cells),
-        out_shape=(
-            jax.ShapeDtypeStruct((Q, width_cells, depth_cells, lanes), f32),
-            x_shape, x_shape, y_shape, y_shape,
-        ),
+    half = (depth_cells - 16, 16)
+    field = populations.reshape(Q, cells, lanes)
+    edge, da, db = pl.pallas_call(
+        functools.partial(edge_kernel, depth_cells, width_cells),
+        out_shape=(jax.ShapeDtypeStruct((Q, width_cells, half[1], lanes), f32), x_shape, x_shape),
         in_specs=[SMEM, ANY],
-        out_specs=(ANY,) + (VMEM,) * 4,
+        out_specs=(ANY, VMEM, VMEM),
         scratch_shapes=[
-            pltpu.VMEM((Q, cells, lanes), f32),
-            pltpu.VMEM((Q, width_cells, depth_cells, lanes), f32),
+            pltpu.VMEM((Q, half[1] * width_cells, lanes), f32),
+            pltpu.VMEM((Q, width_cells, half[1], lanes), f32),
+            pltpu.SemaphoreType.DMA((2,)),
+            pltpu.SemaphoreType.DMA,
+        ],
+        compiler_params=GRANT,
+        cost_estimate=cost(6),
+        name="edge",
+    )(parity, field)
+    middle, ia, ib = pl.pallas_call(
+        functools.partial(middle_kernel, depth_cells, width_cells),
+        out_shape=(jax.ShapeDtypeStruct((Q, width_cells, half[0], lanes), f32), y_shape, y_shape),
+        in_specs=[SMEM, ANY, ANY],
+        out_specs=(ANY, VMEM, VMEM),
+        scratch_shapes=[
+            pltpu.VMEM((Q, half[0] * width_cells, lanes), f32),
+            pltpu.VMEM((Q, width_cells, half[0], lanes), f32),
+            pltpu.VMEM((Q, 2 * HALO, half[1], lanes), f32),
             pltpu.SemaphoreType.DMA((depth_cells // 8,)),
             pltpu.SemaphoreType.DMA,
         ],
         compiler_params=GRANT,
-        cost_estimate=cost(12),
-        name="first",
-    )(parity, populations.reshape(Q, cells, lanes))
+        cost_estimate=cost(6),
+        name="middle",
+    )(parity, field, edge)
 
     xa = swap(da, "depth", depth_count, 0)
     xb = swap(db, "depth", depth_count, 1)
@@ -613,15 +668,16 @@
     depth_rows = depth_cells + 8 + 2 * PAD
     width_rows = width_cells + 2 * HALO
     side = jax.ShapeDtypeStruct((Q, 4, depth_rows, lanes), f32)
-    inner_final, inner_flow, s2, s3, s4 = pl.pallas_call(
+    inner_final, inner_flow, inner_spin, s2, s3, s4 = pl.pallas_call(
         functools.partial(inner_kernel, depth_cells, width_cells),
         out_shape=(
             jax.ShapeDtypeStruct((Q, cells, lanes), f32),
             jax.ShapeDtypeStruct((3, width_cells, depth_rows, lanes), f32),
+            jax.ShapeDtypeStruct((cells, lanes), f32),
             side, side, side,
         ),
-        in_specs=[VMEM, VMEM],
-        out_specs=(VMEM, VMEM, ANY, ANY, ANY),
+        in_specs=[VMEM] * 3,
+        out_specs=(VMEM, VMEM, VMEM, ANY, ANY, ANY),
         scratch_shapes=[
             pltpu.VMEM((Q, width_cells, depth_rows, lanes), f32),
             pltpu.VMEM((Q, width_cells, depth_rows, lanes), f32),
@@ -630,44 +686,43 @@
         compiler_params=GRANT,
         cost_estimate=cost(12),
         name="inner",
-    )(turned, halo)
+    )(edge, middle, halo)
+
+    bumps = transfer.shape[2]
+    row = jnp.concatenate([bump_tables(transfer, ray_cells).reshape(-1), direction.astype(f32)])
+    row = jnp.pad(row, (0, lanes - row.shape[0]))
+    row, _ = lax.optimization_barrier((row, inner_spin))
+    tables = lax.all_to_all(
+        jnp.broadcast_to(row, (image_count, 8, lanes)), "image", 0, 0, tiled=True
+    )
     final, vorticity = pl.pallas_call(
         functools.partial(outer_kernel, depth_cells, width_cells),
         out_shape=(
             jax.ShapeDtypeStruct((Q, cells, lanes), f32),
             jax.ShapeDtypeStruct((cells, lanes), jnp.bfloat16),
         ),
-        in_specs=[SMEM, ANY] + [VMEM] * 5 + [ANY] * 5,
+        in_specs=[SMEM, ANY, ANY] + [VMEM] * 5 + [ANY] * 6,
         out_specs=(ANY, VMEM),
         scratch_shapes=[
-            pltpu.VMEM((Q, 4, depth_cells, lanes), f32),
+            pltpu.VMEM((Q, 4, half[1], lanes), f32),
+            pltpu.VMEM((Q, 4, half[0], lanes), f32),
             pltpu.VMEM((Q, width_rows, depth_rows, lanes), f32),
             pltpu.VMEM((Q, width_rows, depth_rows, lanes), f32),
             pltpu.VMEM((3, width_rows, depth_rows, lanes), f32),
             pltpu.VMEM((Q, cells, lanes), f32),
             pltpu.VMEM((cells, lanes), f32),
-            pltpu.SemaphoreType.DMA((11,)),
+            pltpu.SemaphoreType.DMA((14,)),
         ],
         compiler_params=GRANT,
         cost_estimate=cost(12),
         name="outer",
-    )(parity, turned, halo, ya, yb, ca, cb, inner_final, inner_flow, s2, s3, s4)
-
-    tables = pl.pallas_call(
-        first_rows_kernel,
-        out_shape=jax.ShapeDtypeStruct((image_count, lanes), f32),
-        in_specs=[VMEM],
-        out_specs=VMEM,
-        cost_estimate=cost(1),
-        name="rows",
-    )(gathered)
-    backward = tables[:, 5 * bumps].astype(jnp.int32)
-    tables = bump_tables(tables[:, : 5 * bumps].reshape(-1, 5, bumps), ray_cells).reshape(-1, 5 * bumps)
+    )(parity, edge, middle, halo, ya, yb, ca, cb, inner_final, inner_flow, inner_spin, s2, s3, s4)
+
     groups = depth_count
     partial = pl.pallas_call(
-        functools.partial(render_kernel, depth_cells, width_cells, groups),
+        functools.partial(render_kernel, depth_cells, width_cells, groups, bumps),
         out_shape=jax.ShapeDtypeStruct((groups, 2, 4, width_cells, lanes), f32),
-        in_specs=[SMEM, SMEM, SMEM, VMEM],
+        in_specs=[SMEM, SMEM, VMEM],
         out_specs=VMEM,
         scratch_shapes=[
             pltpu.VMEM((2, depth_cells, width_cells, lanes), f32),
@@ -676,9 +731,9 @@
         compiler_params=GRANT,
         cost_estimate=cost(18),
         name="render",
-    )((i % 2).astype(jnp.int32)[None], tables, backward, vorticity)
+    )((i % 2).astype(jnp.int32)[None], tables, vorticity)
     slabs = lax.all_to_all(partial, "depth", 0, 0, tiled=True)
-    mine = jnp.stack([backward[2 * d + (i + k) % 2] for k in range(2)])
+    mine = jnp.stack([tables[2 * d + (i + k) % 2, 0, 5 * bumps] for k in range(2)])
     image = composite(slabs, mine[:, None])
     pieces = []
     for k in range(2):

time: 125 us -> 115 us (0.920)
  between operations: 14.9 us -> 1.5 us
  starting transfers between devices: 24.6 us -> 31.8 us
  waiting for transfers between devices: 18.7 us -> 13.7 us
  other arithmetic: 5.95 us -> 2.88 us
  Pallas kernels: 56 us -> 58.9 us
    ppermute x6, waiting for transfers between devices: 6.23 us -> 0.02 us  [swap(): lax.ppermute(value, axis, [(i, partner(i, count, phase)) for i in range(c...]
    all_to_all x0 -> x1, starting transfers between devices: none -> 5.25 us  [on_device(): lax.all_to_all(jnp.broadcast_to(row, (image_count, 8, lanes)), 'image', 0...]
    convert_element_type x2 -> x0, other arithmetic: 2.23 us -> none  [on_device(): backward = tables[:, 5 * bumps].astype(jnp.int32)]
    pallas_call x2, Pallas kernels: 13 us -> 14.6 us  [the longest x1 7.52 us: on_device(): pl.pallas_call(functools.partial(middle_kernel, depth_cells, width_cells)...]
    all_to_all x1, starting transfers between devices: 5.14 us -> 6.66 us  [on_device(): slabs = lax.all_to_all(partial, 'depth', 0, 0, tiled=True)]
    unnamed x12 -> x16, local copies, waits for them, and re-layouts: 1.81 us -> 3.18 us
    eq x1 -> x0, other arithmetic: 1.33 us -> none  [composite(): chooser = backward[:, :, None] == 1]
  transfers between devices with their start and end apart: 10 -> 10, of which waited for: 4 -> 2; matrix products, arithmetic and copies ran while one was open for 3% -> 3% of each run, Pallas kernels for 30% -> 30%
where the time goes in v4:
time: 115 us; the launch traced here: 114 us
  Pallas kernels  58.9 us (51%)
  starting transfers between devices  31.8 us (28%)
  waiting for transfers between devices  13.7 us (12%)
  local copies, waits for them, and re-layouts  5.19 us (5%)
  other arithmetic  2.88 us (3%)
  between operations  1.5 us (1%)
    pallas_call x1, Pallas kernels, on_device(): pl.pallas_call(functools.partial(render_kernel, depth_cells, width_cells,...  17.1 us
    pallas_call x1, Pallas kernels, on_device(): pl.pallas_call(functools.partial(inner_kernel, depth_cells, width_cells),...  13.1 us
    pallas_call x1, Pallas kernels, on_device(): pl.pallas_call(functools.partial(outer_kernel, depth_cells, width_cells),...  11.6 us
    ppermute x2, starting transfers between devices, on_device(): pieces.append(lax.ppermute(image[k], ('depth', 'image'), route))  10.7 us
    ppermute x2, waiting for transfers between devices, on_device(): pieces.append(lax.ppermute(image[k], ('depth', 'image'), route))  9.3 us
    ppermute x6, starting transfers between devices, swap(): lax.ppermute(value, axis, [(i, partner(i, count, phase)) for i in range(c...  9.24 us
    pallas_call x1, Pallas kernels, on_device(): pl.pallas_call(functools.partial(middle_kernel, depth_cells, width_cells)...  7.52 us
    pallas_call x1, Pallas kernels, on_device(): pl.pallas_call(functools.partial(edge_kernel, depth_cells, width_cells),...  7.12 us
  transfers between devices with their start and end apart: 10, of which 2 were waited for; matrix products, arithmetic and copies ran while one was open for 3% of the time, Pallas kernels for 30%

profile of v4, /device:TPU:17, one launch (start us, length us, event | category | flops | bytes accessed | tf_op | source)
XLA Modules:
  0.0 114.0 jit_solution(3571320530899505503)
XLA Ops:
  0.6 0.6 pad_add_fusion.parity_ref
  1.3 7.1 %edge.1 = (f32[19,16,16,128]{3,2,1,0:T(8,128)}, s16[10,8,16,128]{3,2,1,0:T(8,128)(2,1)}, s16[10,8,16,128]{3,2,1,0:T(8,128)(2,1)}) custom-call(s32[2]{0:T(128)} %pad_add_fusion.parity_ref, f32[19,512,128]{2,1,0:T(8,128)} %bitcast.237), custom_call_target="tpu_custom_call" | custom-call | bytes 22140000 | tf_op jit(solution)/shard_map/edge/pallas_call | solution.py:619
  8.4 0.8 collective-permute-start
  9.2 1.0 collective-permute-start.1
  10.2 7.5 %middle.1 = (f32[19,16,16,128]{3,2,1,0:T(8,128)}, s16[76,32,128]{2,1,0:T(8,128)(2,1)}, s16[76,32,128]{2,1,0:T(8,128)(2,1)}) custom-call(s32[2]{0:T(128)} %pad_add_fusion.parity_ref, f32[19,512,128]{2,1,0:T(8,128)} %bitcast.238, f32[19,16,16,128]{3,2,1,0:T(8,128)} %get-tuple-element.33.edge_hbm.e_ref.e_hbm), custom_call_target="tpu_custom_call" | custom-call | bytes 22140000 | tf_op jit(solution)/shard_map/middle/pallas_call | solution.py:634
  17.7 1.3 %collective-permute-start.2 = (s16[76,32,128]{2,1,0:T(8,128)(2,1)}, s16[76,32,128]{2,1,0:T(8,128)(2,1)S(1)}, u32[]{:S(2)}, u32[]{:S(2)}) collective-permute-start(s16[76,32,128]{2,1,0:T(8,128)(2,1)} %get-tuple-element.38), channel_id=1, source_target_pairs={{0,1},{1,0},{2,3},{3,2},{4,5},{5,4},{6,7},{7,6},{8,9},{9,8},{10,11... | collective-permute-start | bytes 1867784 | tf_op jit(solution)/shard_map/ppermute | solution.py:601
  19.0 5.3 %collective-permute-start.3 = (s16[76,32,128]{2,1,0:T(8,128)(2,1)}, s16[76,32,128]{2,1,0:T(8,128)(2,1)S(1)}, u32[]{:S(2)}, u32[]{:S(2)}) collective-permute-start(s16[76,32,128]{2,1,0:T(8,128)(2,1)} %get-tuple-element.39), channel_id=1, source_target_pairs={{0,15},{1,2},{2,1},{3,4},{4,3},{5,6},{6,5},{7,8},{8,7},{9,10},{10,... | collective-permute-start | bytes 1867784 | tf_op jit(solution)/shard_map/ppermute | solution.py:601
  25.1 0.7 copy-done.2
  25.8 0.7 copy-done.3
  26.5 2.5 %corner.1 = (f32[19,16,8,128]{3,2,1,0:T(8,128)}, s16[38,16,128]{2,1,0:T(8,128)(2,1)}, s16[38,16,128]{2,1,0:T(8,128)(2,1)}) custom-call(s32[2]{0:T(128)} %pad_add_fusion.parity_ref, s16[10,8,16,128]{3,2,1,0:T(8,128)(2,1)} %copy-done.2, s16[10,8,16,128]{3,2,1,0:T(8,128)(2,1)} %copy-done.3), custom_call_target="tpu_custom_call" | custom-call | bytes 7380000 | tf_op jit(solution)/shard_map/corner/pallas_call | solution.py:655
  29.0 0.9 collective-permute-start.5
  30.0 13.1 %inner.1 = (f32[19,512,128]{2,1,0:T(8,128)}, f32[3,16,56,128]{3,2,1,0:T(8,128)}, f32[512,128]{1,0:T(8,128)}, f32[19,4,56,128]{3,2,1,0:T(8,128)}, f32[19,4,56,128]{3,2,1,0:T(8,128)}, /*index=5*/f32[19,4,56,128]{3,2,1,0:T(8,128)}) custom-call(f32[19,16,16,128]{3,2,1,0:T(8,128)} %get-tuple-element.33.edge_hbm.e_ref.e_hbm, ...), custom_call_target="tpu_custom_call" | custom-call | bytes 44280000 | tf_op jit(solution)/shard_map/inner/pallas_call | solution.py:671
  43.1 0.6 broadcast_in_dim.110
  43.7 5.2 %all-to-all-start = ((f32[16,8,128]{2,1,0:T(8,128)}), f32[16,8,128]{2,1,0:T(8,128)S(1)}, u32[]{:S(2)}, u32[]{:S(2)}) async-start(f32[16,8,128]{2,1,0:T(8,128)} %broadcast_in_dim.110), calls=%async_computation | async-start | bytes 131072 | tf_op jit(solution)/shard_map/all_to_all | solution.py:695
  50.1 11.6 %outer.1 = (f32[19,512,128]{2,1,0:T(8,128)}, bf16[512,128]{1,0:T(8,128)(2,1)}) custom-call(s32[2]{0:T(128)} %pad_add_fusion.parity_ref, f32[19,16,16,128]{3,2,1,0:T(8,128)} %get-tuple-element.33.edge_hbm.e_ref.e_hbm, f32[19,16,16,128]{3,2,1,0:T(8,128)} %get-tuple-element.34.r_ref.r_hbm, f32[19,16,8,128]{3,2,1,0:T(8,128)} %get-tuple-element.37.h_ref, ...), custom_call_target="tpu_custom_call" | custom-call | bytes 44280000 | tf_op jit(solution)/shard_map/outer/pallas_call | solution.py:698
  62.4 17.1 %render.1 = f32[8,2,4,16,128]{4,3,2,1,0:T(8,128)} custom-call(s32[1]{0:T(128)} %bitcast.1.pick_ref, f32[16,8,128]{2,1,0:T(8,128)} %copy-done.4, bf16[512,128]{1,0:T(8,128)(2,1)} %get-tuple-element.49.vort_ref), custom_call_target="tpu_custom_call" | custom-call | bytes 66420000 | tf_op jit(solution)/shard_map/render/pallas_call | solution.py:722
  79.5 6.7 %all-to-all-start.1 = ((f32[8,2,4,16,128]{4,3,2,1,0:T(8,128)}), f32[8,2,4,16,128]{4,3,2,1,0:T(8,128)S(1)}, u32[]{:S(2)}, u32[]{:S(2)}) async-start(f32[8,2,4,16,128]{4,3,2,1,0:T(8,128)} %render.1), calls=%async_computation.1 | async-start | bytes 1048576 | tf_op jit(solution)/shard_map/all_to_all | solution.py:735
  86.2 1.3 %constant_dynamic-slice_fusion.1 = (f32[1,1,1]{2,1,0:T(1,128)}, f32[1,1,1]{2,1,0:T(1,128)}) fusion(f32[16,8,128]{2,1,0:T(8,128)} %copy-done.4, s32[]{:T(128)S(6)} %select_n.447, s32[]{:T(128)S(6)} %select_n.449), kind=kLoop, calls=%fused_computation.54 | loop fusion | bytes 24 | tf_op jit(solution)/shard_map/dynamic_slice | solution.py:736
  87.4 1.2 %maximum_compare_fusion = pred[2]{0:T(512)(128)(4,1)S(1)} fusion(f32[1]{0:T(128)} %bitcast.7, f32[1]{0:T(128)} %bitcast.6), kind=kLoop, calls=%fused_computation.63 | loop fusion | flops 4 | bytes 10 | tf_op jit(solution)/shard_map/gt | solution.py:575
  88.6 4.4 %all-to-all-done.1 = f32[8,2,4,16,128]{4,3,2,1,0:T(8,128)S(1)} async-done(((f32[8,2,4,16,128]{4,3,2,1,0:T(8,128)}), f32[8,2,4,16,128]{4,3,2,1,0:T(8,128)S(1)}, u32[]{:S(2)}, u32[]{:S(2)}) %all-to-all-start.1) | async-done | bytes 524320 | tf_op jit(solution)/shard_map/all_to_all | solution.py:735
  93.4 8.5 %collective-permute-start.6 = (f32[4,16,128]{2,1,0:T(8,128)S(1)}, f32[4,16,128]{2,1,0:T(8,128)S(1)}, u32[]{:S(2)}, u32[]{:S(2)}) collective-permute-start(f32[4,16,128]{2,1,0:T(8,128)S(1)} %get-tuple-element.63), channel_id=1, source_target_pairs={{0,1},{1,0},{2,17},{3,16},{4,33},{5,32},{6,49},{7,48},{8,65},{9,64... | collective-permute-start | bytes 98312 | tf_op jit(solution)/shard_map/ppermute | solution.py:744
  101.8 2.2 %collective-permute-start.7 = (f32[4,16,128]{2,1,0:T(8,128)S(1)}, f32[4,16,128]{2,1,0:T(8,128)S(1)}, u32[]{:S(2)}, u32[]{:S(2)}) collective-permute-start(f32[4,16,128]{2,1,0:T(8,128)S(1)} %get-tuple-element.64), channel_id=1, source_target_pairs={{0,0},{1,1},{2,16},{3,17},{4,32},{5,33},{6,48},{7,49},{8,64},{9,65... | collective-permute-start | bytes 98312 | tf_op jit(solution)/shard_map/ppermute | solution.py:744
  104.1 9.3 %collective-permute-done.7 = f32[4,16,128]{2,1,0:T(8,128)S(1)} collective-permute-done((f32[4,16,128]{2,1,0:T(8,128)S(1)}, f32[4,16,128]{2,1,0:T(8,128)S(1)}, u32[]{:S(2)}, u32[]{:S(2)}) %collective-permute-start.7) | collective-permute-done | bytes 32800 | tf_op jit(solution)/shard_map/ppermute | solution.py:744
  113.4 0.6 maximum_bitcast_fusion
  (35 shorter events, 2.3 us)
Async XLA Ops:
  8.4 16.6 %collective-permute-start = (s16[10,8,16,128]{3,2,1,0:T(8,128)(2,1)}, s16[10,8,16,128]{3,2,1,0:T(8,128)(2,1)S(1)}, u32[]{:S(2)}, u32[]{:S(2)}) collective-permute-start(s16[10,8,16,128]{3,2,1,0:T(8,128)(2,1)} %get-tuple-element.35), channel_id=1, source_target_pairs={{0,16},{16,0},{32,48},{48,32},{64,80},{80,64},{96,112},{112,96},{1... | collective-permute-start | bytes 983048 | tf_op jit(solution)/shard_map/ppermute | solution.py:601
  9.2 15.9 %collective-permute-start.1 = (s16[10,8,16,128]{3,2,1,0:T(8,128)(2,1)}, s16[10,8,16,128]{3,2,1,0:T(8,128)(2,1)S(1)}, u32[]{:S(2)}, u32[]{:S(2)}) collective-permute-start(s16[10,8,16,128]{3,2,1,0:T(8,128)(2,1)} %get-tuple-element.36), channel_id=1, source_target_pairs={{0,112},{16,32},{32,16},{48,64},{64,48},{80,96},{96,80},{112,0},{1... | collective-permute-start | bytes 983048 | tf_op jit(solution)/shard_map/ppermute | solution.py:601
  10.2 14.1 %copy-start.7 = (f32[1,5,8]{2,0,1:T(1,128)S(1)}, f32[1,5,8]{2,0,1:T(1,128)}, u32[]{:S(2)}) copy-start(f32[1,5,8]{2,0,1:T(1,128)} %param.6) | copy-start | bytes 484
  17.7 31.3 %collective-permute-start.2 = (s16[76,32,128]{2,1,0:T(8,128)(2,1)}, s16[76,32,128]{2,1,0:T(8,128)(2,1)S(1)}, u32[]{:S(2)}, u32[]{:S(2)}) collective-permute-start(s16[76,32,128]{2,1,0:T(8,128)(2,1)} %get-tuple-element.38), channel_id=1, source_target_pairs={{0,1},{1,0},{2,3},{3,2},{4,5},{5,4},{6,7},{7,6},{8,9},{9,8},{10,11... | collective-permute-start | bytes 1867784 | tf_op jit(solution)/shard_map/ppermute | solution.py:601
  19.0 30.1 %collective-permute-start.3 = (s16[76,32,128]{2,1,0:T(8,128)(2,1)}, s16[76,32,128]{2,1,0:T(8,128)(2,1)S(1)}, u32[]{:S(2)}, u32[]{:S(2)}) collective-permute-start(s16[76,32,128]{2,1,0:T(8,128)(2,1)} %get-tuple-element.39), channel_id=1, source_target_pairs={{0,15},{1,2},{2,1},{3,4},{4,3},{5,6},{6,5},{7,8},{8,7},{9,10},{10,... | collective-permute-start | bytes 1867784 | tf_op jit(solution)/shard_map/ppermute | solution.py:601
  25.1 0.7 copy-start.2
  25.8 0.7 copy-start.3
  29.0 20.0 %collective-permute-start.4 = (s16[38,16,128]{2,1,0:T(8,128)(2,1)}, s16[38,16,128]{2,1,0:T(8,128)(2,1)S(1)}, u32[]{:S(2)}, u32[]{:S(2)}) collective-permute-start(s16[38,16,128]{2,1,0:T(8,128)(2,1)} %get-tuple-element.40), channel_id=1, source_target_pairs={{0,1},{1,0},{2,3},{3,2},{4,5},{5,4},{6,7},{7,6},{8,9},{9,8},{10,11... | collective-permute-start | bytes 466952 | tf_op jit(solution)/shard_map/ppermute | solution.py:601
  29.0 20.0 %collective-permute-start.5 = (s16[38,16,128]{2,1,0:T(8,128)(2,1)}, s16[38,16,128]{2,1,0:T(8,128)(2,1)S(1)}, u32[]{:S(2)}, u32[]{:S(2)}) collective-permute-start(s16[38,16,128]{2,1,0:T(8,128)(2,1)} %get-tuple-element.41), channel_id=1, source_target_pairs={{0,15},{1,2},{2,1},{3,4},{4,3},{5,6},{6,5},{7,8},{8,7},{9,10},{10,... | collective-permute-start | bytes 466952 | tf_op jit(solution)/shard_map/ppermute | solution.py:601
  43.7 18.1 %all-to-all-start = ((f32[16,8,128]{2,1,0:T(8,128)}), f32[16,8,128]{2,1,0:T(8,128)S(1)}, u32[]{:S(2)}, u32[]{:S(2)}) async-start(f32[16,8,128]{2,1,0:T(8,128)} %broadcast_in_dim.110), calls=%async_computation | async-start | bytes 131072 | tf_op jit(solution)/shard_map/all_to_all | solution.py:695
  49.0 0.7 copy-start.5
  49.0 0.7 copy-start.6
  49.0 0.9 copy-start
  49.0 1.1 copy-start.1
  61.8 0.6 copy-start.4
  79.5 13.5 %all-to-all-start.1 = ((f32[8,2,4,16,128]{4,3,2,1,0:T(8,128)}), f32[8,2,4,16,128]{4,3,2,1,0:T(8,128)S(1)}, u32[]{:S(2)}, u32[]{:S(2)}) async-start(f32[8,2,4,16,128]{4,3,2,1,0:T(8,128)} %render.1), calls=%async_computation.1 | async-start | bytes 1048576 | tf_op jit(solution)/shard_map/all_to_all | solution.py:735
  93.4 10.7 %collective-permute-start.6 = (f32[4,16,128]{2,1,0:T(8,128)S(1)}, f32[4,16,128]{2,1,0:T(8,128)S(1)}, u32[]{:S(2)}, u32[]{:S(2)}) collective-permute-start(f32[4,16,128]{2,1,0:T(8,128)S(1)} %get-tuple-element.63), channel_id=1, source_target_pairs={{0,1},{1,0},{2,17},{3,16},{4,33},{5,32},{6,49},{7,48},{8,65},{9,64... | collective-permute-start | bytes 98312 | tf_op jit(solution)/shard_map/ppermute | solution.py:744
  101.8 11.5 %collective-permute-start.7 = (f32[4,16,128]{2,1,0:T(8,128)S(1)}, f32[4,16,128]{2,1,0:T(8,128)S(1)}, u32[]{:S(2)}, u32[]{:S(2)}) collective-permute-start(f32[4,16,128]{2,1,0:T(8,128)S(1)} %get-tuple-element.64), channel_id=1, source_target_pairs={{0,0},{1,1},{2,16},{3,17},{4,32},{5,33},{6,48},{7,49},{8,64},{9,65... | collective-permute-start | bytes 98312 | tf_op jit(solution)/shard_map/ppermute | solution.py:744

commit v5 on v4

--- a/solution.py
+++ b/solution.py
@@ -126,7 +126,7 @@
             r_ref[p, y, to_row : to_row + 8, :] = value if cz == 0 else pltpu.roll(value, cz % 128, 1)
         return carry
 
-    lax.fori_loop(0, width_cells, at_y, 0, unroll=2)
+    lax.fori_loop(0, width_cells, at_y, 0, unroll=8)
 
 
 def edge_kernel(depth_cells, width_cells, parity_ref, f_hbm, r_hbm, da_ref, db_ref, f_ref, r_ref, in_sems, out_sem):
@@ -168,7 +168,7 @@
             db_ref[number, t] = pack_code(*db)
         return carry
 
-    lax.fori_loop(0, width_cells // 2, face_x, 0)
+    lax.fori_loop(0, width_cells // 2, face_x, 0, unroll=2)
     keep_r.wait()
 
 
@@ -339,7 +339,7 @@
 
 
 def inner_kernel(
-    depth_cells, width_cells, e_ref, r_ref, h_ref, final_ref, flow_ref, spin_ref, s2_hbm, s3_hbm, s4_hbm, sa_ref, sb_ref, sems
+    depth_cells, width_cells, e_hbm, r_hbm, h_ref, sa_ref, sb_ref, final_ref, flow_ref, plain_ref, e_ref, r_ref, sems
 ):
     tiles = depth_cells // 8
     rows = row_index()
@@ -348,77 +348,61 @@
         for p in range(Q):
             pieces = [r_ref[p, y, 8 * t : 8 * t + 8, :] for t in range(tiles - 2)]
             pieces = [e_ref[p, y, 0:8, :]] + pieces + [e_ref[p, y, 8:16, :]]
-            put_streamed(sa_ref, p, y, pieces, decode(h_ref[p, y], p), rows)
-        return carry
-
-    lax.fori_loop(0, width_cells, own, 0)
-
-    def hand_on(source, target, step):
-        low, high = (step, width_cells - 2 - step)
-        copies = [
-            pltpu.make_async_copy(source.at[:, pl.ds(low, 2)], target.at[:, pl.ds(0, 2)], sems.at[step - 1, 0]),
-            pltpu.make_async_copy(source.at[:, pl.ds(high, 2)], target.at[:, pl.ds(2, 2)], sems.at[step - 1, 1]),
-        ]
-        for copy in copies:
-            copy.start()
-        return copies
+            put_streamed(sa_ref, p, y + HALO, pieces, decode(h_ref[p, y], p), rows)
+        return carry
+
+    parts = 4
+    count = width_cells // parts
+    loads = []
+    for part in range(parts):
+        at = pl.ds(part * count, count)
+        loads.append(
+            [
+                pltpu.make_async_copy(e_hbm.at[:, at], e_ref.at[:, at], sems.at[part, 0]),
+                pltpu.make_async_copy(r_hbm.at[:, at], r_ref.at[:, at], sems.at[part, 1]),
+            ]
+        )
+        for load in loads[-1]:
+            load.start()
+    for part in range(parts):
+        for load in loads[part]:
+            load.wait()
+        lax.fori_loop(part * count, (part + 1) * count, own, 0)
 
     def stage(source, target, step, shift):
         def pair(k, carry):
-            step_row(source, target, step + 2 * k, tiles + 1, shift)
-            step_row(source, target, step + 2 * k + 1, tiles + 1, shift)
+            step_row(source, target, HALO + step + 2 * k, tiles + 1, shift)
+            step_row(source, target, HALO + step + 2 * k + 1, tiles + 1, shift)
             return carry
 
         lax.fori_loop(0, (width_cells - 2 * step) // 2, pair, 0)
 
     stage(sa_ref, sb_ref, 1, 0)
-    kept2 = hand_on(sb_ref, s2_hbm, 1)
     stage(sb_ref, sa_ref, 2, 0)
-    kept3 = hand_on(sa_ref, s3_hbm, 2)
-    for copy in kept2:
-        copy.wait()
     stage(sa_ref, sb_ref, 3, 4)
-    kept4 = hand_on(sb_ref, s4_hbm, 3)
 
     def last(y, carry):
         flow_row(sb_ref, flow_ref, y, tiles)
-        final_row(sb_ref, final_ref, y, 0, tiles, width_cells)
-        return carry
-
-    lax.fori_loop(STEPS, width_cells - STEPS, last, 0)
+        final_row(sb_ref, final_ref, y, HALO, tiles, width_cells)
+        return carry
+
+    lax.fori_loop(HALO + STEPS, HALO + width_cells - STEPS, last, 0, unroll=2)
 
     def spins(y, carry):
-        spin_row(flow_ref, spin_ref, y, 0, tiles, width_cells)
-        return carry
-
-    lax.fori_loop(HALO, width_cells - HALO, spins, 0, unroll=2)
-    for copy in kept3 + kept4:
-        copy.wait()
+        spin_row(flow_ref, plain_ref, y, HALO, tiles, width_cells)
+        return carry
+
+    lax.fori_loop(2 * HALO, width_cells, spins, 0, unroll=2)
 
 
 def outer_kernel(
-    depth_cells, width_cells, parity_ref, e_hbm, r_hbm, h_ref, ya_ref, yb_ref, ca_ref, cb_ref,
-    final_in, flow_in, spin_in, s2_in, s3_in, s4_in, out_hbm, vort_ref,
-    e_ref, r_ref, sa_ref, sb_ref, flow_ref, out_ref, plain_ref, sems,
+    depth_cells, width_cells, parity_ref, ya_ref, yb_ref, ca_ref, cb_ref,
+    sa_in, sb_in, final_in, flow_in, plain_in,
+    out_hbm, vort_ref, sa_ref, sb_ref, out_ref, flow_ref, plain_ref, out_sem,
 ):
     tiles = depth_cells // 8
     rows = row_index()
     odd_image = jnp.full((8, 128), parity_ref[1], jnp.int32) == 1
-
-    moves = []
-    for source, target in ((e_hbm, e_ref), (r_hbm, r_ref)):
-        moves.append((source.at[:, pl.ds(0, 2)], target.at[:, pl.ds(0, 2)]))
-        moves.append((source.at[:, pl.ds(width_cells - 2, 2)], target.at[:, pl.ds(2, 2)]))
-    for step, source, target in ((1, s2_in, sb_ref), (2, s3_in, sa_ref), (3, s4_in, sb_ref)):
-        moves.append((source.at[:, pl.ds(0, 2)], target.at[:, pl.ds(HALO + step, 2)]))
-        moves.append((source.at[:, pl.ds(2, 2)], target.at[:, pl.ds(HALO + width_cells - 2 - step, 2)]))
-    inner = pl.ds(STEPS, width_cells - 2 * STEPS)
-    moves.append((flow_in.at[:, inner], flow_ref.at[:, pl.ds(HALO + STEPS, width_cells - 2 * STEPS)]))
-    moves.append((final_in, out_ref))
-    moves.append((spin_in, plain_ref))
-    copies = [pltpu.make_async_copy(a, b, sems.at[k]) for k, (a, b) in enumerate(moves)]
-    for copy in copies:
-        copy.start()
 
     low_face = face_list(0, 1)
     high_face = face_list(width_cells - 1, -1)
@@ -441,14 +425,6 @@
             put_streamed(sa_ref, ph, yh - width_cells + HALO, low[1:], low[0], rows)
             put_streamed(sa_ref, pl_, yl + width_cells + HALO, high[1:], high[0], rows)
 
-    for copy in copies[:4]:
-        copy.wait()
-    for k, y in enumerate((0, 1, width_cells - 2, width_cells - 1)):
-        for p in range(Q):
-            pieces = [r_ref[p, k, 8 * t : 8 * t + 8, :] for t in range(tiles - 2)]
-            pieces = [e_ref[p, k, 0:8, :]] + pieces + [e_ref[p, k, 8:16, :]]
-            put_streamed(sa_ref, p, y + HALO, pieces, decode(h_ref[p, y], p), rows)
-
     def stage(source, target, step, shift):
         reach = HALO - step
 
@@ -460,14 +436,8 @@
         lax.fori_loop(0, HALO, both, 0)
 
     stage(sa_ref, sb_ref, 1, 0)
-    for copy in copies[4:6]:
-        copy.wait()
     stage(sb_ref, sa_ref, 2, 0)
-    for copy in copies[6:8]:
-        copy.wait()
     stage(sa_ref, sb_ref, 3, 4)
-    for copy in copies[8:13]:
-        copy.wait()
 
     def finish(k, carry):
         final_row(sb_ref, out_ref, HALO + k, HALO, tiles, width_cells)
@@ -475,7 +445,7 @@
         return carry
 
     lax.fori_loop(0, STEPS, finish, 0)
-    keep_out = pltpu.make_async_copy(out_ref, out_hbm, sems.at[13])
+    keep_out = pltpu.make_async_copy(out_ref, out_hbm, out_sem)
     keep_out.start()
 
     def flows(k, carry):
@@ -519,7 +489,7 @@
 BLOCK = 4
 
 
-def render_kernel(depth_cells, width_cells, groups, bumps, pick_ref, table_ref, vort_ref, image_ref, place_ref, fade_ref):
+def render_kernel(depth_cells, width_cells, functions, bumps, table_ref, vort_ref, image_ref, place_ref, fade_ref):
     def prepare(x, carry):
         at = pl.ds(pl.multiple_of(x * width_cells, width_cells), width_cells)
         value = vort_ref[at, :].astype(jnp.float32)
@@ -533,10 +503,7 @@
 
     lax.fori_loop(0, depth_cells, prepare, 0)
 
-    def one(number, carry):
-        group = number // 2
-        slot = number % 2
-        m = 2 * group + (pick_ref[0] + slot) % 2
+    def one(m, carry):
         order = jnp.where(table_ref[m, 0, 5 * bumps] > 0.5, 1, 0)
 
         def cells(block, state):
@@ -562,35 +529,38 @@
 
         zero = jnp.zeros((width_cells, 128), jnp.float32)
         clear, red, green, blue = lax.fori_loop(0, depth_cells // BLOCK, cells, (zero + 1.0, zero, zero, zero))
-        image_ref[group, slot, 0] = red
-        image_ref[group, slot, 1] = green
-        image_ref[group, slot, 2] = blue
-        image_ref[group, slot, 3] = clear
-        return carry
-
-    lax.fori_loop(0, 2 * groups, one, 0)
+        image_ref[m, 0] = red
+        image_ref[m, 1] = green
+        image_ref[m, 2] = blue
+        image_ref[m, 3] = clear
+        return carry
+
+    lax.fori_loop(0, functions, one, 0)
 
 
 def composite(slabs, backward):
-    chooser = backward[:, :, None] > 0.5
     count = slabs.shape[0]
     clear = 1.0
     color = [0.0] * 3
     for step in range(count):
-        piece = [jnp.where(chooser, slabs[count - 1 - step, :, c], slabs[step, :, c]) for c in range(4)]
+        piece = [jnp.where(backward, slabs[count - 1 - step, :, c], slabs[step, :, c]) for c in range(4)]
         color = [color[c] + clear * piece[c] for c in range(3)]
         clear = clear * piece[3]
-    return jnp.stack(color + [1.0 - clear], axis=1)
-
-
-ANY = pl.BlockSpec(memory_space=pl.ANY)
+    return jnp.stack(color + [1.0 - clear])
+
+
+HBM = pl.BlockSpec(memory_space=pltpu.HBM)
 VMEM = pl.BlockSpec(memory_space=pltpu.VMEM)
 SMEM = pl.BlockSpec(memory_space=pltpu.SMEM)
-GRANT = pltpu.CompilerParams(vmem_limit_bytes=58 * 1024 * 1024)
+GRANT = pltpu.CompilerParams(vmem_limit_bytes=14 * 1024 * 1024)
 
 
 def cost(microseconds):
     return pl.CostEstimate(flops=0, bytes_accessed=int(microseconds * 3.69e6), transcendentals=0)
+
+
+def in_hbm(value):
+    return pltpu.with_memory_space_constraint(value, pltpu.HBM)
 
 
 def partner(index, count, phase):
@@ -615,12 +585,12 @@
     y_shape = jax.ShapeDtypeStruct((faces, depth_cells, lanes), i16)
     c_shape = jax.ShapeDtypeStruct((faces // 2, 16, lanes), i16)
     half = (depth_cells - 16, 16)
-    field = populations.reshape(Q, cells, lanes)
+    field = pltpu.with_memory_space_constraint(populations.reshape(Q, cells, lanes), pltpu.HBM)
     edge, da, db = pl.pallas_call(
         functools.partial(edge_kernel, depth_cells, width_cells),
-        out_shape=(jax.ShapeDtypeStruct((Q, width_cells, half[1], lanes), f32), x_shape, x_shape),
-        in_specs=[SMEM, ANY],
-        out_specs=(ANY, VMEM, VMEM),
+        out_shape=(pltpu.HBM((Q, width_cells, half[1], lanes), f32), x_shape, x_shape),
+        in_specs=[SMEM, HBM],
+        out_specs=(HBM, VMEM, VMEM),
         scratch_shapes=[
             pltpu.VMEM((Q, half[1] * width_cells, lanes), f32),
             pltpu.VMEM((Q, width_cells, half[1], lanes), f32),
@@ -633,9 +603,9 @@
     )(parity, field)
     middle, ia, ib = pl.pallas_call(
         functools.partial(middle_kernel, depth_cells, width_cells),
-        out_shape=(jax.ShapeDtypeStruct((Q, width_cells, half[0], lanes), f32), y_shape, y_shape),
-        in_specs=[SMEM, ANY, ANY],
-        out_specs=(ANY, VMEM, VMEM),
+        out_shape=(pltpu.HBM((Q, width_cells, half[0], lanes), f32), y_shape, y_shape),
+        in_specs=[SMEM, HBM, HBM],
+        out_specs=(HBM, VMEM, VMEM),
         scratch_shapes=[
             pltpu.VMEM((Q, half[0] * width_cells, lanes), f32),
             pltpu.VMEM((Q, width_cells, half[0], lanes), f32),
@@ -646,7 +616,7 @@
         compiler_params=GRANT,
         cost_estimate=cost(6),
         name="middle",
-    )(parity, field, edge)
+    )(parity, field, in_hbm(edge))
 
     xa = swap(da, "depth", depth_count, 0)
     xb = swap(db, "depth", depth_count, 1)
@@ -667,85 +637,81 @@
 
     depth_rows = depth_cells + 8 + 2 * PAD
     width_rows = width_cells + 2 * HALO
-    side = jax.ShapeDtypeStruct((Q, 4, depth_rows, lanes), f32)
-    inner_final, inner_flow, inner_spin, s2, s3, s4 = pl.pallas_call(
+    stages = (
+        pltpu.VMEM((Q, width_rows, depth_rows, lanes), f32),
+        pltpu.VMEM((Q, width_rows, depth_rows, lanes), f32),
+        pltpu.VMEM((Q, cells, lanes), f32),
+        pltpu.VMEM((3, width_rows, depth_rows, lanes), f32),
+        pltpu.VMEM((cells, lanes), f32),
+    )
+    state = pl.pallas_call(
         functools.partial(inner_kernel, depth_cells, width_cells),
-        out_shape=(
-            jax.ShapeDtypeStruct((Q, cells, lanes), f32),
-            jax.ShapeDtypeStruct((3, width_cells, depth_rows, lanes), f32),
-            jax.ShapeDtypeStruct((cells, lanes), f32),
-            side, side, side,
-        ),
-        in_specs=[VMEM] * 3,
-        out_specs=(VMEM, VMEM, VMEM, ANY, ANY, ANY),
+        out_shape=stages,
+        in_specs=[HBM, HBM, VMEM],
+        out_specs=(VMEM,) * 5,
         scratch_shapes=[
-            pltpu.VMEM((Q, width_cells, depth_rows, lanes), f32),
-            pltpu.VMEM((Q, width_cells, depth_rows, lanes), f32),
-            pltpu.SemaphoreType.DMA((3, 2)),
+            pltpu.VMEM((Q, width_cells, half[1], lanes), f32),
+            pltpu.VMEM((Q, width_cells, half[0], lanes), f32),
+            pltpu.SemaphoreType.DMA((4, 2)),
         ],
         compiler_params=GRANT,
         cost_estimate=cost(12),
         name="inner",
-    )(edge, middle, halo)
+    )(in_hbm(edge), in_hbm(middle), halo)
 
     bumps = transfer.shape[2]
     row = jnp.concatenate([bump_tables(transfer, ray_cells).reshape(-1), direction.astype(f32)])
     row = jnp.pad(row, (0, lanes - row.shape[0]))
-    row, _ = lax.optimization_barrier((row, inner_spin))
+    row, _ = lax.optimization_barrier((row, halo))
     tables = lax.all_to_all(
         jnp.broadcast_to(row, (image_count, 8, lanes)), "image", 0, 0, tiled=True
     )
-    final, vorticity = pl.pallas_call(
+    final, vorticity, *_ = pl.pallas_call(
         functools.partial(outer_kernel, depth_cells, width_cells),
         out_shape=(
             jax.ShapeDtypeStruct((Q, cells, lanes), f32),
             jax.ShapeDtypeStruct((cells, lanes), jnp.bfloat16),
+            *stages,
         ),
-        in_specs=[SMEM, ANY, ANY] + [VMEM] * 5 + [ANY] * 6,
-        out_specs=(ANY, VMEM),
-        scratch_shapes=[
-            pltpu.VMEM((Q, 4, half[1], lanes), f32),
-            pltpu.VMEM((Q, 4, half[0], lanes), f32),
-            pltpu.VMEM((Q, width_rows, depth_rows, lanes), f32),
-            pltpu.VMEM((Q, width_rows, depth_rows, lanes), f32),
-            pltpu.VMEM((3, width_rows, depth_rows, lanes), f32),
-            pltpu.VMEM((Q, cells, lanes), f32),
-            pltpu.VMEM((cells, lanes), f32),
-            pltpu.SemaphoreType.DMA((14,)),
-        ],
+        in_specs=[SMEM] + [VMEM] * 9,
+        out_specs=(HBM,) + (VMEM,) * 6,
+        scratch_shapes=[pltpu.SemaphoreType.DMA],
+        input_output_aliases={5 + k: 2 + k for k in range(5)},
         compiler_params=GRANT,
         cost_estimate=cost(12),
         name="outer",
-    )(parity, edge, middle, halo, ya, yb, ca, cb, inner_final, inner_flow, inner_spin, s2, s3, s4)
-
-    groups = depth_count
+    )(parity, ya, yb, ca, cb, *state)
+
+    functions = image_count
     partial = pl.pallas_call(
-        functools.partial(render_kernel, depth_cells, width_cells, groups, bumps),
-        out_shape=jax.ShapeDtypeStruct((groups, 2, 4, width_cells, lanes), f32),
-        in_specs=[SMEM, SMEM, VMEM],
+        functools.partial(render_kernel, depth_cells, width_cells, functions, bumps),
+        out_shape=jax.ShapeDtypeStruct((functions, 4, width_cells, lanes), f32),
+        in_specs=[SMEM, VMEM],
         out_specs=VMEM,
         scratch_shapes=[
             pltpu.VMEM((2, depth_cells, width_cells, lanes), f32),
             pltpu.VMEM((2, depth_cells, width_cells, lanes), f32),
         ],
         compiler_params=GRANT,
-        cost_estimate=cost(18),
+        cost_estimate=cost(16),
         name="render",
-    )((i % 2).astype(jnp.int32)[None], tables, vorticity)
-    slabs = lax.all_to_all(partial, "depth", 0, 0, tiled=True)
-    mine = jnp.stack([tables[2 * d + (i + k) % 2, 0, 5 * bumps] for k in range(2)])
-    image = composite(slabs, mine[:, None])
-    pieces = []
-    for k in range(2):
-        route = []
-        for sd in range(depth_count):
-            for si in range(image_count):
-                route.append((sd * image_count + si, (si // 2) * image_count + 2 * sd + (si + k) % 2))
-        pieces.append(lax.ppermute(image[k], ("depth", "image"), route))
-    flip = (i % 2) == 1
-    top = jnp.where(flip, pieces[1], pieces[0])
-    bottom = jnp.where(flip, pieces[0], pieces[1])
-    images = jnp.concatenate([top, bottom], axis=1)[None]
+    )(tables, vorticity)
+    halves = image_count // depth_count
+    groups = [
+        [sd * image_count + halves * row + side for sd in range(depth_count) for side in range(halves)]
+        for row in range(depth_count)
+    ]
+    slabs = lax.all_to_all(
+        partial, ("depth", "image"), 0, 0, axis_index_groups=groups, tiled=True
+    ).reshape(depth_count, halves, 4, width_cells, lanes)
+    image = composite(slabs, tables[halves * d + i % halves, 0, 5 * bumps] > 0.5)
+    route = [
+        (sd * image_count + si, (si // halves) * image_count + halves * sd + si % halves)
+        for sd in range(depth_count)
+        for si in range(image_count)
+    ]
+    images = lax.ppermute(image, ("depth", "image"), route)
+    images = images.reshape(1, 4, halves * width_cells, lanes)
     return (
         final.reshape(populations.shape),
         vorticity.reshape(depth_cells, width_cells, lanes),

time: 115 us -> 100 us (0.87)
  Pallas kernels: 58.9 us -> 49.3 us
  waiting for transfers between devices: 13.7 us -> 11 us
  starting transfers between devices: 31.8 us -> 30 us
    ppermute x2 -> x1, waiting for transfers between devices: 9.3 us -> 3.3 us  [on_device(): images = lax.ppermute(image, ('depth', 'image'), route)]
    pallas_call x1, Pallas kernels: 13.1 us -> 9.56 us  [on_device(): pl.pallas_call(functools.partial(inner_kernel, depth_cells, width_cells),...]
    all_to_all x1, waiting for transfers between devices: 4.41 us -> 7.7 us  [on_device(): lax.all_to_all(partial, ('depth', 'image'), 0, 0, axis_index_groups=group...]
    pallas_call x1, Pallas kernels: 7.12 us -> 5.02 us  [on_device(): pl.pallas_call(functools.partial(edge_kernel, depth_cells, width_cells),...]
    ppermute x2 -> x1, starting transfers between devices: 10.7 us -> 8.86 us  [on_device(): images = lax.ppermute(image, ('depth', 'image'), route)]
    add x3, other arithmetic: 0.28 us -> 2.02 us  [composite(): color = [color[c] + clear * piece[c] for c in range(3)]]
    pallas_call x1, Pallas kernels: 7.52 us -> 6.1 us  [on_device(): pl.pallas_call(functools.partial(middle_kernel, depth_cells, width_cells)...]
    pallas_call x1, Pallas kernels: 11.6 us -> 10.2 us  [on_device(): pl.pallas_call(functools.partial(outer_kernel, depth_cells, width_cells),...]
  transfers between devices with their start and end apart: 10 -> 9, of which waited for: 2 -> 2; matrix products, arithmetic and copies ran while one was open for 3% -> 1% of each run, Pallas kernels for 30% -> 28%
where the time goes in v5:
time: 100 us; the launch traced here: 99.1 us
  Pallas kernels  49.3 us (49%)
  starting transfers between devices  30 us (30%)
  waiting for transfers between devices  11 us (11%)
  local copies, waits for them, and re-layouts  4.58 us (5%)
  other arithmetic  2.81 us (3%)
  between operations  1.46 us (1%)
    pallas_call x1, Pallas kernels, on_device(): pl.pallas_call(functools.partial(render_kernel, depth_cells, width_cells,...  16.8 us
    pallas_call x1, Pallas kernels, on_device(): pl.pallas_call(functools.partial(outer_kernel, depth_cells, width_cells),...  10.2 us
    pallas_call x1, Pallas kernels, on_device(): pl.pallas_call(functools.partial(inner_kernel, depth_cells, width_cells),...  9.56 us
    ppermute x6, starting transfers between devices, swap(): lax.ppermute(value, axis, [(i, partner(i, count, phase)) for i in range(c...  9.24 us
    ppermute x1, starting transfers between devices, on_device(): images = lax.ppermute(image, ('depth', 'image'), route)  8.86 us
    all_to_all x1, waiting for transfers between devices, on_device(): lax.all_to_all(partial, ('depth', 'image'), 0, 0, axis_index_groups=group...  7.7 us
    all_to_all x1, starting transfers between devices, on_device(): lax.all_to_all(partial, ('depth', 'image'), 0, 0, axis_index_groups=group...  6.65 us
    pallas_call x1, Pallas kernels, on_device(): pl.pallas_call(functools.partial(middle_kernel, depth_cells, width_cells)...  6.1 us
  transfers between devices with their start and end apart: 9, of which 2 were waited for; matrix products, arithmetic and copies ran while one was open for 1% of the time, Pallas kernels for 28%

profile of v5, /device:TPU:17, one launch (start us, length us, event | category | flops | bytes accessed | tf_op | source)
XLA Modules:
  0.0 99.1 jit_solution(6239887669040138412)
XLA Ops:
  0.7 5.0 %edge.1 = (f32[19,16,16,128]{3,2,1,0:T(8,128)}, s16[10,8,16,128]{3,2,1,0:T(8,128)(2,1)S(1)}, s16[10,8,16,128]{3,2,1,0:T(8,128)(2,1)S(1)}) custom-call(s32[2]{0:T(128)S(1)} %pad_add_fusion.parity_ref, f32[19,512,128]{2,1,0:T(8,128)} %bitcast.215), custom_call_target="tpu_custom_call" | custom-call | bytes 22140000 | tf_op jit(solution)/shard_map/edge/pallas_call | solution.py:589
  5.8 0.8 collective-permute-start.2
  6.5 1.0 collective-permute-start.3
  7.5 6.1 %middle.1 = (f32[19,16,16,128]{3,2,1,0:T(8,128)}, s16[76,32,128]{2,1,0:T(8,128)(2,1)}, s16[76,32,128]{2,1,0:T(8,128)(2,1)}) custom-call(s32[2]{0:T(128)S(1)} %pad_add_fusion.parity_ref, f32[19,512,128]{2,1,0:T(8,128)} %bitcast.216, f32[19,16,16,128]{3,2,1,0:T(8,128)} %get-tuple-element.32.edge_hbm.e_hbm), custom_call_target="tpu_custom_call" | custom-call | bytes 22140000 | tf_op jit(solution)/shard_map/middle/pallas_call | solution.py:604
  13.6 1.3 %collective-permute-start = (s16[76,32,128]{2,1,0:T(8,128)(2,1)}, s16[76,32,128]{2,1,0:T(8,128)(2,1)S(1)}, u32[]{:S(2)}, u32[]{:S(2)}) collective-permute-start(s16[76,32,128]{2,1,0:T(8,128)(2,1)} %get-tuple-element.33), channel_id=1, source_target_pairs={{0,1},{1,0},{2,3},{3,2},{4,5},{5,4},{6,7},{7,6},{8,9},{9,8},{10,11... | collective-permute-start | bytes 1867784 | tf_op jit(solution)/shard_map/ppermute | solution.py:571
  14.9 5.3 %collective-permute-start.1 = (s16[76,32,128]{2,1,0:T(8,128)(2,1)}, s16[76,32,128]{2,1,0:T(8,128)(2,1)}, u32[]{:S(2)}, u32[]{:S(2)}) collective-permute-start(s16[76,32,128]{2,1,0:T(8,128)(2,1)} %get-tuple-element.34), channel_id=1, source_target_pairs={{0,15},{1,2},{2,1},{3,4},{4,3},{5,6},{6,5},{7,8},{8,7},{9,10},{10,... | collective-permute-start | bytes 1867784 | tf_op jit(solution)/shard_map/ppermute | solution.py:571
  21.0 1.6 %corner.1 = (f32[19,16,8,128]{3,2,1,0:T(8,128)S(1)}, s16[38,16,128]{2,1,0:T(8,128)(2,1)}, s16[38,16,128]{2,1,0:T(8,128)(2,1)}) custom-call(s32[2]{0:T(128)S(1)} %pad_add_fusion.parity_ref, s16[10,8,16,128]{3,2,1,0:T(8,128)(2,1)S(1)} %collective-permute-done.2.xa_ref, s16[10,8,16,128]{3,2,1,0:T(8,128)(2,1)S(1)} %collective-permute-done.3.xb_ref), custom_call_target="tpu_custom_call" | custom-call | bytes 7380000 | tf_op jit(solution)/shard_map/corner/pallas_call | solution.py:625
  22.6 1.0 %copy-done = f32[19,16,8,128]{3,2,1,0:T(8,128)} copy-done((f32[19,16,8,128]{3,2,1,0:T(8,128)}, f32[19,16,8,128]{3,2,1,0:T(8,128)S(1)}, u32[]{:S(2)}) %copy-start) | copy-done | bytes 1245208
  23.6 0.9 collective-permute-start.5
  24.6 0.6 broadcast_in_dim.2
  25.3 5.2 %all-to-all-start = ((f32[16,8,128]{2,1,0:T(8,128)}), f32[16,8,128]{2,1,0:T(8,128)S(1)}, u32[]{:S(2)}, u32[]{:S(2)}) async-start(f32[16,8,128]{2,1,0:T(8,128)} %broadcast_in_dim.2), calls=%async_computation | async-start | bytes 131072 | tf_op jit(solution)/shard_map/all_to_all | solution.py:666
  30.5 1.3 %copy-done.1 = f32[19,16,8,128]{3,2,1,0:T(8,128)S(1)} copy-done((f32[19,16,8,128]{3,2,1,0:T(8,128)S(1)}, f32[19,16,8,128]{3,2,1,0:T(8,128)}, u32[]{:S(2)}) %copy-start.1) | copy-done | bytes 1245208
  31.8 9.6 %inner.1 = (f32[19,26,56,128]{3,2,1,0:T(8,128)S(1)}, f32[19,26,56,128]{3,2,1,0:T(8,128)S(1)}, f32[19,512,128]{2,1,0:T(8,128)S(1)}, f32[3,26,56,128]{3,2,1,0:T(8,128)S(1)}, f32[512,128]{1,0:T(8,128)S(1)}) custom-call(f32[19,16,16,128]{3,2,1,0:T(8,128)} %get-tuple-element.32.edge_hbm.e_hbm, f32[19,16,16,128]{3,2,1,0:T(8,128)} %get-tuple-element.39.r_hbm, ...), custom_call_target="tpu_custom_call" | custom-call | bytes 44280000 | tf_op jit(solution)/shard_map/inner/pallas_call | solution.py:647
  41.4 10.2 %outer.1 = (f32[19,512,128]{2,1,0:T(8,128)}, bf16[512,128]{1,0:T(8,128)(2,1)}, f32[19,26,56,128]{3,2,1,0:T(8,128)S(1)}, f32[19,26,56,128]{3,2,1,0:T(8,128)S(1)},...) custom-call(s32[2]{0:T(128)S(1)} %pad_add_fusion.parity_ref, ...), custom_call_target="tpu_custom_call", output_to_operand_aliasing={{2}: (5, {}), {3}: (6, {}), {4}: (7, {}), {5}: (8, {}), {6}... | custom-call | bytes 44280000 | tf_op jit(solution)/shard_map/outer/pallas_call | solution.py:669
  51.7 0.9 copy-done.2
  52.6 16.8 %render.1 = f32[16,4,16,128]{3,2,1,0:T(8,128)} custom-call(f32[16,8,128]{2,1,0:T(8,128)S(1)} %all-to-all-done.table_ref, bf16[512,128]{1,0:T(8,128)(2,1)S(1)} %copy-done.2), custom_call_target="tpu_custom_call" | custom-call | bytes 59040000 | tf_op jit(solution)/shard_map/render/pallas_call | solution.py:686
  69.4 6.6 %all-to-all-start.1 = ((f32[16,4,16,128]{3,2,1,0:T(8,128)}), f32[16,4,16,128]{3,2,1,0:T(8,128)S(1)}, u32[]{:S(2)}, u32[]{:S(2)}) async-start(f32[16,4,16,128]{3,2,1,0:T(8,128)} %render.1), calls=%async_computation.1 | async-start | bytes 1048576 | tf_op jit(solution)/shard_map/all_to_all | solution.py:704
  76.6 7.7 %all-to-all-done.1 = f32[16,4,16,128]{3,2,1,0:T(8,128)S(1)} async-done(((f32[16,4,16,128]{3,2,1,0:T(8,128)}), f32[16,4,16,128]{3,2,1,0:T(8,128)S(1)}, u32[]{:S(2)}, u32[]{:S(2)}) %all-to-all-start.1) | async-done | bytes 524320 | tf_op jit(solution)/shard_map/all_to_all | solution.py:704
  84.3 0.7 add_bitcast_fusion.1
  85.0 0.7 fusion.7
  85.7 0.7 add_bitcast_fusion
  86.3 8.9 %collective-permute-start.6 = (f32[4,2,16,128]{3,2,1,0:T(8,128)S(1)}, f32[4,2,16,128]{3,2,1,0:T(8,128)S(1)}, u32[]{:S(2)}, u32[]{:S(2)}) collective-permute-start(f32[4,2,16,128]{3,2,1,0:T(8,128)S(1)} %pad_maximum_fusion), channel_id=1, source_target_pairs={{0,0},{1,1},{2,16},{3,17},{4,32},{5,33},{6,48},{7,49},{8,64},{9,65... | collective-permute-start | bytes 196616 | tf_op jit(solution)/shard_map/ppermute | solution.py:713
  95.2 3.3 %collective-permute-done.6 = f32[4,2,16,128]{3,2,1,0:T(8,128)S(1)} collective-permute-done((f32[4,2,16,128]{3,2,1,0:T(8,128)S(1)}, f32[4,2,16,128]{3,2,1,0:T(8,128)S(1)}, u32[]{:S(2)}, u32[]{:S(2)}) %collective-permute-start.6) | collective-permute-done | bytes 65568 | tf_op jit(solution)/shard_map/ppermute | solution.py:713
  98.5 0.6 copy.89
  (22 shorter events, 0.9 us)
Async XLA Ops:
  5.8 14.4 %copy-start.3 = (f32[1,5,8]{2,0,1:T(1,128)S(1)}, f32[1,5,8]{2,0,1:T(1,128)}, u32[]{:S(2)}) copy-start(f32[1,5,8]{2,0,1:T(1,128)} %param.6) | copy-start | bytes 484
  5.8 15.2 %collective-permute-start.2 = (s16[10,8,16,128]{3,2,1,0:T(8,128)(2,1)S(1)}, s16[10,8,16,128]{3,2,1,0:T(8,128)(2,1)S(1)}, u32[]{:S(2)}, u32[]{:S(2)}) collective-permute-start(s16[10,8,16,128]{3,2,1,0:T(8,128)(2,1)S(1)} %get-tuple-element.35), channel_id=1, source_target_pairs={{0,16},{16,0},{32,48},{48,32},{64,80},{80,64},{96,112},{112,96},{1... | collective-permute-start | bytes 983048 | tf_op jit(solution)/shard_map/ppermute | solution.py:571
  6.5 14.5 %collective-permute-start.3 = (s16[10,8,16,128]{3,2,1,0:T(8,128)(2,1)S(1)}, s16[10,8,16,128]{3,2,1,0:T(8,128)(2,1)S(1)}, u32[]{:S(2)}, u32[]{:S(2)}) collective-permute-start(s16[10,8,16,128]{3,2,1,0:T(8,128)(2,1)S(1)} %get-tuple-element.36), channel_id=1, source_target_pairs={{0,112},{16,32},{32,16},{48,64},{64,48},{80,96},{96,80},{112,0},{1... | collective-permute-start | bytes 983048 | tf_op jit(solution)/shard_map/ppermute | solution.py:571
  13.6 27.8 %collective-permute-start = (s16[76,32,128]{2,1,0:T(8,128)(2,1)}, s16[76,32,128]{2,1,0:T(8,128)(2,1)S(1)}, u32[]{:S(2)}, u32[]{:S(2)}) collective-permute-start(s16[76,32,128]{2,1,0:T(8,128)(2,1)} %get-tuple-element.33), channel_id=1, source_target_pairs={{0,1},{1,0},{2,3},{3,2},{4,5},{5,4},{6,7},{7,6},{8,9},{9,8},{10,11... | collective-permute-start | bytes 1867784 | tf_op jit(solution)/shard_map/ppermute | solution.py:571
  14.9 26.5 %collective-permute-start.1 = (s16[76,32,128]{2,1,0:T(8,128)(2,1)}, s16[76,32,128]{2,1,0:T(8,128)(2,1)}, u32[]{:S(2)}, u32[]{:S(2)}) collective-permute-start(s16[76,32,128]{2,1,0:T(8,128)(2,1)} %get-tuple-element.34), channel_id=1, source_target_pairs={{0,15},{1,2},{2,1},{3,4},{4,3},{5,6},{6,5},{7,8},{8,7},{9,10},{10,... | collective-permute-start | bytes 1867784 | tf_op jit(solution)/shard_map/ppermute | solution.py:571
  22.6 1.0 %copy-start = (f32[19,16,8,128]{3,2,1,0:T(8,128)}, f32[19,16,8,128]{3,2,1,0:T(8,128)S(1)}, u32[]{:S(2)}) copy-start(f32[19,16,8,128]{3,2,1,0:T(8,128)S(1)} %get-tuple-element.40.h_ref) | copy-start | bytes 3735556
  23.6 17.8 %collective-permute-start.4 = (s16[38,16,128]{2,1,0:T(8,128)(2,1)}, s16[38,16,128]{2,1,0:T(8,128)(2,1)}, u32[]{:S(2)}, u32[]{:S(2)}) collective-permute-start(s16[38,16,128]{2,1,0:T(8,128)(2,1)} %get-tuple-element.37), channel_id=1, source_target_pairs={{0,1},{1,0},{2,3},{3,2},{4,5},{5,4},{6,7},{7,6},{8,9},{9,8},{10,11... | collective-permute-start | bytes 466952 | tf_op jit(solution)/shard_map/ppermute | solution.py:571
  23.6 17.8 %collective-permute-start.5 = (s16[38,16,128]{2,1,0:T(8,128)(2,1)}, s16[38,16,128]{2,1,0:T(8,128)(2,1)}, u32[]{:S(2)}, u32[]{:S(2)}) collective-permute-start(s16[38,16,128]{2,1,0:T(8,128)(2,1)} %get-tuple-element.38), channel_id=1, source_target_pairs={{0,15},{1,2},{2,1},{3,4},{4,3},{5,6},{6,5},{7,8},{8,7},{9,10},{10,... | collective-permute-start | bytes 466952 | tf_op jit(solution)/shard_map/ppermute | solution.py:571
  25.3 26.4 %all-to-all-start = ((f32[16,8,128]{2,1,0:T(8,128)}), f32[16,8,128]{2,1,0:T(8,128)S(1)}, u32[]{:S(2)}, u32[]{:S(2)}) async-start(f32[16,8,128]{2,1,0:T(8,128)} %broadcast_in_dim.2), calls=%async_computation | async-start | bytes 131072 | tf_op jit(solution)/shard_map/all_to_all | solution.py:666
  30.5 1.3 %copy-start.1 = (f32[19,16,8,128]{3,2,1,0:T(8,128)S(1)}, f32[19,16,8,128]{3,2,1,0:T(8,128)}, u32[]{:S(2)}) copy-start(f32[19,16,8,128]{3,2,1,0:T(8,128)} %copy-done) | copy-start | bytes 3735556
  51.7 0.9 copy-start.2
  69.4 14.9 %all-to-all-start.1 = ((f32[16,4,16,128]{3,2,1,0:T(8,128)}), f32[16,4,16,128]{3,2,1,0:T(8,128)S(1)}, u32[]{:S(2)}, u32[]{:S(2)}) async-start(f32[16,4,16,128]{3,2,1,0:T(8,128)} %render.1), calls=%async_computation.1 | async-start | bytes 1048576 | tf_op jit(solution)/shard_map/all_to_all | solution.py:704
  86.3 12.2 %collective-permute-start.6 = (f32[4,2,16,128]{3,2,1,0:T(8,128)S(1)}, f32[4,2,16,128]{3,2,1,0:T(8,128)S(1)}, u32[]{:S(2)}, u32[]{:S(2)}) collective-permute-start(f32[4,2,16,128]{3,2,1,0:T(8,128)S(1)} %pad_maximum_fusion), channel_id=1, source_target_pairs={{0,0},{1,1},{2,16},{3,17},{4,32},{5,33},{6,48},{7,49},{8,64},{9,65... | collective-permute-start | bytes 196616 | tf_op jit(solution)/shard_map/ppermute | solution.py:713

commit v6 on v5

--- a/solution.py
+++ b/solution.py
@@ -241,7 +241,7 @@
         X_PLACE[b_] = (number_, n_, True)
 
 
-def corner_kernel(width_cells, parity_ref, xa_ref, xb_ref, h_ref, ca_ref, cb_ref):
+def corner_kernel(width_cells, parity_ref, xa_ref, xb_ref, h_hbm, ca_ref, cb_ref, h_ref, out_sem):
     rows = row_index()
     odd_depth = jnp.full((8, 128), parity_ref[0], jnp.int32) == 1
     odd_image = jnp.full((8, 128), parity_ref[1], jnp.int32) == 1
@@ -260,6 +260,8 @@
         return carry
 
     lax.fori_loop(0, width_cells // 2, halo, 0)
+    keep_h = pltpu.make_async_copy(h_ref, h_hbm, out_sem)
+    keep_h.start()
     low_face = face_list(0, 1)
     high_face = face_list(width_cells - 1, -1)
     for index in range(0, len(low_face), 2):
@@ -270,6 +272,7 @@
             b.append(jnp.where(odd_image, high, low))
         ca_ref[index // 2] = pack16(*a)
         cb_ref[index // 2] = pack16(*b)
+    keep_h.wait()
 
 
 PAD = 8
@@ -339,7 +342,7 @@
 
 
 def inner_kernel(
-    depth_cells, width_cells, e_hbm, r_hbm, h_ref, sa_ref, sb_ref, final_ref, flow_ref, plain_ref, e_ref, r_ref, sems
+    depth_cells, width_cells, e_hbm, r_hbm, h_hbm, sa_ref, sb_ref, final_ref, flow_ref, plain_ref, e_ref, r_ref, h_ref, sems
 ):
     tiles = depth_cells // 8
     rows = row_index()
@@ -360,6 +363,7 @@
             [
                 pltpu.make_async_copy(e_hbm.at[:, at], e_ref.at[:, at], sems.at[part, 0]),
                 pltpu.make_async_copy(r_hbm.at[:, at], r_ref.at[:, at], sems.at[part, 1]),
+                pltpu.make_async_copy(h_hbm.at[:, at], h_ref.at[:, at], sems.at[part, 2]),
             ]
         )
         for load in loads[-1]:
@@ -433,7 +437,7 @@
             step_row(source, target, HALO + width_cells - step + k, tiles + 1, shift)
             return carry
 
-        lax.fori_loop(0, HALO, both, 0)
+        lax.fori_loop(0, HALO, both, 0, unroll=HALO)
 
     stage(sa_ref, sb_ref, 1, 0)
     stage(sb_ref, sa_ref, 2, 0)
@@ -489,10 +493,10 @@
 BLOCK = 4
 
 
-def render_kernel(depth_cells, width_cells, functions, bumps, table_ref, vort_ref, image_ref, place_ref, fade_ref):
+def render_kernel(depth_cells, width_cells, functions, bumps, table_ref, plain_ref, image_ref, place_ref, fade_ref):
     def prepare(x, carry):
         at = pl.ds(pl.multiple_of(x * width_cells, width_cells), width_cells)
-        value = vort_ref[at, :].astype(jnp.float32)
+        value = plain_ref[at, :].astype(jnp.bfloat16).astype(jnp.float32)
         level = value / (value + LEVEL_OFFSET)
         place = STRETCH * level - CENTRE
         fade = jnp.exp2(-place * place)
@@ -538,15 +542,20 @@
     lax.fori_loop(0, functions, one, 0)
 
 
-def composite(slabs, backward):
-    count = slabs.shape[0]
-    clear = 1.0
-    color = [0.0] * 3
-    for step in range(count):
-        piece = [jnp.where(backward, slabs[count - 1 - step, :, c], slabs[step, :, c]) for c in range(4)]
-        color = [color[c] + clear * piece[c] for c in range(3)]
-        clear = clear * piece[3]
-    return jnp.stack(color + [1.0 - clear])
+def composite_kernel(slabs, halves, order_ref, piece_ref, image_ref):
+    backward = order_ref[0] > 0.5
+    width_cells = piece_ref.shape[3]
+    for side in range(halves):
+        at = slice(side * width_cells, (side + 1) * width_cells)
+        clear = jnp.ones(piece_ref.shape[3:], jnp.float32)
+        color = [jnp.zeros_like(clear) for c in range(3)]
+        for step in range(slabs):
+            slab = jnp.where(backward, slabs - 1 - step, step)
+            color = [color[c] + clear * piece_ref[slab, side, c] for c in range(3)]
+            clear = clear * piece_ref[slab, side, 3]
+        for c in range(3):
+            image_ref[c, at, :] = color[c]
+        image_ref[3, at, :] = 1.0 - clear
 
 
 HBM = pl.BlockSpec(memory_space=pltpu.HBM)
@@ -561,6 +570,10 @@
 
 def in_hbm(value):
     return pltpu.with_memory_space_constraint(value, pltpu.HBM)
+
+
+def in_vmem(value):
+    return pltpu.with_memory_space_constraint(value, pltpu.VMEM)
 
 
 def partner(index, count, phase):
@@ -624,9 +637,10 @@
     yb = swap(ib, "image", image_count, 1)
     halo, ca, cb = pl.pallas_call(
         functools.partial(corner_kernel, width_cells),
-        out_shape=(jax.ShapeDtypeStruct((Q, width_cells, 8, lanes), f32), c_shape, c_shape),
+        out_shape=(pltpu.HBM((Q, width_cells, 8, lanes), f32), c_shape, c_shape),
         in_specs=[SMEM, VMEM, VMEM],
-        out_specs=(VMEM,) * 3,
+        out_specs=(HBM, VMEM, VMEM),
+        scratch_shapes=[pltpu.VMEM((Q, width_cells, 8, lanes), f32), pltpu.SemaphoreType.DMA],
         compiler_params=GRANT,
         cost_estimate=cost(2),
         name="corner",
@@ -647,17 +661,18 @@
     state = pl.pallas_call(
         functools.partial(inner_kernel, depth_cells, width_cells),
         out_shape=stages,
-        in_specs=[HBM, HBM, VMEM],
+        in_specs=[HBM] * 3,
         out_specs=(VMEM,) * 5,
         scratch_shapes=[
             pltpu.VMEM((Q, width_cells, half[1], lanes), f32),
             pltpu.VMEM((Q, width_cells, half[0], lanes), f32),
-            pltpu.SemaphoreType.DMA((4, 2)),
+            pltpu.VMEM((Q, width_cells, 8, lanes), f32),
+            pltpu.SemaphoreType.DMA((4, 3)),
         ],
         compiler_params=GRANT,
         cost_estimate=cost(12),
         name="inner",
-    )(in_hbm(edge), in_hbm(middle), halo)
+    )(in_hbm(edge), in_hbm(middle), in_hbm(halo))
 
     bumps = transfer.shape[2]
     row = jnp.concatenate([bump_tables(transfer, ray_cells).reshape(-1), direction.astype(f32)])
@@ -666,7 +681,7 @@
     tables = lax.all_to_all(
         jnp.broadcast_to(row, (image_count, 8, lanes)), "image", 0, 0, tiled=True
     )
-    final, vorticity, *_ = pl.pallas_call(
+    final, vorticity, *_, plain = pl.pallas_call(
         functools.partial(outer_kernel, depth_cells, width_cells),
         out_shape=(
             jax.ShapeDtypeStruct((Q, cells, lanes), f32),
@@ -695,7 +710,7 @@
         compiler_params=GRANT,
         cost_estimate=cost(16),
         name="render",
-    )(tables, vorticity)
+    )(tables, in_vmem(plain))
     halves = image_count // depth_count
     groups = [
         [sd * image_count + halves * row + side for sd in range(depth_count) for side in range(halves)]
@@ -704,14 +719,21 @@
     slabs = lax.all_to_all(
         partial, ("depth", "image"), 0, 0, axis_index_groups=groups, tiled=True
     ).reshape(depth_count, halves, 4, width_cells, lanes)
-    image = composite(slabs, tables[halves * d + i % halves, 0, 5 * bumps] > 0.5)
+    image = pl.pallas_call(
+        functools.partial(composite_kernel, depth_count, halves),
+        out_shape=jax.ShapeDtypeStruct((4, halves * width_cells, lanes), f32),
+        in_specs=[SMEM, VMEM],
+        out_specs=VMEM,
+        cost_estimate=cost(1),
+        name="composite",
+    )(tables[halves * d + i % halves, 0, 5 * bumps][None], in_vmem(slabs))
     route = [
         (sd * image_count + si, (si // halves) * image_count + halves * sd + si % halves)
         for sd in range(depth_count)
         for si in range(image_count)
     ]
     images = lax.ppermute(image, ("depth", "image"), route)
-    images = images.reshape(1, 4, halves * width_cells, lanes)
+    images = images[None]
     return (
         final.reshape(populations.shape),
         vorticity.reshape(depth_cells, width_cells, lanes),

time: 100 us -> 97.3 us (0.973)
  other arithmetic: 2.81 us -> 0.19 us
  local copies, waits for them, and re-layouts: 4.58 us -> 2 us
  Pallas kernels: 49.3 us -> 51.2 us
    unnamed x9 -> x3, local copies, waits for them, and re-layouts: 3.87 us -> 0.64 us
    add x3 -> x0, other arithmetic: 2.02 us -> none  [composite(): color = [color[c] + clear * piece[c] for c in range(3)]]
    pallas_call x0 -> x1, Pallas kernels: none -> 1.29 us  [on_device(): pl.pallas_call(functools.partial(composite_kernel, depth_count, halves),...]
  transfers between devices with their start and end apart: 9 -> 9, of which waited for: 2 -> 2; matrix products, arithmetic and copies ran while one was open for 1% -> 2% of each run, Pallas kernels for 28% -> 29%
where the time goes in v6:
time: 97.3 us; the launch traced here: 96.1 us
  Pallas kernels  51.2 us (53%)
  starting transfers between devices  30.1 us (31%)
  waiting for transfers between devices  11.2 us (12%)
  local copies, waits for them, and re-layouts  2 us (2%)
  between operations  1.43 us (1%)
    pallas_call x1, Pallas kernels, on_device(): pl.pallas_call(functools.partial(render_kernel, depth_cells, width_cells,...  16.8 us
    pallas_call x1, Pallas kernels, on_device(): pl.pallas_call(functools.partial(inner_kernel, depth_cells, width_cells),...  9.95 us
    pallas_call x1, Pallas kernels, on_device(): pl.pallas_call(functools.partial(outer_kernel, depth_cells, width_cells),...  9.5 us
    ppermute x6, starting transfers between devices, swap(): lax.ppermute(value, axis, [(i, partner(i, count, phase)) for i in range(c...  9.31 us
    ppermute x1, starting transfers between devices, on_device(): images = lax.ppermute(image, ('depth', 'image'), route)  8.84 us
    all_to_all x1, waiting for transfers between devices, on_device(): lax.all_to_all(partial, ('depth', 'image'), 0, 0, axis_index_groups=group...  7.64 us
    all_to_all x1, starting transfers between devices, on_device(): lax.all_to_all(partial, ('depth', 'image'), 0, 0, axis_index_groups=group...  6.65 us
    pallas_call x1, Pallas kernels, on_device(): pl.pallas_call(functools.partial(middle_kernel, depth_cells, width_cells)...  6.13 us
  transfers between devices with their start and end apart: 9, of which 2 were waited for; matrix products, arithmetic and copies ran while one was open for 2% of the time, Pallas kernels for 29%

profile of v6, /device:TPU:17, one launch (start us, length us, event | category | flops | bytes accessed | tf_op | source)
XLA Modules:
  0.0 96.1 jit_solution(10517229482716134938)
XLA Ops:
  0.6 0.1 pad_add_fusion.parity_ref
  0.7 5.0 %edge.1 = (f32[19,16,16,128]{3,2,1,0:T(8,128)}, s16[10,8,16,128]{3,2,1,0:T(8,128)(2,1)S(1)}, s16[10,8,16,128]{3,2,1,0:T(8,128)(2,1)S(1)}) custom-call(s32[2]{0:T(128)S(1)} %pad_add_fusion.parity_ref, f32[19,512,128]{2,1,0:T(8,128)} %bitcast.11), custom_call_target="tpu_custom_call" | custom-call | bytes 22140000 | tf_op jit(solution)/shard_map/edge/pallas_call | solution.py:602
  5.8 0.8 collective-permute-start.2
  6.5 1.0 %collective-permute-start.3 = (s16[10,8,16,128]{3,2,1,0:T(8,128)(2,1)S(1)}, s16[10,8,16,128]{3,2,1,0:T(8,128)(2,1)S(1)}, u32[]{:S(2)}, u32[]{:S(2)}) collective-permute-start(s16[10,8,16,128]{3,2,1,0:T(8,128)(2,1)S(1)} %get-tuple-element.37), channel_id=1, source_target_pairs={{0,112},{16,32},{32,16},{48,64},{64,48},{80,96},{96,80},{112,0},{1... | collective-permute-start | bytes 983048 | tf_op jit(solution)/shard_map/ppermute | solution.py:584
  7.5 6.1 %middle.1 = (f32[19,16,16,128]{3,2,1,0:T(8,128)}, s16[76,32,128]{2,1,0:T(8,128)(2,1)}, s16[76,32,128]{2,1,0:T(8,128)(2,1)}) custom-call(s32[2]{0:T(128)S(1)} %pad_add_fusion.parity_ref, f32[19,512,128]{2,1,0:T(8,128)} %bitcast.12, f32[19,16,16,128]{3,2,1,0:T(8,128)} %get-tuple-element.33.edge_hbm.e_hbm), custom_call_target="tpu_custom_call" | custom-call | bytes 22140000 | tf_op jit(solution)/shard_map/middle/pallas_call | solution.py:617
  13.6 1.3 %collective-permute-start = (s16[76,32,128]{2,1,0:T(8,128)(2,1)}, s16[76,32,128]{2,1,0:T(8,128)(2,1)}, u32[]{:S(2)}, u32[]{:S(2)}) collective-permute-start(s16[76,32,128]{2,1,0:T(8,128)(2,1)} %get-tuple-element.34), channel_id=1, source_target_pairs={{0,1},{1,0},{2,3},{3,2},{4,5},{5,4},{6,7},{7,6},{8,9},{9,8},{10,11... | collective-permute-start | bytes 1867784 | tf_op jit(solution)/shard_map/ppermute | solution.py:584
  14.9 5.3 %collective-permute-start.1 = (s16[76,32,128]{2,1,0:T(8,128)(2,1)}, s16[76,32,128]{2,1,0:T(8,128)(2,1)}, u32[]{:S(2)}, u32[]{:S(2)}) collective-permute-start(s16[76,32,128]{2,1,0:T(8,128)(2,1)} %get-tuple-element.35), channel_id=1, source_target_pairs={{0,15},{1,2},{2,1},{3,4},{4,3},{5,6},{6,5},{7,8},{8,7},{9,10},{10,... | collective-permute-start | bytes 1867784 | tf_op jit(solution)/shard_map/ppermute | solution.py:584
  20.9 0.1 reshape.64
  21.0 2.5 %corner.1 = (f32[19,16,8,128]{3,2,1,0:T(8,128)}, s16[38,16,128]{2,1,0:T(8,128)(2,1)}, s16[38,16,128]{2,1,0:T(8,128)(2,1)S(1)}) custom-call(s32[2]{0:T(128)S(1)} %pad_add_fusion.parity_ref, s16[10,8,16,128]{3,2,1,0:T(8,128)(2,1)S(1)} %collective-permute-done.2.xa_ref, s16[10,8,16,128]{3,2,1,0:T(8,128)(2,1)S(1)} %collective-permute-done.3.xb_ref), custom_call_target="tpu_custom_call" | custom-call | bytes 7380000 | tf_op jit(solution)/shard_map/corner/pallas_call | solution.py:638
  23.5 0.1 collective-permute-start.4
  23.6 0.9 collective-permute-start.5
  24.5 0.1 fusion.3
  24.6 0.6 broadcast_in_dim.8
  25.2 5.3 %all-to-all-start = ((f32[16,8,128]{2,1,0:T(8,128)}), f32[16,8,128]{2,1,0:T(8,128)S(1)}, u32[]{:S(2)}, u32[]{:S(2)}) async-start(f32[16,8,128]{2,1,0:T(8,128)} %broadcast_in_dim.8), calls=%async_computation | async-start | bytes 131072 | tf_op jit(solution)/shard_map/all_to_all | solution.py:681
  30.6 9.9 %inner.1 = (f32[19,26,56,128]{3,2,1,0:T(8,128)S(1)}, f32[19,26,56,128]{3,2,1,0:T(8,128)S(1)}, f32[19,512,128]{2,1,0:T(8,128)S(1)}, f32[3,26,56,128]{3,2,1,0:T(8,128)S(1)}, f32[512,128]{1,0:T(8,128)S(1)}) custom-call(f32[19,16,16,128]{3,2,1,0:T(8,128)} %get-tuple-element.33.edge_hbm.e_hbm, f32[19,16,16,128]{3,2,1,0:T(8,128)} %get-tuple-element.40.r_hbm, ...), custom_call_target="tpu_custom_call" | custom-call | bytes 44280000 | tf_op jit(solution)/shard_map/inner/pallas_call | solution.py:661
  40.6 9.5 %outer.1 = (f32[19,512,128]{2,1,0:T(8,128)}, bf16[512,128]{1,0:T(8,128)(2,1)}, f32[19,26,56,128]{3,2,1,0:T(8,128)S(1)}, f32[19,26,56,128]{3,2,1,0:T(8,128)S(1)},...) custom-call(s32[2]{0:T(128)S(1)} %pad_add_fusion.parity_ref, ...), custom_call_target="tpu_custom_call", output_to_operand_aliasing={{2}: (5, {}), {3}: (6, {}), {4}: (7, {}), {5}: (8, {}), {6}... | custom-call | bytes 44280000 | tf_op jit(solution)/shard_map/outer/pallas_call | solution.py:684
  50.1 16.8 %render.1 = f32[16,4,16,128]{3,2,1,0:T(8,128)} custom-call(f32[16,8,128]{2,1,0:T(8,128)S(1)} %all-to-all-done.table_ref, f32[512,128]{1,0:T(8,128)S(1)} %get-tuple-element.50.plain_ref), custom_call_target="tpu_custom_call" | custom-call | bytes 59040000 | tf_op jit(solution)/shard_map/render/pallas_call | solution.py:701
  66.9 6.7 %all-to-all-start.1 = ((f32[16,4,16,128]{3,2,1,0:T(8,128)}), f32[16,4,16,128]{3,2,1,0:T(8,128)S(1)}, u32[]{:S(2)}, u32[]{:S(2)}) async-start(f32[16,4,16,128]{3,2,1,0:T(8,128)} %render.1), calls=%async_computation.1 | async-start | bytes 1048576 | tf_op jit(solution)/shard_map/all_to_all | solution.py:719
  73.5 0.6 constant_dynamic-slice_fusion
  74.2 7.6 %all-to-all-done.1 = f32[16,4,16,128]{3,2,1,0:T(8,128)S(1)} async-done(((f32[16,4,16,128]{3,2,1,0:T(8,128)}), f32[16,4,16,128]{3,2,1,0:T(8,128)S(1)}, u32[]{:S(2)}, u32[]{:S(2)}) %all-to-all-start.1) | async-done | bytes 524320 | tf_op jit(solution)/shard_map/all_to_all | solution.py:719
  81.8 1.3 %composite.1 = f32[4,32,128]{2,1,0:T(8,128)} custom-call(f32[1]{0:T(128)} %bitcast.6.order_ref, f32[8,2,4,16,128]{4,3,2,1,0:T(8,128)S(1)} %bitcast.10), custom_call_target="tpu_custom_call" | custom-call | bytes 3690000 | tf_op jit(solution)/shard_map/composite/pallas_call | solution.py:722
  83.1 8.8 %collective-permute-start.6 = (f32[4,32,128]{2,1,0:T(8,128)}, f32[4,32,128]{2,1,0:T(8,128)S(1)}, u32[]{:S(2)}, u32[]{:S(2)}) collective-permute-start(f32[4,32,128]{2,1,0:T(8,128)} %composite.1), channel_id=1, source_target_pairs={{0,0},{1,1},{2,16},{3,17},{4,32},{5,33},{6,48},{7,49},{8,64},{9,65... | collective-permute-start | bytes 196616 | tf_op jit(solution)/shard_map/ppermute | solution.py:735
  92.0 3.5 %collective-permute-done.6 = f32[4,32,128]{2,1,0:T(8,128)S(1)} collective-permute-done((f32[4,32,128]{2,1,0:T(8,128)}, f32[4,32,128]{2,1,0:T(8,128)S(1)}, u32[]{:S(2)}, u32[]{:S(2)}) %collective-permute-start.6) | collective-permute-done | bytes 65568 | tf_op jit(solution)/shard_map/ppermute | solution.py:735
  95.5 0.6 copy.19
  (13 shorter events, 0.1 us)
Async XLA Ops:
  5.8 14.5 %copy-start = (f32[1,5,8]{2,0,1:T(1,128)S(1)}, f32[1,5,8]{2,0,1:T(1,128)}, u32[]{:S(2)}) copy-start(f32[1,5,8]{2,0,1:T(1,128)} %param.6) | copy-start | bytes 484
  5.8 15.2 %collective-permute-start.2 = (s16[10,8,16,128]{3,2,1,0:T(8,128)(2,1)S(1)}, s16[10,8,16,128]{3,2,1,0:T(8,128)(2,1)S(1)}, u32[]{:S(2)}, u32[]{:S(2)}) collective-permute-start(s16[10,8,16,128]{3,2,1,0:T(8,128)(2,1)S(1)} %get-tuple-element.36), channel_id=1, source_target_pairs={{0,16},{16,0},{32,48},{48,32},{64,80},{80,64},{96,112},{112,96},{1... | collective-permute-start | bytes 983048 | tf_op jit(solution)/shard_map/ppermute | solution.py:584
  6.5 14.5 %collective-permute-start.3 = (s16[10,8,16,128]{3,2,1,0:T(8,128)(2,1)S(1)}, s16[10,8,16,128]{3,2,1,0:T(8,128)(2,1)S(1)}, u32[]{:S(2)}, u32[]{:S(2)}) collective-permute-start(s16[10,8,16,128]{3,2,1,0:T(8,128)(2,1)S(1)} %get-tuple-element.37), channel_id=1, source_target_pairs={{0,112},{16,32},{32,16},{48,64},{64,48},{80,96},{96,80},{112,0},{1... | collective-permute-start | bytes 983048 | tf_op jit(solution)/shard_map/ppermute | solution.py:584
  13.6 26.9 %collective-permute-start = (s16[76,32,128]{2,1,0:T(8,128)(2,1)}, s16[76,32,128]{2,1,0:T(8,128)(2,1)}, u32[]{:S(2)}, u32[]{:S(2)}) collective-permute-start(s16[76,32,128]{2,1,0:T(8,128)(2,1)} %get-tuple-element.34), channel_id=1, source_target_pairs={{0,1},{1,0},{2,3},{3,2},{4,5},{5,4},{6,7},{7,6},{8,9},{9,8},{10,11... | collective-permute-start | bytes 1867784 | tf_op jit(solution)/shard_map/ppermute | solution.py:584
  14.9 25.6 %collective-permute-start.1 = (s16[76,32,128]{2,1,0:T(8,128)(2,1)}, s16[76,32,128]{2,1,0:T(8,128)(2,1)}, u32[]{:S(2)}, u32[]{:S(2)}) collective-permute-start(s16[76,32,128]{2,1,0:T(8,128)(2,1)} %get-tuple-element.35), channel_id=1, source_target_pairs={{0,15},{1,2},{2,1},{3,4},{4,3},{5,6},{6,5},{7,8},{8,7},{9,10},{10,... | collective-permute-start | bytes 1867784 | tf_op jit(solution)/shard_map/ppermute | solution.py:584
  23.5 17.0 %collective-permute-start.4 = (s16[38,16,128]{2,1,0:T(8,128)(2,1)}, s16[38,16,128]{2,1,0:T(8,128)(2,1)S(1)}, u32[]{:S(2)}, u32[]{:S(2)}) collective-permute-start(s16[38,16,128]{2,1,0:T(8,128)(2,1)} %get-tuple-element.38), channel_id=1, source_target_pairs={{0,1},{1,0},{2,3},{3,2},{4,5},{5,4},{6,7},{7,6},{8,9},{9,8},{10,11... | collective-permute-start | bytes 466952 | tf_op jit(solution)/shard_map/ppermute | solution.py:584
  23.6 16.9 %collective-permute-start.5 = (s16[38,16,128]{2,1,0:T(8,128)(2,1)S(1)}, s16[38,16,128]{2,1,0:T(8,128)(2,1)S(1)}, u32[]{:S(2)}, u32[]{:S(2)}) collective-permute-start(s16[38,16,128]{2,1,0:T(8,128)(2,1)S(1)} %get-tuple-element.39), channel_id=1, source_target_pairs={{0,15},{1,2},{2,1},{3,4},{4,3},{5,6},{6,5},{7,8},{8,7},{9,10},{10,... | collective-permute-start | bytes 466952 | tf_op jit(solution)/shard_map/ppermute | solution.py:584
  25.2 24.9 %all-to-all-start = ((f32[16,8,128]{2,1,0:T(8,128)}), f32[16,8,128]{2,1,0:T(8,128)S(1)}, u32[]{:S(2)}, u32[]{:S(2)}) async-start(f32[16,8,128]{2,1,0:T(8,128)} %broadcast_in_dim.8), calls=%async_computation | async-start | bytes 131072 | tf_op jit(solution)/shard_map/all_to_all | solution.py:681
  66.9 14.9 %all-to-all-start.1 = ((f32[16,4,16,128]{3,2,1,0:T(8,128)}), f32[16,4,16,128]{3,2,1,0:T(8,128)S(1)}, u32[]{:S(2)}, u32[]{:S(2)}) async-start(f32[16,4,16,128]{3,2,1,0:T(8,128)} %render.1), calls=%async_computation.1 | async-start | bytes 1048576 | tf_op jit(solution)/shard_map/all_to_all | solution.py:719
  83.1 12.4 %collective-permute-start.6 = (f32[4,32,128]{2,1,0:T(8,128)}, f32[4,32,128]{2,1,0:T(8,128)S(1)}, u32[]{:S(2)}, u32[]{:S(2)}) collective-permute-start(f32[4,32,128]{2,1,0:T(8,128)} %composite.1), channel_id=1, source_target_pairs={{0,0},{1,1},{2,16},{3,17},{4,32},{5,33},{6,48},{7,49},{8,64},{9,65... | collective-permute-start | bytes 196616 | tf_op jit(solution)/shard_map/ppermute | solution.py:735

commit v7 on v6

--- a/solution.py
+++ b/solution.py
@@ -129,7 +129,14 @@
     lax.fori_loop(0, width_cells, at_y, 0, unroll=8)
 
 
-def edge_kernel(depth_cells, width_cells, parity_ref, f_hbm, r_hbm, da_ref, db_ref, f_ref, r_ref, in_sems, out_sem):
+def keep_chunk(r_ref, r_hbm, k, sems):
+    at = pl.ds(8 * k, 8)
+    copy = pltpu.make_async_copy(r_ref.at[:, :, at], r_hbm.at[:, :, at], sems.at[k])
+    copy.start()
+    return copy
+
+
+def edge_kernel(depth_cells, width_cells, parity_ref, f_hbm, r_hbm, da_ref, db_ref, f_ref, r_ref, in_sems, out_sems):
     rows = row_index()
     chunk = 8 * width_cells
     loads = []
@@ -141,11 +148,11 @@
         )
     for load in loads:
         load.start()
+    keeps = []
     for k, load in enumerate(loads):
         load.wait()
         collide_chunk(f_ref, r_ref, k * chunk, 8 * k, width_cells)
-    keep_r = pltpu.make_async_copy(r_ref, r_hbm, out_sem)
-    keep_r.start()
+        keeps.append(keep_chunk(r_ref, r_hbm, k, out_sems))
 
     odd_depth = jnp.full((8, 128), parity_ref[0], jnp.int32) == 1
 
@@ -169,11 +176,12 @@
         return carry
 
     lax.fori_loop(0, width_cells // 2, face_x, 0, unroll=2)
-    keep_r.wait()
+    for keep in keeps:
+        keep.wait()
 
 
 def middle_kernel(
-    depth_cells, width_cells, parity_ref, f_hbm, edge_hbm, r_hbm, ia_ref, ib_ref, f_ref, r_ref, edge_ref, in_sems, out_sem
+    depth_cells, width_cells, parity_ref, f_hbm, edge_hbm, r_hbm, ia_ref, ib_ref, f_ref, r_ref, edge_ref, in_sems, out_sems
 ):
     chunk = 8 * width_cells
     tiles = depth_cells // 8
@@ -194,11 +202,11 @@
         )
     for load in loads:
         load.start()
+    keeps = []
     for j in range(tiles - 2):
         loads[j].wait()
         collide_chunk(f_ref, r_ref, j * chunk, 8 * j, width_cells)
-    keep_r = pltpu.make_async_copy(r_ref, r_hbm, out_sem)
-    keep_r.start()
+        keeps.append(keep_chunk(r_ref, r_hbm, j, out_sems))
     for load in loads[tiles - 2 :]:
         load.wait()
 
@@ -223,7 +231,8 @@
                 b.append(jnp.where(odd_image, high, low))
             ia_ref[index, 16 * c : 16 * c + 16, :] = pack_code(*a)
             ib_ref[index, 16 * c : 16 * c + 16, :] = pack_code(*b)
-    keep_r.wait()
+    for keep in keeps:
+        keep.wait()
 
 
 def x_halo(low, high, n, second, rows):
@@ -379,7 +388,7 @@
             step_row(source, target, HALO + step + 2 * k + 1, tiles + 1, shift)
             return carry
 
-        lax.fori_loop(0, (width_cells - 2 * step) // 2, pair, 0)
+        lax.fori_loop(0, (width_cells - 2 * step) // 2, pair, 0, unroll=True)
 
     stage(sa_ref, sb_ref, 1, 0)
     stage(sb_ref, sa_ref, 2, 0)
@@ -532,7 +541,7 @@
             return clear, red, green, blue
 
         zero = jnp.zeros((width_cells, 128), jnp.float32)
-        clear, red, green, blue = lax.fori_loop(0, depth_cells // BLOCK, cells, (zero + 1.0, zero, zero, zero))
+        clear, red, green, blue = lax.fori_loop(0, depth_cells // BLOCK, cells, (zero + 1.0, zero, zero, zero), unroll=2)
         image_ref[m, 0] = red
         image_ref[m, 1] = green
         image_ref[m, 2] = blue
@@ -608,7 +617,7 @@
             pltpu.VMEM((Q, half[1] * width_cells, lanes), f32),
             pltpu.VMEM((Q, width_cells, half[1], lanes), f32),
             pltpu.SemaphoreType.DMA((2,)),
-            pltpu.SemaphoreType.DMA,
+            pltpu.SemaphoreType.DMA((2,)),
         ],
         compiler_params=GRANT,
         cost_estimate=cost(6),
@@ -624,7 +633,7 @@
             pltpu.VMEM((Q, width_cells, half[0], lanes), f32),
             pltpu.VMEM((Q, 2 * HALO, half[1], lanes), f32),
             pltpu.SemaphoreType.DMA((depth_cells // 8,)),
-            pltpu.SemaphoreType.DMA,
+            pltpu.SemaphoreType.DMA((depth_cells // 8 - 2,)),
         ],
         compiler_params=GRANT,
         cost_estimate=cost(6),

time: 97.3 us -> 94.8 us (0.974)
  Pallas kernels: 51.2 us -> 48.7 us
    pallas_call x1, Pallas kernels: 9.95 us -> 8.69 us  [on_device(): pl.pallas_call(functools.partial(inner_kernel, depth_cells, width_cells),...]
  transfers between devices with their start and end apart: 9 -> 9, of which waited for: 2 -> 2; matrix products, arithmetic and copies ran while one was open for 2% -> 2% of each run, Pallas kernels for 29% -> 28%
where the time goes in v7:
time: 94.8 us; the launch traced here: 93.6 us
  Pallas kernels  48.7 us (51%)
  starting transfers between devices  30.1 us (32%)
  waiting for transfers between devices  11.2 us (12%)
  local copies, waits for them, and re-layouts  2 us (2%)
  between operations  1.44 us (2%)
    pallas_call x1, Pallas kernels, on_device(): pl.pallas_call(functools.partial(render_kernel, depth_cells, width_cells,...  16.4 us
    pallas_call x1, Pallas kernels, on_device(): pl.pallas_call(functools.partial(outer_kernel, depth_cells, width_cells),...  9.5 us
    ppermute x6, starting transfers between devices, swap(): lax.ppermute(value, axis, [(i, partner(i, count, phase)) for i in range(c...  9.31 us
    ppermute x1, starting transfers between devices, on_device(): images = lax.ppermute(image, ('depth', 'image'), route)  8.83 us
    pallas_call x1, Pallas kernels, on_device(): pl.pallas_call(functools.partial(inner_kernel, depth_cells, width_cells),...  8.69 us
    all_to_all x1, waiting for transfers between devices, on_device(): lax.all_to_all(partial, ('depth', 'image'), 0, 0, axis_index_groups=group...  7.64 us
    all_to_all x1, starting transfers between devices, on_device(): lax.all_to_all(partial, ('depth', 'image'), 0, 0, axis_index_groups=group...  6.65 us
    pallas_call x1, Pallas kernels, on_device(): pl.pallas_call(functools.partial(middle_kernel, depth_cells, width_cells)...  5.76 us
  transfers between devices with their start and end apart: 9, of which 2 were waited for; matrix products, arithmetic and copies ran while one was open for 2% of the time, Pallas kernels for 28%

profile of v7, /device:TPU:17, one launch (start us, length us, event | category | flops | bytes accessed | tf_op | source)
XLA Modules:
  0.0 93.6 jit_solution(16874288874023836850)
XLA Ops:
  0.6 0.1 pad_add_fusion.parity_ref
  0.7 4.6 %edge.1 = (f32[19,16,16,128]{3,2,1,0:T(8,128)}, s16[10,8,16,128]{3,2,1,0:T(8,128)(2,1)S(1)}, s16[10,8,16,128]{3,2,1,0:T(8,128)(2,1)S(1)}) custom-call(s32[2]{0:T(128)S(1)} %pad_add_fusion.parity_ref, f32[19,512,128]{2,1,0:T(8,128)} %bitcast.11), custom_call_target="tpu_custom_call" | custom-call | bytes 22140000 | tf_op jit(solution)/shard_map/edge/pallas_call | solution.py:611
  5.4 0.8 collective-permute-start.2
  6.1 1.0 %collective-permute-start.3 = (s16[10,8,16,128]{3,2,1,0:T(8,128)(2,1)S(1)}, s16[10,8,16,128]{3,2,1,0:T(8,128)(2,1)S(1)}, u32[]{:S(2)}, u32[]{:S(2)}) collective-permute-start(s16[10,8,16,128]{3,2,1,0:T(8,128)(2,1)S(1)} %get-tuple-element.37), channel_id=1, source_target_pairs={{0,112},{16,32},{32,16},{48,64},{64,48},{80,96},{96,80},{112,0},{1... | collective-permute-start | bytes 983048 | tf_op jit(solution)/shard_map/ppermute | solution.py:593
  7.1 5.8 %middle.1 = (f32[19,16,16,128]{3,2,1,0:T(8,128)}, s16[76,32,128]{2,1,0:T(8,128)(2,1)}, s16[76,32,128]{2,1,0:T(8,128)(2,1)}) custom-call(s32[2]{0:T(128)S(1)} %pad_add_fusion.parity_ref, f32[19,512,128]{2,1,0:T(8,128)} %bitcast.12, f32[19,16,16,128]{3,2,1,0:T(8,128)} %get-tuple-element.33.edge_hbm.e_hbm), custom_call_target="tpu_custom_call" | custom-call | bytes 22140000 | tf_op jit(solution)/shard_map/middle/pallas_call | solution.py:626
  12.9 1.3 %collective-permute-start = (s16[76,32,128]{2,1,0:T(8,128)(2,1)}, s16[76,32,128]{2,1,0:T(8,128)(2,1)}, u32[]{:S(2)}, u32[]{:S(2)}) collective-permute-start(s16[76,32,128]{2,1,0:T(8,128)(2,1)} %get-tuple-element.34), channel_id=1, source_target_pairs={{0,1},{1,0},{2,3},{3,2},{4,5},{5,4},{6,7},{7,6},{8,9},{9,8},{10,11... | collective-permute-start | bytes 1867784 | tf_op jit(solution)/shard_map/ppermute | solution.py:593
  14.2 5.3 %collective-permute-start.1 = (s16[76,32,128]{2,1,0:T(8,128)(2,1)}, s16[76,32,128]{2,1,0:T(8,128)(2,1)}, u32[]{:S(2)}, u32[]{:S(2)}) collective-permute-start(s16[76,32,128]{2,1,0:T(8,128)(2,1)} %get-tuple-element.35), channel_id=1, source_target_pairs={{0,15},{1,2},{2,1},{3,4},{4,3},{5,6},{6,5},{7,8},{8,7},{9,10},{10,... | collective-permute-start | bytes 1867784 | tf_op jit(solution)/shard_map/ppermute | solution.py:593
  20.2 0.1 reshape.64
  20.2 2.5 %corner.1 = (f32[19,16,8,128]{3,2,1,0:T(8,128)}, s16[38,16,128]{2,1,0:T(8,128)(2,1)}, s16[38,16,128]{2,1,0:T(8,128)(2,1)S(1)}) custom-call(s32[2]{0:T(128)S(1)} %pad_add_fusion.parity_ref, s16[10,8,16,128]{3,2,1,0:T(8,128)(2,1)S(1)} %collective-permute-done.2.xa_ref, s16[10,8,16,128]{3,2,1,0:T(8,128)(2,1)S(1)} %collective-permute-done.3.xb_ref), custom_call_target="tpu_custom_call" | custom-call | bytes 7380000 | tf_op jit(solution)/shard_map/corner/pallas_call | solution.py:647
  22.7 0.1 collective-permute-start.4
  22.8 0.9 collective-permute-start.5
  23.7 0.1 fusion.3
  23.8 0.6 broadcast_in_dim.8
  24.4 5.3 %all-to-all-start = ((f32[16,8,128]{2,1,0:T(8,128)}), f32[16,8,128]{2,1,0:T(8,128)S(1)}, u32[]{:S(2)}, u32[]{:S(2)}) async-start(f32[16,8,128]{2,1,0:T(8,128)} %broadcast_in_dim.8), calls=%async_computation | async-start | bytes 131072 | tf_op jit(solution)/shard_map/all_to_all | solution.py:690
  29.8 8.7 %inner.1 = (f32[19,26,56,128]{3,2,1,0:T(8,128)S(1)}, f32[19,26,56,128]{3,2,1,0:T(8,128)S(1)}, f32[19,512,128]{2,1,0:T(8,128)S(1)}, f32[3,26,56,128]{3,2,1,0:T(8,128)S(1)}, f32[512,128]{1,0:T(8,128)S(1)}) custom-call(f32[19,16,16,128]{3,2,1,0:T(8,128)} %get-tuple-element.33.edge_hbm.e_hbm, f32[19,16,16,128]{3,2,1,0:T(8,128)} %get-tuple-element.40.r_hbm, ...), custom_call_target="tpu_custom_call" | custom-call | bytes 44280000 | tf_op jit(solution)/shard_map/inner/pallas_call | solution.py:670
  38.5 9.5 %outer.1 = (f32[19,512,128]{2,1,0:T(8,128)}, bf16[512,128]{1,0:T(8,128)(2,1)}, f32[19,26,56,128]{3,2,1,0:T(8,128)S(1)}, f32[19,26,56,128]{3,2,1,0:T(8,128)S(1)},...) custom-call(s32[2]{0:T(128)S(1)} %pad_add_fusion.parity_ref, ...), custom_call_target="tpu_custom_call", output_to_operand_aliasing={{2}: (5, {}), {3}: (6, {}), {4}: (7, {}), {5}: (8, {}), {6}... | custom-call | bytes 44280000 | tf_op jit(solution)/shard_map/outer/pallas_call | solution.py:693
  48.1 16.4 %render.1 = f32[16,4,16,128]{3,2,1,0:T(8,128)} custom-call(f32[16,8,128]{2,1,0:T(8,128)S(1)} %all-to-all-done.table_ref, f32[512,128]{1,0:T(8,128)S(1)} %get-tuple-element.50.plain_ref), custom_call_target="tpu_custom_call" | custom-call | bytes 59040000 | tf_op jit(solution)/shard_map/render/pallas_call | solution.py:710
  64.4 6.6 %all-to-all-start.1 = ((f32[16,4,16,128]{3,2,1,0:T(8,128)}), f32[16,4,16,128]{3,2,1,0:T(8,128)S(1)}, u32[]{:S(2)}, u32[]{:S(2)}) async-start(f32[16,4,16,128]{3,2,1,0:T(8,128)} %render.1), calls=%async_computation.1 | async-start | bytes 1048576 | tf_op jit(solution)/shard_map/all_to_all | solution.py:728
  71.1 0.6 constant_dynamic-slice_fusion
  71.7 7.6 %all-to-all-done.1 = f32[16,4,16,128]{3,2,1,0:T(8,128)S(1)} async-done(((f32[16,4,16,128]{3,2,1,0:T(8,128)}), f32[16,4,16,128]{3,2,1,0:T(8,128)S(1)}, u32[]{:S(2)}, u32[]{:S(2)}) %all-to-all-start.1) | async-done | bytes 524320 | tf_op jit(solution)/shard_map/all_to_all | solution.py:728
  79.4 1.3 %composite.1 = f32[4,32,128]{2,1,0:T(8,128)} custom-call(f32[1]{0:T(128)} %bitcast.6.order_ref, f32[8,2,4,16,128]{4,3,2,1,0:T(8,128)S(1)} %bitcast.10), custom_call_target="tpu_custom_call" | custom-call | bytes 3690000 | tf_op jit(solution)/shard_map/composite/pallas_call | solution.py:731
  80.6 8.8 %collective-permute-start.6 = (f32[4,32,128]{2,1,0:T(8,128)}, f32[4,32,128]{2,1,0:T(8,128)S(1)}, u32[]{:S(2)}, u32[]{:S(2)}) collective-permute-start(f32[4,32,128]{2,1,0:T(8,128)} %composite.1), channel_id=1, source_target_pairs={{0,0},{1,1},{2,16},{3,17},{4,32},{5,33},{6,48},{7,49},{8,64},{9,65... | collective-permute-start | bytes 196616 | tf_op jit(solution)/shard_map/ppermute | solution.py:744
  89.5 3.5 %collective-permute-done.6 = f32[4,32,128]{2,1,0:T(8,128)S(1)} collective-permute-done((f32[4,32,128]{2,1,0:T(8,128)}, f32[4,32,128]{2,1,0:T(8,128)S(1)}, u32[]{:S(2)}, u32[]{:S(2)}) %collective-permute-start.6) | collective-permute-done | bytes 65568 | tf_op jit(solution)/shard_map/ppermute | solution.py:744
  93.0 0.6 copy.19
  (13 shorter events, 0.1 us)
Async XLA Ops:
  5.3 14.1 %copy-start = (f32[1,5,8]{2,0,1:T(1,128)S(1)}, f32[1,5,8]{2,0,1:T(1,128)}, u32[]{:S(2)}) copy-start(f32[1,5,8]{2,0,1:T(1,128)} %param.6) | copy-start | bytes 484
  5.4 14.9 %collective-permute-start.2 = (s16[10,8,16,128]{3,2,1,0:T(8,128)(2,1)S(1)}, s16[10,8,16,128]{3,2,1,0:T(8,128)(2,1)S(1)}, u32[]{:S(2)}, u32[]{:S(2)}) collective-permute-start(s16[10,8,16,128]{3,2,1,0:T(8,128)(2,1)S(1)} %get-tuple-element.36), channel_id=1, source_target_pairs={{0,16},{16,0},{32,48},{48,32},{64,80},{80,64},{96,112},{112,96},{1... | collective-permute-start | bytes 983048 | tf_op jit(solution)/shard_map/ppermute | solution.py:593
  6.1 14.1 %collective-permute-start.3 = (s16[10,8,16,128]{3,2,1,0:T(8,128)(2,1)S(1)}, s16[10,8,16,128]{3,2,1,0:T(8,128)(2,1)S(1)}, u32[]{:S(2)}, u32[]{:S(2)}) collective-permute-start(s16[10,8,16,128]{3,2,1,0:T(8,128)(2,1)S(1)} %get-tuple-element.37), channel_id=1, source_target_pairs={{0,112},{16,32},{32,16},{48,64},{64,48},{80,96},{96,80},{112,0},{1... | collective-permute-start | bytes 983048 | tf_op jit(solution)/shard_map/ppermute | solution.py:593
  12.9 25.7 %collective-permute-start = (s16[76,32,128]{2,1,0:T(8,128)(2,1)}, s16[76,32,128]{2,1,0:T(8,128)(2,1)}, u32[]{:S(2)}, u32[]{:S(2)}) collective-permute-start(s16[76,32,128]{2,1,0:T(8,128)(2,1)} %get-tuple-element.34), channel_id=1, source_target_pairs={{0,1},{1,0},{2,3},{3,2},{4,5},{5,4},{6,7},{7,6},{8,9},{9,8},{10,11... | collective-permute-start | bytes 1867784 | tf_op jit(solution)/shard_map/ppermute | solution.py:593
  14.2 24.4 %collective-permute-start.1 = (s16[76,32,128]{2,1,0:T(8,128)(2,1)}, s16[76,32,128]{2,1,0:T(8,128)(2,1)}, u32[]{:S(2)}, u32[]{:S(2)}) collective-permute-start(s16[76,32,128]{2,1,0:T(8,128)(2,1)} %get-tuple-element.35), channel_id=1, source_target_pairs={{0,15},{1,2},{2,1},{3,4},{4,3},{5,6},{6,5},{7,8},{8,7},{9,10},{10,... | collective-permute-start | bytes 1867784 | tf_op jit(solution)/shard_map/ppermute | solution.py:593
  22.7 15.8 %collective-permute-start.4 = (s16[38,16,128]{2,1,0:T(8,128)(2,1)}, s16[38,16,128]{2,1,0:T(8,128)(2,1)S(1)}, u32[]{:S(2)}, u32[]{:S(2)}) collective-permute-start(s16[38,16,128]{2,1,0:T(8,128)(2,1)} %get-tuple-element.38), channel_id=1, source_target_pairs={{0,1},{1,0},{2,3},{3,2},{4,5},{5,4},{6,7},{7,6},{8,9},{9,8},{10,11... | collective-permute-start | bytes 466952 | tf_op jit(solution)/shard_map/ppermute | solution.py:593
  22.8 15.7 %collective-permute-start.5 = (s16[38,16,128]{2,1,0:T(8,128)(2,1)S(1)}, s16[38,16,128]{2,1,0:T(8,128)(2,1)S(1)}, u32[]{:S(2)}, u32[]{:S(2)}) collective-permute-start(s16[38,16,128]{2,1,0:T(8,128)(2,1)S(1)} %get-tuple-element.39), channel_id=1, source_target_pairs={{0,15},{1,2},{2,1},{3,4},{4,3},{5,6},{6,5},{7,8},{8,7},{9,10},{10,... | collective-permute-start | bytes 466952 | tf_op jit(solution)/shard_map/ppermute | solution.py:593
  24.4 23.6 %all-to-all-start = ((f32[16,8,128]{2,1,0:T(8,128)}), f32[16,8,128]{2,1,0:T(8,128)S(1)}, u32[]{:S(2)}, u32[]{:S(2)}) async-start(f32[16,8,128]{2,1,0:T(8,128)} %broadcast_in_dim.8), calls=%async_computation | async-start | bytes 131072 | tf_op jit(solution)/shard_map/all_to_all | solution.py:690
  64.4 14.9 %all-to-all-start.1 = ((f32[16,4,16,128]{3,2,1,0:T(8,128)}), f32[16,4,16,128]{3,2,1,0:T(8,128)S(1)}, u32[]{:S(2)}, u32[]{:S(2)}) async-start(f32[16,4,16,128]{3,2,1,0:T(8,128)} %render.1), calls=%async_computation.1 | async-start | bytes 1048576 | tf_op jit(solution)/shard_map/all_to_all | solution.py:728
  80.6 12.4 %collective-permute-start.6 = (f32[4,32,128]{2,1,0:T(8,128)}, f32[4,32,128]{2,1,0:T(8,128)S(1)}, u32[]{:S(2)}, u32[]{:S(2)}) collective-permute-start(f32[4,32,128]{2,1,0:T(8,128)} %composite.1), channel_id=1, source_target_pairs={{0,0},{1,1},{2,16},{3,17},{4,32},{5,33},{6,48},{7,49},{8,64},{9,65... | collective-permute-start | bytes 196616 | tf_op jit(solution)/shard_map/ppermute | solution.py:744

commit v8 on v7

--- a/solution.py
+++ b/solution.py
@@ -23,6 +23,8 @@
 AXIS_PAIRS = ((1, 2), (3, 4), (5, 6))
 DIAG_PAIRS = ((7, 8), (9, 10), (11, 12), (13, 14), (15, 16), (17, 18))
 SCALE = 8192.0
+
+FACE_PARTS = 2
 
 X_PAIRS = tuple(
     (a, b, 5) for a, b in zip((1, 7, 9, 11, 13), (2, 8, 10, 12, 14))
@@ -181,7 +183,8 @@
 
 
 def middle_kernel(
-    depth_cells, width_cells, parity_ref, f_hbm, edge_hbm, r_hbm, ia_ref, ib_ref, f_ref, r_ref, edge_ref, in_sems, out_sems
+    depth_cells, width_cells, parity_ref, f_hbm, edge_hbm, r_hbm, ia_hbm, ib_hbm, f_ref, r_ref, edge_ref, ia_ref, ib_ref,
+    in_sems, out_sems, face_sems
 ):
     chunk = 8 * width_cells
     tiles = depth_cells // 8
@@ -221,6 +224,7 @@
 
     low_face = face_list(0, 1)
     high_face = face_list(width_cells - 1, -1)
+    part = len(low_face) // FACE_PARTS
     for index, ((yl, pl_), (yh, ph)) in enumerate(zip(low_face, high_face)):
         for c in range(tiles // 2):
             a, b = [], []
@@ -231,6 +235,11 @@
                 b.append(jnp.where(odd_image, high, low))
             ia_ref[index, 16 * c : 16 * c + 16, :] = pack_code(*a)
             ib_ref[index, 16 * c : 16 * c + 16, :] = pack_code(*b)
+        if (index + 1) % part == 0:
+            at = pl.ds(index + 1 - part, part)
+            for k, (source, target) in enumerate(((ia_ref, ia_hbm), (ib_ref, ib_hbm))):
+                keeps.append(pltpu.make_async_copy(source.at[at], target.at[at], face_sems.at[k, index // part]))
+                keeps[-1].start()
     for keep in keeps:
         keep.wait()
 
@@ -409,9 +418,9 @@
 
 
 def outer_kernel(
-    depth_cells, width_cells, parity_ref, ya_ref, yb_ref, ca_ref, cb_ref,
+    depth_cells, width_cells, parity_ref, ya_hbm, yb_hbm, ca_ref, cb_ref,
     sa_in, sb_in, final_in, flow_in, plain_in,
-    out_hbm, vort_ref, sa_ref, sb_ref, out_ref, flow_ref, plain_ref, out_sem,
+    out_hbm, vort_ref, sa_ref, sb_ref, out_ref, flow_ref, plain_ref, ya_ref, yb_ref, out_sem, face_sems,
 ):
     tiles = depth_cells // 8
     rows = row_index()
@@ -419,7 +428,22 @@
 
     low_face = face_list(0, 1)
     high_face = face_list(width_cells - 1, -1)
+    part = len(low_face) // FACE_PARTS
+    loads = []
+    for n in range(FACE_PARTS):
+        at = pl.ds(n * part, part)
+        loads.append(
+            [
+                pltpu.make_async_copy(source.at[at], target.at[at], face_sems.at[k, n])
+                for k, (source, target) in enumerate(((ya_hbm, ya_ref), (yb_hbm, yb_ref)))
+            ]
+        )
+        for load in loads[-1]:
+            load.start()
     for index in range(0, len(low_face), 2):
+        if index % part == 0:
+            for load in loads[index // part]:
+                load.wait()
         corner_a, corner_b = wide(ca_ref[index // 2]), wide(cb_ref[index // 2])
         for k in range(2):
             (yl, pl_), (yh, ph) = low_face[index + k], high_face[index + k]
@@ -625,15 +649,18 @@
     )(parity, field)
     middle, ia, ib = pl.pallas_call(
         functools.partial(middle_kernel, depth_cells, width_cells),
-        out_shape=(pltpu.HBM((Q, width_cells, half[0], lanes), f32), y_shape, y_shape),
+        out_shape=(pltpu.HBM((Q, width_cells, half[0], lanes), f32), pltpu.HBM(y_shape.shape, i16), pltpu.HBM(y_shape.shape, i16)),
         in_specs=[SMEM, HBM, HBM],
-        out_specs=(HBM, VMEM, VMEM),
+        out_specs=(HBM,) * 3,
         scratch_shapes=[
             pltpu.VMEM((Q, half[0] * width_cells, lanes), f32),
             pltpu.VMEM((Q, width_cells, half[0], lanes), f32),
             pltpu.VMEM((Q, 2 * HALO, half[1], lanes), f32),
+            pltpu.VMEM(y_shape.shape, i16),
+            pltpu.VMEM(y_shape.shape, i16),
             pltpu.SemaphoreType.DMA((depth_cells // 8,)),
             pltpu.SemaphoreType.DMA((depth_cells // 8 - 2,)),
+            pltpu.SemaphoreType.DMA((2, FACE_PARTS)),
         ],
         compiler_params=GRANT,
         cost_estimate=cost(6),
@@ -697,14 +724,19 @@
             jax.ShapeDtypeStruct((cells, lanes), jnp.bfloat16),
             *stages,
         ),
-        in_specs=[SMEM] + [VMEM] * 9,
+        in_specs=[SMEM, HBM, HBM] + [VMEM] * 7,
         out_specs=(HBM,) + (VMEM,) * 6,
-        scratch_shapes=[pltpu.SemaphoreType.DMA],
+        scratch_shapes=[
+            pltpu.VMEM(y_shape.shape, i16),
+            pltpu.VMEM(y_shape.shape, i16),
+            pltpu.SemaphoreType.DMA,
+            pltpu.SemaphoreType.DMA((2, FACE_PARTS)),
+        ],
         input_output_aliases={5 + k: 2 + k for k in range(5)},
         compiler_params=GRANT,
         cost_estimate=cost(12),
         name="outer",
-    )(parity, ya, yb, ca, cb, *state)
+    )(parity, in_hbm(ya), in_hbm(yb), ca, cb, *state)
 
     functions = image_count
     partial = pl.pallas_call(

time: 94.8 us -> 94.4 us (level)
  Pallas kernels: 48.7 us -> 47.5 us
  transfers between devices with their start and end apart: 9 -> 9, of which waited for: 2 -> 2; matrix products, arithmetic and copies ran while one was open for 2% -> 1% of each run, Pallas kernels for 28% -> 27%
where the time goes in v8:
time: 94.4 us; the launch traced here: 93.2 us
  Pallas kernels  47.5 us (50%)
  starting transfers between devices  30.1 us (32%)
  waiting for transfers between devices  11.3 us (12%)
  local copies, waits for them, and re-layouts  2.72 us (3%)
  between operations  1.44 us (2%)
    pallas_call x1, Pallas kernels, on_device(): pl.pallas_call(functools.partial(render_kernel, depth_cells, width_cells,...  16.4 us
    pallas_call x1, Pallas kernels, on_device(): pl.pallas_call(functools.partial(outer_kernel, depth_cells, width_cells),...  9.71 us
    ppermute x6, starting transfers between devices, swap(): lax.ppermute(value, axis, [(i, partner(i, count, phase)) for i in range(c...  9.31 us
    ppermute x1, starting transfers between devices, on_device(): images = lax.ppermute(image, ('depth', 'image'), route)  8.83 us
    pallas_call x1, Pallas kernels, on_device(): pl.pallas_call(functools.partial(inner_kernel, depth_cells, width_cells),...  8.69 us
    all_to_all x1, waiting for transfers between devices, on_device(): lax.all_to_all(partial, ('depth', 'image'), 0, 0, axis_index_groups=group...  7.73 us
    all_to_all x1, starting transfers between devices, on_device(): lax.all_to_all(partial, ('depth', 'image'), 0, 0, axis_index_groups=group...  6.65 us
    all_to_all x1, starting transfers between devices, on_device(): lax.all_to_all(jnp.broadcast_to(row, (image_count, 8, lanes)), 'image', 0...  5.35 us
  transfers between devices with their start and end apart: 9, of which 2 were waited for; matrix products, arithmetic and copies ran while one was open for 1% of the time, Pallas kernels for 27%

profile of v8, /device:TPU:17, one launch (start us, length us, event | category | flops | bytes accessed | tf_op | source)
XLA Modules:
  0.0 93.2 jit_solution(6247675149712050090)
XLA Ops:
  0.6 0.1 pad_add_fusion.parity_ref
  0.7 4.6 %edge.1 = (f32[19,16,16,128]{3,2,1,0:T(8,128)}, s16[10,8,16,128]{3,2,1,0:T(8,128)(2,1)S(1)}, s16[10,8,16,128]{3,2,1,0:T(8,128)(2,1)S(1)}) custom-call(s32[2]{0:T(128)S(1)} %pad_add_fusion.parity_ref, f32[19,512,128]{2,1,0:T(8,128)} %bitcast.11), custom_call_target="tpu_custom_call" | custom-call | bytes 22140000 | tf_op jit(solution)/shard_map/edge/pallas_call | solution.py:635
  5.4 0.8 collective-permute-start.2
  6.1 1.0 %collective-permute-start.3 = (s16[10,8,16,128]{3,2,1,0:T(8,128)(2,1)S(1)}, s16[10,8,16,128]{3,2,1,0:T(8,128)(2,1)S(1)}, u32[]{:S(2)}, u32[]{:S(2)}) collective-permute-start(s16[10,8,16,128]{3,2,1,0:T(8,128)(2,1)S(1)} %get-tuple-element.37), channel_id=1, source_target_pairs={{0,112},{16,32},{32,16},{48,64},{64,48},{80,96},{96,80},{112,0},{1... | collective-permute-start | bytes 983048 | tf_op jit(solution)/shard_map/ppermute | solution.py:617
  7.1 5.1 %middle.1 = (f32[19,16,16,128]{3,2,1,0:T(8,128)}, s16[76,32,128]{2,1,0:T(8,128)(2,1)}, s16[76,32,128]{2,1,0:T(8,128)(2,1)}) custom-call(s32[2]{0:T(128)S(1)} %pad_add_fusion.parity_ref, f32[19,512,128]{2,1,0:T(8,128)} %bitcast.12, f32[19,16,16,128]{3,2,1,0:T(8,128)} %get-tuple-element.33.edge_hbm.e_hbm), custom_call_target="tpu_custom_call" | custom-call | bytes 22140000 | tf_op jit(solution)/shard_map/middle/pallas_call | solution.py:650
  12.2 1.3 %collective-permute-start = (s16[76,32,128]{2,1,0:T(8,128)(2,1)}, s16[76,32,128]{2,1,0:T(8,128)(2,1)S(1)}, u32[]{:S(2)}, u32[]{:S(2)}) collective-permute-start(s16[76,32,128]{2,1,0:T(8,128)(2,1)} %get-tuple-element.34), channel_id=1, source_target_pairs={{0,1},{1,0},{2,3},{3,2},{4,5},{5,4},{6,7},{7,6},{8,9},{9,8},{10,11... | collective-permute-start | bytes 1867784 | tf_op jit(solution)/shard_map/ppermute | solution.py:617
  13.4 5.3 %collective-permute-start.1 = (s16[76,32,128]{2,1,0:T(8,128)(2,1)}, s16[76,32,128]{2,1,0:T(8,128)(2,1)}, u32[]{:S(2)}, u32[]{:S(2)}) collective-permute-start(s16[76,32,128]{2,1,0:T(8,128)(2,1)} %get-tuple-element.35), channel_id=1, source_target_pairs={{0,15},{1,2},{2,1},{3,4},{4,3},{5,6},{6,5},{7,8},{8,7},{9,10},{10,... | collective-permute-start | bytes 1867784 | tf_op jit(solution)/shard_map/ppermute | solution.py:617
  19.4 0.1 reshape.64
  19.5 1.8 %corner.1 = (f32[19,16,8,128]{3,2,1,0:T(8,128)}, s16[38,16,128]{2,1,0:T(8,128)(2,1)S(1)}, s16[38,16,128]{2,1,0:T(8,128)(2,1)S(1)}) custom-call(s32[2]{0:T(128)S(1)} %pad_add_fusion.parity_ref, s16[10,8,16,128]{3,2,1,0:T(8,128)(2,1)S(1)} %collective-permute-done.2.xa_ref, s16[10,8,16,128]{3,2,1,0:T(8,128)(2,1)S(1)} %collective-permute-done.3.xb_ref), custom_call_target="tpu_custom_call" | custom-call | bytes 7380000 | tf_op jit(solution)/shard_map/corner/pallas_call | solution.py:674
  21.4 0.1 collective-permute-start.4
  21.5 0.9 collective-permute-start.5
  22.4 0.6 broadcast_in_dim.8
  23.1 5.3 %all-to-all-start = ((f32[16,8,128]{2,1,0:T(8,128)}), f32[16,8,128]{2,1,0:T(8,128)S(1)}, u32[]{:S(2)}, u32[]{:S(2)}) async-start(f32[16,8,128]{2,1,0:T(8,128)} %broadcast_in_dim.8), calls=%async_computation | async-start | bytes 131072 | tf_op jit(solution)/shard_map/all_to_all | solution.py:717
  28.4 8.7 %inner.1 = (f32[19,26,56,128]{3,2,1,0:T(8,128)S(1)}, f32[19,26,56,128]{3,2,1,0:T(8,128)S(1)}, f32[19,512,128]{2,1,0:T(8,128)S(1)}, f32[3,26,56,128]{3,2,1,0:T(8,128)S(1)}, f32[512,128]{1,0:T(8,128)S(1)}) custom-call(f32[19,16,16,128]{3,2,1,0:T(8,128)} %get-tuple-element.33.edge_hbm.e_hbm, f32[19,16,16,128]{3,2,1,0:T(8,128)} %get-tuple-element.40.r_hbm, ...), custom_call_target="tpu_custom_call" | custom-call | bytes 44280000 | tf_op jit(solution)/shard_map/inner/pallas_call | solution.py:697
  37.2 0.8 copy-done
  38.0 9.7 %outer.1 = (f32[19,512,128]{2,1,0:T(8,128)}, bf16[512,128]{1,0:T(8,128)(2,1)}, f32[19,26,56,128]{3,2,1,0:T(8,128)S(1)}, f32[19,26,56,128]{3,2,1,0:T(8,128)S(1)},...) custom-call(s32[2]{0:T(128)S(1)} %pad_add_fusion.parity_ref, ...), custom_call_target="tpu_custom_call", output_to_operand_aliasing={{2}: (5, {}), {3}: (6, {}), {4}: (7, {}), {5}: (8, {}), {6}... | custom-call | bytes 44280000 | tf_op jit(solution)/shard_map/outer/pallas_call | solution.py:720
  47.7 16.4 %render.1 = f32[16,4,16,128]{3,2,1,0:T(8,128)} custom-call(f32[16,8,128]{2,1,0:T(8,128)S(1)} %all-to-all-done.table_ref, f32[512,128]{1,0:T(8,128)S(1)} %get-tuple-element.50.plain_ref), custom_call_target="tpu_custom_call" | custom-call | bytes 59040000 | tf_op jit(solution)/shard_map/render/pallas_call | solution.py:742
  64.1 6.7 %all-to-all-start.1 = ((f32[16,4,16,128]{3,2,1,0:T(8,128)}), f32[16,4,16,128]{3,2,1,0:T(8,128)S(1)}, u32[]{:S(2)}, u32[]{:S(2)}) async-start(f32[16,4,16,128]{3,2,1,0:T(8,128)} %render.1), calls=%async_computation.1 | async-start | bytes 1048576 | tf_op jit(solution)/shard_map/all_to_all | solution.py:760
  70.8 0.6 constant_dynamic-slice_fusion
  71.3 7.7 %all-to-all-done.1 = f32[16,4,16,128]{3,2,1,0:T(8,128)S(1)} async-done(((f32[16,4,16,128]{3,2,1,0:T(8,128)}), f32[16,4,16,128]{3,2,1,0:T(8,128)S(1)}, u32[]{:S(2)}, u32[]{:S(2)}) %all-to-all-start.1) | async-done | bytes 524320 | tf_op jit(solution)/shard_map/all_to_all | solution.py:760
  79.0 1.2 %composite.1 = f32[4,32,128]{2,1,0:T(8,128)} custom-call(f32[1]{0:T(128)} %bitcast.6.order_ref, f32[8,2,4,16,128]{4,3,2,1,0:T(8,128)S(1)} %bitcast.10), custom_call_target="tpu_custom_call" | custom-call | bytes 3690000 | tf_op jit(solution)/shard_map/composite/pallas_call | solution.py:763
  80.3 8.8 %collective-permute-start.6 = (f32[4,32,128]{2,1,0:T(8,128)}, f32[4,32,128]{2,1,0:T(8,128)S(1)}, u32[]{:S(2)}, u32[]{:S(2)}) collective-permute-start(f32[4,32,128]{2,1,0:T(8,128)} %composite.1), channel_id=1, source_target_pairs={{0,0},{1,1},{2,16},{3,17},{4,32},{5,33},{6,48},{7,49},{8,64},{9,65... | collective-permute-start | bytes 196616 | tf_op jit(solution)/shard_map/ppermute | solution.py:776
  89.1 3.5 %collective-permute-done.6 = f32[4,32,128]{2,1,0:T(8,128)S(1)} collective-permute-done((f32[4,32,128]{2,1,0:T(8,128)}, f32[4,32,128]{2,1,0:T(8,128)S(1)}, u32[]{:S(2)}, u32[]{:S(2)}) %collective-permute-start.6) | collective-permute-done | bytes 65568 | tf_op jit(solution)/shard_map/ppermute | solution.py:776
  92.6 0.6 copy.19
  (15 shorter events, 0.1 us)
Async XLA Ops:
  5.3 13.4 %copy-start.1 = (f32[1,5,8]{2,0,1:T(1,128)S(1)}, f32[1,5,8]{2,0,1:T(1,128)}, u32[]{:S(2)}) copy-start(f32[1,5,8]{2,0,1:T(1,128)} %param.6) | copy-start | bytes 484
  5.4 14.2 %collective-permute-start.2 = (s16[10,8,16,128]{3,2,1,0:T(8,128)(2,1)S(1)}, s16[10,8,16,128]{3,2,1,0:T(8,128)(2,1)S(1)}, u32[]{:S(2)}, u32[]{:S(2)}) collective-permute-start(s16[10,8,16,128]{3,2,1,0:T(8,128)(2,1)S(1)} %get-tuple-element.36), channel_id=1, source_target_pairs={{0,16},{16,0},{32,48},{48,32},{64,80},{80,64},{96,112},{112,96},{1... | collective-permute-start | bytes 983048 | tf_op jit(solution)/shard_map/ppermute | solution.py:617
  6.1 13.4 %collective-permute-start.3 = (s16[10,8,16,128]{3,2,1,0:T(8,128)(2,1)S(1)}, s16[10,8,16,128]{3,2,1,0:T(8,128)(2,1)S(1)}, u32[]{:S(2)}, u32[]{:S(2)}) collective-permute-start(s16[10,8,16,128]{3,2,1,0:T(8,128)(2,1)S(1)} %get-tuple-element.37), channel_id=1, source_target_pairs={{0,112},{16,32},{32,16},{48,64},{64,48},{80,96},{96,80},{112,0},{1... | collective-permute-start | bytes 983048 | tf_op jit(solution)/shard_map/ppermute | solution.py:617
  12.2 25.0 %collective-permute-start = (s16[76,32,128]{2,1,0:T(8,128)(2,1)}, s16[76,32,128]{2,1,0:T(8,128)(2,1)S(1)}, u32[]{:S(2)}, u32[]{:S(2)}) collective-permute-start(s16[76,32,128]{2,1,0:T(8,128)(2,1)} %get-tuple-element.34), channel_id=1, source_target_pairs={{0,1},{1,0},{2,3},{3,2},{4,5},{5,4},{6,7},{7,6},{8,9},{9,8},{10,11... | collective-permute-start | bytes 1867784 | tf_op jit(solution)/shard_map/ppermute | solution.py:617
  13.4 23.7 %collective-permute-start.1 = (s16[76,32,128]{2,1,0:T(8,128)(2,1)}, s16[76,32,128]{2,1,0:T(8,128)(2,1)}, u32[]{:S(2)}, u32[]{:S(2)}) collective-permute-start(s16[76,32,128]{2,1,0:T(8,128)(2,1)} %get-tuple-element.35), channel_id=1, source_target_pairs={{0,15},{1,2},{2,1},{3,4},{4,3},{5,6},{6,5},{7,8},{8,7},{9,10},{10,... | collective-permute-start | bytes 1867784 | tf_op jit(solution)/shard_map/ppermute | solution.py:617
  21.4 15.8 %collective-permute-start.4 = (s16[38,16,128]{2,1,0:T(8,128)(2,1)S(1)}, s16[38,16,128]{2,1,0:T(8,128)(2,1)S(1)}, u32[]{:S(2)}, u32[]{:S(2)}) collective-permute-start(s16[38,16,128]{2,1,0:T(8,128)(2,1)S(1)} %get-tuple-element.38), channel_id=1, source_target_pairs={{0,1},{1,0},{2,3},{3,2},{4,5},{5,4},{6,7},{7,6},{8,9},{9,8},{10,11... | collective-permute-start | bytes 466952 | tf_op jit(solution)/shard_map/ppermute | solution.py:617
  21.5 15.7 %collective-permute-start.5 = (s16[38,16,128]{2,1,0:T(8,128)(2,1)S(1)}, s16[38,16,128]{2,1,0:T(8,128)(2,1)S(1)}, u32[]{:S(2)}, u32[]{:S(2)}) collective-permute-start(s16[38,16,128]{2,1,0:T(8,128)(2,1)S(1)} %get-tuple-element.39), channel_id=1, source_target_pairs={{0,15},{1,2},{2,1},{3,4},{4,3},{5,6},{6,5},{7,8},{8,7},{9,10},{10,... | collective-permute-start | bytes 466952 | tf_op jit(solution)/shard_map/ppermute | solution.py:617
  23.1 24.6 %all-to-all-start = ((f32[16,8,128]{2,1,0:T(8,128)}), f32[16,8,128]{2,1,0:T(8,128)S(1)}, u32[]{:S(2)}, u32[]{:S(2)}) async-start(f32[16,8,128]{2,1,0:T(8,128)} %broadcast_in_dim.8), calls=%async_computation | async-start | bytes 131072 | tf_op jit(solution)/shard_map/all_to_all | solution.py:717
  37.2 0.8 copy-start
  64.1 14.9 %all-to-all-start.1 = ((f32[16,4,16,128]{3,2,1,0:T(8,128)}), f32[16,4,16,128]{3,2,1,0:T(8,128)S(1)}, u32[]{:S(2)}, u32[]{:S(2)}) async-start(f32[16,4,16,128]{3,2,1,0:T(8,128)} %render.1), calls=%async_computation.1 | async-start | bytes 1048576 | tf_op jit(solution)/shard_map/all_to_all | solution.py:760
  80.3 12.4 %collective-permute-start.6 = (f32[4,32,128]{2,1,0:T(8,128)}, f32[4,32,128]{2,1,0:T(8,128)S(1)}, u32[]{:S(2)}, u32[]{:S(2)}) collective-permute-start(f32[4,32,128]{2,1,0:T(8,128)} %composite.1), channel_id=1, source_target_pairs={{0,0},{1,1},{2,16},{3,17},{4,32},{5,33},{6,48},{7,49},{8,64},{9,65... | collective-permute-start | bytes 196616 | tf_op jit(solution)/shard_map/ppermute | solution.py:776
